TPU v7x, 32 devices: a whole 2x2x4 slice. The times are simulated.
32 devices in a mesh: wide: 8 (over z, x), narrow: 4 (over y, core).
Axes of the slice: x: 2, y: 2, z: 4, core: 2. Of those that a mesh axis runs over, the one named last changes fastest.
Arguments:
- first_input: bfloat16 [512, 256, 512], P(('wide', 'narrow')), may hold values from -6 to 6
- second_input: bfloat16 [512, 256, 512], P(('wide', 'narrow')), may hold values from -6 to 6
- cotangent: bfloat16 [512, 256, 512], P(('wide', 'narrow')), may hold values from -6 to 6
- lengths: int32 [512], P(('wide', 'narrow')), may hold values from 232 to 256, as said below
- conv_weight: bfloat16 [7, 512], P(None, ('wide', 'narrow')), may hold values from -2 to 2
- conv_bias: bfloat16 [512], P(('wide', 'narrow')), may hold values from -3 to 3
- norm_gain: bfloat16 [512], P(('wide', 'narrow')), may hold values from 0.5 to 2
- norm_bias: bfloat16 [512], P(('wide', 'narrow')), may hold values from -3 to 3
- up_weight: bfloat16 [512, 1536], P(('wide', 'narrow')), may hold values from -0.25 to 0.25
- up_bias: bfloat16 [1536], P(('wide', 'narrow')), may hold values from -3 to 3
- down_weight: bfloat16 [1536, 512], P(('wide', 'narrow')), may hold values from -0.15625 to 0.15625
- down_bias: bfloat16 [512], P(('wide', 'narrow')), may hold values from -2 to 2
- layer_scale: bfloat16 [512], P(('wide', 'narrow')), may hold values from 0.29882812 to 1.5
Outputs:
- first_output: bfloat16 [512, 256, 512], P(('wide', 'narrow'))
- second_output: bfloat16 [512, 256, 512], P(('wide', 'narrow'))
- input_grad: bfloat16 [512, 256, 512], P(('wide', 'narrow'))
- grad_conv_weight: float32 [7, 512], P(None, ('wide', 'narrow'))
- grad_conv_bias: float32 [512], P(('wide', 'narrow'))
- grad_norm_gain: float32 [512], P(('wide', 'narrow'))
- grad_norm_bias: float32 [512], P(('wide', 'narrow'))
- grad_up_weight: float32 [512, 1536], P(('wide', 'narrow'))
- grad_up_bias: float32 [1536], P(('wide', 'narrow'))
- grad_down_weight: float32 [1536, 512], P(('wide', 'narrow'))
- grad_down_bias: float32 [512], P(('wide', 'narrow'))
- grad_layer_scale: float32 [512], P(('wide', 'narrow'))
Inputs may be any that keep to these rules, and one draw needn't show every extreme that they name: Each clip has 256 or 232 frames; both lengths occur.
All inputs are finite; a program needn't handle non-finite values.
Results may differ from a plain program's by a relative error of at most 0.007.
Values may be sent and summed in bfloat16 or wider, within the bound.
No kernel may reach another device: no remote copies, remote signals or barrier semaphores. Data moves between devices by JAX's collectives and lax.ppermute only.
A program may use at most 256 MiB of HBM per device.

v0:
```python
import jax
import jax.numpy as jnp
from jax import lax
from jax.sharding import PartitionSpec as P


def depthwise(masked, kernel_taps, conv_bias):
    margin = kernel_taps.shape[0] // 2
    frames = masked.shape[1]
    padded = jnp.pad(masked, ((0, 0), (margin, margin), (0, 0)))
    result = conv_bias + jnp.zeros_like(masked)
    for offset in range(kernel_taps.shape[0]):
        result = result + kernel_taps[offset] * padded[:, offset : offset + frames]
    return result


def normalize(conv_out, norm_gain, norm_bias):
    average = jnp.mean(conv_out, axis=-1, keepdims=True)
    centred = conv_out - average
    variance = jnp.mean(centred * centred, axis=-1, keepdims=True)
    return centred * lax.rsqrt(variance + 1e-06) * norm_gain + norm_bias


def pre_norm(masked, kernel_taps, conv_bias, norm_gain, norm_bias):
    return normalize(depthwise(masked, kernel_taps, conv_bias), norm_gain, norm_bias)


def exact_gelu(values):
    return jax.nn.gelu(values, approximate=False)


def gather_again(
    conv_weight,
    conv_bias,
    norm_gain,
    norm_bias,
    up_weight,
    up_bias,
    down_weight,
    down_bias,
    layer_scale,
):
    return (
        lax.all_gather(conv_weight, ("wide", "narrow"), axis=1, tiled=True),
        lax.all_gather(conv_bias, ("wide", "narrow"), axis=0, tiled=True),
        lax.all_gather(norm_gain, ("wide", "narrow"), axis=0, tiled=True),
        lax.all_gather(norm_bias, ("wide", "narrow"), axis=0, tiled=True),
        lax.all_gather(up_weight, ("wide", "narrow"), axis=0, tiled=True),
        lax.all_gather(up_bias, ("wide", "narrow"), axis=0, tiled=True),
        lax.all_gather(down_weight, ("wide", "narrow"), axis=0, tiled=True),
        lax.all_gather(down_bias, ("wide", "narrow"), axis=0, tiled=True),
        lax.all_gather(layer_scale, ("wide", "narrow"), axis=0, tiled=True),
    )


def small_floats(weights):
    (
        conv_weight,
        conv_bias,
        norm_gain,
        norm_bias,
        up_weight,
        up_bias,
        down_weight,
        down_bias,
        layer_scale,
    ) = weights
    return (
        conv_weight.astype(jnp.float32),
        conv_bias.astype(jnp.float32),
        norm_gain.astype(jnp.float32),
        norm_bias.astype(jnp.float32),
        up_bias.astype(jnp.float32),
        down_bias.astype(jnp.float32),
        layer_scale.astype(jnp.float32),
    )


def run_forward(inputs, validity, weights):
    up_weight = weights[4]
    down_weight = weights[6]
    taps, conv_shift, gain, norm_shift, up_shift, down_shift, scale = small_floats(weights)
    values = inputs.astype(jnp.float32)
    masked = values * validity
    normed = pre_norm(masked, taps, conv_shift, gain, norm_shift)
    width = normed.shape[-1]
    normed_low = normed.astype(jnp.bfloat16).reshape(-1, width)
    hidden = jnp.dot(normed_low, up_weight, preferred_element_type=jnp.float32) + up_shift
    active = exact_gelu(hidden).astype(jnp.bfloat16)
    branch = (
        jnp.dot(active, down_weight, preferred_element_type=jnp.float32) + down_shift
    ).reshape(values.shape)
    output = validity * (values + scale * branch)
    return (output, (masked, normed_low, hidden, active, branch))


def down_section(cotangent, validity, weights, kept):
    masked, normed_low, hidden, active, branch = kept
    down_weight = weights[6]
    scale = weights[8].astype(jnp.float32)
    width = masked.shape[-1]
    upstream = cotangent.astype(jnp.float32) * validity
    grad_scale = jnp.sum(upstream * branch, axis=(0, 1))
    grad_branch = (upstream * scale).astype(jnp.bfloat16).reshape(-1, width)
    grad_down_bias = jnp.sum(grad_branch.astype(jnp.float32), axis=0)
    grad_down_weight = jnp.dot(active.T, grad_branch, preferred_element_type=jnp.float32)
    grad_active = jnp.dot(grad_branch, down_weight.T, preferred_element_type=jnp.float32)
    return ((grad_down_weight, grad_down_bias, grad_scale), grad_active)


def up_section(grad_active, weights, kept):
    masked, normed_low, hidden, active, branch = kept
    up_weight = weights[4]
    gelu_out, gelu_back = jax.vjp(exact_gelu, hidden)
    grad_hidden = gelu_back(grad_active)[0].astype(jnp.bfloat16)
    grad_up_bias = jnp.sum(grad_hidden.astype(jnp.float32), axis=0)
    grad_up_weight = jnp.dot(normed_low.T, grad_hidden, preferred_element_type=jnp.float32)
    grad_normed = jnp.dot(grad_hidden, up_weight.T, preferred_element_type=jnp.float32).reshape(
        masked.shape
    )
    return ((grad_up_weight, grad_up_bias), grad_normed)


def front_section(grad_normed, cotangent, validity, weights, kept):
    masked = kept[0]
    taps, conv_shift, gain, norm_shift, up_shift, down_shift, scale = small_floats(weights)
    normed_out, norm_back = jax.vjp(pre_norm, masked, taps, conv_shift, gain, norm_shift)
    grad_masked, grad_taps, grad_conv_shift, grad_gain, grad_norm_shift = norm_back(grad_normed)
    grad_inputs = validity * (cotangent.astype(jnp.float32) + grad_masked)
    return ((grad_taps, grad_conv_shift, grad_gain, grad_norm_shift), grad_inputs)


def on_device(
    first_input,
    second_input,
    cotangent,
    lengths,
    conv_weight,
    conv_bias,
    norm_gain,
    norm_bias,
    up_weight,
    up_bias,
    down_weight,
    down_bias,
    layer_scale,
):
    frame_index = lax.broadcasted_iota(jnp.int32, (first_input.shape[0], first_input.shape[1]), 1)
    validity = (frame_index < lengths[:, None]).astype(jnp.float32)[:, :, None]
    first_weights = (
        lax.all_gather(conv_weight, ("wide", "narrow"), axis=1, tiled=True),
        lax.all_gather(conv_bias, ("wide", "narrow"), axis=0, tiled=True),
        lax.all_gather(norm_gain, ("wide", "narrow"), axis=0, tiled=True),
        lax.all_gather(norm_bias, ("wide", "narrow"), axis=0, tiled=True),
        lax.all_gather(up_weight, ("wide", "narrow"), axis=0, tiled=True),
        lax.all_gather(up_bias, ("wide", "narrow"), axis=0, tiled=True),
        lax.all_gather(down_weight, ("wide", "narrow"), axis=0, tiled=True),
        lax.all_gather(down_bias, ("wide", "narrow"), axis=0, tiled=True),
        lax.all_gather(layer_scale, ("wide", "narrow"), axis=0, tiled=True),
    )
    first_output, first_kept = run_forward(first_input, validity, first_weights)
    forward_weights = gather_again(
        conv_weight,
        conv_bias,
        norm_gain,
        norm_bias,
        up_weight,
        up_bias,
        down_weight,
        down_bias,
        layer_scale,
    )
    backward_weights = gather_again(
        conv_weight,
        conv_bias,
        norm_gain,
        norm_bias,
        up_weight,
        up_bias,
        down_weight,
        down_bias,
        layer_scale,
    )
    second_output, kept = run_forward(second_input, validity, forward_weights)
    down_grads, grad_active = down_section(cotangent, validity, backward_weights, kept)
    up_grads, grad_normed = up_section(grad_active, backward_weights, kept)
    front_grads, grad_inputs = front_section(
        grad_normed, cotangent, validity, backward_weights, kept
    )
    summed = (
        lax.psum_scatter(front_grads[0], ("wide", "narrow"), scatter_dimension=1, tiled=True),
        lax.psum_scatter(front_grads[1], ("wide", "narrow"), scatter_dimension=0, tiled=True),
        lax.psum_scatter(front_grads[2], ("wide", "narrow"), scatter_dimension=0, tiled=True),
        lax.psum_scatter(front_grads[3], ("wide", "narrow"), scatter_dimension=0, tiled=True),
        lax.psum_scatter(up_grads[0], ("wide", "narrow"), scatter_dimension=0, tiled=True),
        lax.psum_scatter(up_grads[1], ("wide", "narrow"), scatter_dimension=0, tiled=True),
        lax.psum_scatter(down_grads[0], ("wide", "narrow"), scatter_dimension=0, tiled=True),
        lax.psum_scatter(down_grads[1], ("wide", "narrow"), scatter_dimension=0, tiled=True),
        lax.psum_scatter(down_grads[2], ("wide", "narrow"), scatter_dimension=0, tiled=True),
    )
    return (
        first_output.astype(jnp.bfloat16),
        second_output.astype(jnp.bfloat16),
        grad_inputs.astype(jnp.bfloat16),
        summed[0],
        summed[1],
        summed[2],
        summed[3],
        summed[4],
        summed[5],
        summed[6],
        summed[7],
        summed[8],
    )


def solution(mesh):
    placed = (
        P(("wide", "narrow"), None, None),
        P(("wide", "narrow"), None, None),
        P(("wide", "narrow"), None, None),
        P(("wide", "narrow")),
        P(None, ("wide", "narrow")),
        P(("wide", "narrow")),
        P(("wide", "narrow")),
        P(("wide", "narrow")),
        P(("wide", "narrow"), None),
        P(("wide", "narrow")),
        P(("wide", "narrow"), None),
        P(("wide", "narrow")),
        P(("wide", "narrow")),
    )
    return jax.shard_map(
        on_device,
        mesh=mesh,
        in_specs=placed,
        out_specs=(
            P(("wide", "narrow"), None, None),
            P(("wide", "narrow"), None, None),
            P(("wide", "narrow"), None, None),
            P(None, ("wide", "narrow")),
            P(("wide", "narrow")),
            P(("wide", "narrow")),
            P(("wide", "narrow")),
            P(("wide", "narrow"), None),
            P(("wide", "narrow")),
            P(("wide", "narrow"), None),
            P(("wide", "narrow")),
            P(("wide", "narrow")),
        ),
        check_vma=False,
    )
```

profile of v0, /device:TPU:0, one launch (start us, length us, event | category | flops | bytes accessed | tf_op | source)
XLA Modules:
  0.0 764.9 jit_solution(15539036311810666707)
XLA Ops:
  13.8 42.2 %all-reduce.29 = (bf16[512]{0:T(512)(128)(2,1)S(1)}, bf16[512]{0:T(512)(128)(2,1)S(1)}, bf16[512]{0:T(512)(128)(2,1)S(1)}, bf16[1536]{0:T(1024)(128)(2,1)S(1)}, ...) all-reduce(bf16[512]{0:T(512)(128)(2,1)S(1)} %dynamic-update-slice., ...), channel_id=1, replica_groups=mesh['wide'=8,'narrow'=4] {'wide','narrow'}, use_global_device_ids=true, to_apply=%add.17 | all-reduce | flops 4096 | bytes 16384
  56.0 40.7 %all-gather = bf16[32,16,7]{1,2,0:T(8,128)(2,1)S(1)} all-gather(bf16[1,16,7]{1,2,0:T(8,128)(2,1)} %bitcast.90), channel_id=1, replica_groups=mesh['wide'=8,'narrow'=4] {'wide','narrow'}, dimensions={0}, use_global_device_ids=true | all-gather | bytes 7392 | tf_op jit(solution)/shard_map/all_gather | solution.py:151
  97.8 6.1 convert_multiply_fusion.1
  104.0 31.9 %fusion.98 = (f32[16,256]{1,0:T(8,128)S(1)}, f32[16,256,512]{2,1,0:T(8,128)S(1)}, f32[16,256]{1,0:T(8,128)S(1)}, f32[16,256,512]{2,1,0:T(8,128)}) fusion(f32[512]{0:T(512)S(1)} %bitcast.70, f32[512]{0:T(512)S(1)} %bitcast.72, f32[512]{0:T(512)S(1)} %bitcast.74, f32[16,256,512]{2,1,0:T(8,128)S(1)} %get-tuple-element.54, f32[512]{0:T(512)S(1)} %bitcast.76, ...), kind=kLoop, calls=%fused_computation.170 | loop fusion | flops 62906368 | bytes 33603584 | tf_op jit(solution)/shard_map/reduce_sum | solution.py:18
  135.9 7.2 multiply_reduce_fusion.10
  146.5 4.9 add_convert_fusion.1
  151.4 62.2 %multiply_convert_fusion = (bf16[4096,1536]{1,0:T(8,128)(2,1)}, f32[4096,1536]{1,0:T(8,128)}, f32[4096,1536]{1,0:T(8,128)}) fusion(f32[1536]{0:T(1024)S(1)} %convert_element_type.96, bf16[4096,512]{1,0:T(8,128)(2,1)} %bitcast.63, bf16[512,1536]{1,0:T(8,128)(2,1)} %all-gather.4.cloned.1.call-done), kind=kOutput, calls=%fused_computation.8 | convolution fusion | flops 6857687040 | bytes 68687872 | tf_op jit(solution)/shard_map/dot_general | solution.py:88
  213.6 60.8 %fusion.2.clone.6 = bf16[4096,1536]{1,0:T(8,128)(2,1)} fusion(bf16[4096,512]{1,0:T(8,128)(2,1)S(1)} %bitcast.65, bf16[512,1536]{1,0:T(8,128)(2,1)S(1)} %copy-done.32, f32[1536]{0:T(1024)S(1)} %convert_element_type.96), kind=kOutput, calls=%fused_computation.4.clone.clone.clone.clone.clone.1 | convolution fusion | flops 6857687040 | bytes 18356224 | tf_op jit(solution)/shard_map/dot_general | solution.py:88
  274.5 12.2 %convolution_add_fusion = f32[4096,512]{1,0:T(8,128)} fusion(bf16[4096,1536]{1,0:T(8,128)(2,1)} %get-tuple-element.37, bf16[1536,512]{1,0:T(8,128)(2,1)} %all-gather.6.cloned.1.call-done, f32[512]{0:T(512)S(1)} %copy-done.31), kind=kOutput, calls=%fused_computation.120 | convolution fusion | flops 6444548096 | bytes 22546432 | tf_op jit(solution)/shard_map/dot_general | solution.py:91
  286.8 8.9 %fusion.62 = f32[4096,512]{1,0:T(8,128)} fusion(bf16[1536,512]{1,0:T(8,128)(2,1)S(1)} %copy-done.34, f32[512]{0:T(512)S(1)} %copy-done.31, bf16[4096,1536]{1,0:T(8,128)(2,1)S(1)} %copy-done.35), kind=kOutput, calls=%fused_computation.119 | convolution fusion | flops 6444548096 | bytes 22546432 | tf_op jit(solution)/shard_map/dot_general | solution.py:91
  295.6 11.8 %convert_reduce_fusion.1 = (f32[512]{0:T(512)S(1)}, bf16[16,256,512]{2,1,0:T(8,128)(2,1)}, bf16[16,256,512]{2,1,0:T(8,128)(2,1)}, bf16[16,256,512]{2,1,0:T(8,128)(2,1)}) fusion(f32[512]{0:T(512)S(1)} %copy-done.30, f32[16,256]{1,0:T(8,128)S(1)} %copy-done.9, bf16[16,256,512]{2,1,0:T(8,128)(2,1)S(1)} %copy-done.3, bf16[16,256,512]{2,1,0:T(8,128)(2,1)S(1)} %copy-done.4, ...), kind=kLoop, calls=%fused_computation.92 | loop fusion | flops 33553920 | bytes 41963520 | tf_op jit(solution)/shard_map/reduce_sum | solution.py:105
  307.4 28.2 %convert_reduce_fusion = (f32[1536]{0:T(1024)S(1)}, bf16[4096,1536]{1,0:T(8,128)(2,1)}) fusion(f32[4096,1536]{1,0:T(8,128)} %get-tuple-element.38, bf16[4096,512]{1,0:T(8,128)(2,1)} %bitcast.61, bf16[1536,512]{1,0:T(8,128)(2,1)} %all-gather.6.cloned.1.call-done, f32[4096,1536]{1,0:T(8,128)} %get-tuple-element.65, f32[1536]{0:T(1024)S(1)} %convert_element_type.96), kind=kOutput, calls=%fused_computation.6 | convolution fusion | flops 6549404160 | bytes 68694016 | tf_op jit(solution)/shard_map/dot_general | solution.py:107
  335.6 9.6 %fusion.101 = (f32[512]{0:T(512)S(1)}, f32[4096,512]{1,0:T(8,128)S(1)}) fusion(bf16[4096,1536]{1,0:T(8,128)(2,1)} %get-tuple-element.69, bf16[512,1536]{1,0:T(8,128)(2,1)S(1)} %copy-done.33), kind=kOutput, calls=%fused_computation.173 | convolution fusion | flops 6444547584 | bytes 22546432 | tf_op jit(solution)/shard_map/dot_general | solution.py:118
  345.3 8.1 %multiply_reduce_fusion = (f32[512]{0:T(512)S(1)}, f32[16,256]{1,0:T(8,128)S(1)}) fusion(f32[16,256,512]{2,1,0:T(8,128)} %copy-done, f32[16,256]{1,0:T(8,128)S(1)} %copy-done.11, f32[16,256]{1,0:T(8,128)S(1)} %copy-done.7, f32[4096,512]{1,0:T(8,128)S(1)} %get-tuple-element.67, f32[16,256,512]{2,1,0:T(8,128)S(1)} %bitcast.58, f32[512]{0:T(512)S(1)} %copy-done.15), kind=kLoop, calls=%fused_computation.93 | loop fusion | flops 14675456 | bytes 25219072 | tf_op jit(solution)/shard_map/transpose(jvp())/reduce_sum | solution.py:21
  353.4 7.8 %add_add_fusion = f32[16,256,512]{2,1,0:T(8,128)} fusion(f32[16,256,512]{2,1,0:T(8,128)} %copy-done, f32[16,256]{1,0:T(8,128)S(1)} %multiply_multiply_fusion.10, f32[16,256]{1,0:T(8,128)S(1)} %copy-done.11, f32[16,256]{1,0:T(8,128)S(1)} %copy-done.7, f32[512]{0:T(512)S(1)} %copy-done.15, f32[4096,512]{1,0:T(8,128)S(1)} %get-tuple-element.67), kind=kLoop, calls=%fused_computation.38 | loop fusion | flops 12582912 | bytes 25217024 | tf_op jit(solution)/shard_map/transpose(jvp())/add_any | solution.py:20
  361.3 4.0 reduce_sum.175
  365.4 50.1 %multiply_reduce_fusion.7 = (f32[512]{0:T(512)S(1)}, f32[512]{0:T(512)S(1)}, f32[512]{0:T(512)S(1)}, f32[512]{0:T(512)S(1)}, f32[512]{0:T(512)S(1)}, /*index=5*/...) fusion(f32[16,256,512]{2,1,0:T(8,128)} %copy-done.2, ...), kind=kLoop, calls=%fused_computation.100 | loop fusion | flops 73395712 | bytes 100780032 | tf_op jit(solution)/shard_map/transpose(jvp())/reduce_sum | solution.py:13
  416.4 12.3 %fusion.103 = f32[1536,512]{1,0:T(8,128)} fusion(bf16[4096,1536]{1,0:T(8,128)(2,1)} %get-tuple-element.37, bf16[4096,512]{1,0:T(8,128)(2,1)} %bitcast.62), kind=kOutput, calls=%fused_computation.175 | convolution fusion | flops 6442450944 | bytes 19922944 | tf_op jit(solution)/shard_map/dot_general | solution.py:106
  428.8 12.2 %fusion.102 = f32[512,1536]{1,0:T(8,128)} fusion(bf16[4096,512]{1,0:T(8,128)(2,1)} %bitcast.64, bf16[4096,1536]{1,0:T(8,128)(2,1)} %get-tuple-element.69), kind=kOutput, calls=%fused_computation.174 | convolution fusion | flops 6442450944 | bytes 19922944 | tf_op jit(solution)/shard_map/dot_general | solution.py:117
  441.0 37.2 %all-reduce.28 = (f32[512]{0:T(512)S(1)}, f32[512]{0:T(512)S(1)}, f32[512]{0:T(512)S(1)}, f32[1536]{0:T(1024)S(1)}, f32[512]{0:T(512)S(1)}, /*index=5*/f32[512]{0:T(512)S(1)}) all-reduce(f32[512]{0:T(512)S(1)} %get-tuple-element.20, f32[512]{0:T(512)S(1)} %get-tuple-element.18, ...), channel_id=3, replica_groups=mesh['wide'=8,'narrow'=4] {'wide','narrow'}, use_global_device_ids=true, to_apply=%region_15.16.clone | all-reduce | flops 4096 | bytes 32768
  481.8 23.1 %fusion.57 = bf16[16,256,512]{2,1,0:T(8,128)(2,1)} fusion(bf16[16,256,512]{2,1,0:T(8,128)(2,1)} %param.15, f32[16,256,512]{2,1,0:T(8,128)} %get-tuple-element.48, f32[16,256,512]{2,1,0:T(8,128)} %get-tuple-element.47, f32[16,256,512]{2,1,0:T(8,128)} %get-tuple-element.46, f32[16,256,512]{2,1,0:T(8,128)} %get-tuple-element.43, ...), kind=kLoop, calls=%fused_computation.85 | loop fusion | flops 20971520 | bytes 67125248 | tf_op jit(solution)/shard_map/convert_element_type | solution.py:204
  504.9 41.5 %reduce-scatter.10.cloned.1.call-done = f32[16,7]{1,0:T(8,128)} async-done(((f32[512,7]{1,0:T(8,128)}), f32[16,7]{1,0:T(8,128)}) %reduce-scatter.10.cloned.1.call-update) | async-done | bytes 464
  547.8 102.9 %reduce-scatter.8.cloned.1.call-done = f32[48,512]{1,0:T(8,128)} async-done(((f32[1536,512]{1,0:T(8,128)}), f32[48,512]{1,0:T(8,128)}) %reduce-scatter.8.cloned.1.call-update) | async-done | bytes 98320 | tf_op jit(solution)/shard_map/reduce_scatter | solution.py:197
  650.7 107.3 %reduce-scatter.6.cloned.1.call-done = f32[16,1536]{1,0:T(8,128)} async-done(((f32[512,1536]{1,0:T(8,128)}), f32[16,1536]{1,0:T(8,128)}) %reduce-scatter.6.cloned.1.call-update) | async-done | bytes 98320 | tf_op jit(solution)/shard_map/reduce_scatter | solution.py:195
  (128 shorter events, 17.0 us)
Async XLA Ops:
  7.2 144.2 %all-gather.4.cloned.1.call-start = ((), (), s32[]{:S(2)}) async-start(), calls=%async_computation.3 | async-start | bytes 1622016 | tf_op jit(solution)/shard_map/all_gather | solution.py:155
  7.9 266.6 %all-gather.6.cloned.1.call-start = ((), (), s32[]{:S(2)}) async-start(), calls=%async_computation.4 | async-start | bytes 1622016 | tf_op jit(solution)/shard_map/all_gather | solution.py:157
  8.7 537.8 %reduce-scatter.10.cloned.1.call-start = ((), (), s32[]{:S(2)}) async-start(), calls=%async_computation.7 | async-start | bytes 270336
  97.0 6.9 copy-start.16
  103.9 32.0 %copy-start.2 = (f32[16,256,512]{2,1,0:T(8,128)}, f32[16,256,512]{2,1,0:T(8,128)S(1)}, u32[]{:S(2)}) copy-start(f32[16,256,512]{2,1,0:T(8,128)S(1)} %get-tuple-element.54) | copy-start | bytes 25165828
  135.9 10.6 %copy-start = (f32[16,256,512]{2,1,0:T(8,128)}, f32[16,256,512]{2,1,0:T(8,128)S(1)}, u32[]{:S(2)}) copy-start(f32[16,256,512]{2,1,0:T(8,128)S(1)} %get-tuple-element.40) | copy-start | bytes 25165828
  135.9 10.6 %slice-start = ((s8[8388608]{0:T(1024)(128)(4,1)}), s8[4194304]{0:T(1024)(128)(4,1)S(1)}, s32[]{:S(2)}) async-start(s8[8388608]{0:T(1024)(128)(4,1)} %bitcast.59), calls=%async_computation.8 | async-start | bytes 8388608
  151.4 62.2 %copy-start.5 = (bf16[16,256,512]{2,1,0:T(8,128)(2,1)S(1)}, bf16[16,256,512]{2,1,0:T(8,128)(2,1)}, u32[]{:S(2)}) copy-start(bf16[16,256,512]{2,1,0:T(8,128)(2,1)} %get-tuple-element.64) | copy-start | bytes 12582916
  151.4 62.2 %copy-start.32 = (bf16[512,1536]{1,0:T(8,128)(2,1)S(1)}, bf16[512,1536]{1,0:T(8,128)(2,1)}, u32[]{:S(2)}) copy-start(bf16[512,1536]{1,0:T(8,128)(2,1)} %all-gather.4.cloned.1.call-done) | copy-start | bytes 4718596
  213.6 60.9 %copy-start.31 = (f32[512]{0:T(512)S(1)}, f32[512]{0:T(512)}, u32[]{:S(2)}) copy-start(f32[512]{0:T(512)} %convert_element_type.98) | copy-start | bytes 6148
  274.5 12.2 %copy-start.34 = (bf16[1536,512]{1,0:T(8,128)(2,1)S(1)}, bf16[1536,512]{1,0:T(8,128)(2,1)}, u32[]{:S(2)}) copy-start(bf16[1536,512]{1,0:T(8,128)(2,1)} %all-gather.6.cloned.1.call-done) | copy-start | bytes 4718596
  274.5 12.2 %copy-start.35 = (bf16[4096,1536]{1,0:T(8,128)(2,1)S(1)}, bf16[4096,1536]{1,0:T(8,128)(2,1)}, u32[]{:S(2)}) copy-start(bf16[4096,1536]{1,0:T(8,128)(2,1)} %fusion.2.clone.6) | copy-start | bytes 37748740
  286.7 8.9 %copy-start.3 = (bf16[16,256,512]{2,1,0:T(8,128)(2,1)S(1)}, bf16[16,256,512]{2,1,0:T(8,128)(2,1)}, u32[]{:S(2)}) copy-start(bf16[16,256,512]{2,1,0:T(8,128)(2,1)} %param.15) | copy-start | bytes 12582916
  286.7 8.9 %copy-start.4 = (bf16[16,256,512]{2,1,0:T(8,128)(2,1)S(1)}, bf16[16,256,512]{2,1,0:T(8,128)(2,1)}, u32[]{:S(2)}) copy-start(bf16[16,256,512]{2,1,0:T(8,128)(2,1)} %param.14) | copy-start | bytes 12582916
  286.7 8.9 %copy-start.9 = (f32[16,256]{1,0:T(8,128)S(1)}, f32[16,256]{1,0:T(8,128)}, u32[]{:S(2)}) copy-start(f32[16,256]{1,0:T(8,128)} %copy-done.8) | copy-start | bytes 49156
  286.8 8.9 %copy-start.30 = (f32[512]{0:T(512)S(1)}, f32[512]{0:T(512)}, u32[]{:S(2)}) copy-start(f32[512]{0:T(512)} %convert_element_type.90) | copy-start | bytes 6148
  307.4 28.2 %copy-start.33 = (bf16[512,1536]{1,0:T(8,128)(2,1)S(1)}, bf16[512,1536]{1,0:T(8,128)(2,1)}, u32[]{:S(2)}) copy-start(bf16[512,1536]{1,0:T(8,128)(2,1)} %all-gather.4.cloned.1.call-done) | copy-start | bytes 4718596
  335.6 9.6 %copy-start.7 = (f32[16,256]{1,0:T(8,128)S(1)}, f32[16,256]{1,0:T(8,128)}, u32[]{:S(2)}) copy-start(f32[16,256]{1,0:T(8,128)} %copy-done.6) | copy-start | bytes 49156
  335.6 9.6 %copy-start.11 = (f32[16,256]{1,0:T(8,128)S(1)}, f32[16,256]{1,0:T(8,128)}, u32[]{:S(2)}) copy-start(f32[16,256]{1,0:T(8,128)} %copy-done.10) | copy-start | bytes 49156
  335.6 9.6 %copy-start.15 = (f32[512]{0:T(512)S(1)}, f32[512]{0:T(512)}, u32[]{:S(2)}) copy-start(f32[512]{0:T(512)} %copy-done.14) | copy-start | bytes 6148
  345.2 8.2 %copy-start.1 = (f32[4096,512]{1,0:T(8,128)}, f32[4096,512]{1,0:T(8,128)S(1)}, u32[]{:S(2)}) copy-start(f32[4096,512]{1,0:T(8,128)S(1)} %get-tuple-element.67) | copy-start | bytes 25165828
  345.3 8.1 %copy-start.13 = (f32[16,256]{1,0:T(8,128)S(1)}, f32[16,256]{1,0:T(8,128)}, u32[]{:S(2)}) copy-start(f32[16,256]{1,0:T(8,128)} %copy-done.12) | copy-start | bytes 49156
  416.3 234.3 %reduce-scatter.8.cloned.1.call-start = ((), (), s32[]{:S(2)}) async-start(), calls=%async_computation.6 | async-start | bytes 3244032 | tf_op jit(solution)/shard_map/reduce_scatter | solution.py:197
  428.7 329.2 %reduce-scatter.6.cloned.1.call-start = ((), (), s32[]{:S(2)}) async-start(), calls=%async_computation.5 | async-start | bytes 3244032 | tf_op jit(solution)/shard_map/reduce_scatter | solution.py:195
  (19 other events, 85.7 us)
Sparse Core Ops, SparseCore 0:
  10.9 57.7 all-gather.3
  71.6 53.9 all-gather.5
  416.5 129.9 reduce-scatter.9
  553.2 97.4 reduce-scatter.7
  657.4 100.4 reduce-scatter.5
where the time goes:
time: 775 us; the launch traced here: 765 us
  waiting for transfers between devices  253 us (33%)
  matrix products  206 us (27%)
  other arithmetic  158 us (20%)
  blocking collectives  120 us (15%)
  between operations  14.8 us (2%)
  local copies, waits for them, and re-layouts  11.9 us (2%)
    dot_general x2, matrix products, run_forward(): jnp.dot(normed_low, up_weight, preferred_element_type=jnp.float32)  123 us
    reduce_scatter x1, waiting for transfers between devices, on_device(): lax.psum_scatter(up_grads[0], ('wide', 'narrow'), scatter_dimension=0, ti...  107 us
    reduce_scatter x1, waiting for transfers between devices, on_device(): lax.psum_scatter(down_grads[0], ('wide', 'narrow'), scatter_dimension=0,...  103 us
    unnamed x2, blocking collectives  79.4 us
    reduce_sum x1, other arithmetic, depthwise(): result = result + kernel_taps[offset] * padded[:, offset:offset + frames]  50.1 us
    unnamed x6, waiting for transfers between devices  43 us
    all_gather x1, blocking collectives, on_device(): lax.all_gather(conv_weight, ('wide', 'narrow'), axis=1, tiled=True)  40.7 us
    reduce_sum x1, other arithmetic, normalize(): average = jnp.mean(conv_out, axis=-1, keepdims=True)  31.9 us
  transfers between devices with their start and end apart: 5, of which 3 were waited for; matrix products, arithmetic and copies ran while one was open for 31% of the time, Pallas kernels for 0%

commit v1 on v0

v1 whole, which is shorter than its diff:
```python
import functools
import math

import jax
import jax.numpy as jnp
from jax import lax
from jax.experimental import pallas as pl
from jax.experimental.pallas import tpu as pltpu
from jax.sharding import Mesh
from jax.sharding import PartitionSpec as P

bf16, f32 = jnp.bfloat16, jnp.float32
AXES = ("wide", "half", "core")
CHIPS = ("wide", "half")
ROOT = math.sqrt(0.5)
LANES = 128
HALO = 8
TAIL = 32
SMALL = 16
VMEM = 60 * 2**20
BLOCK = 4

TAPS = 7
CONV_BIAS, GAIN, SHIFT, DOWN_BIAS, SCALE, UP_BIAS = 7, 8, 9, 10, 11, 12


def dot(a, b, ca=1, cb=0, precision=None):
    return lax.dot_general(
        a, b, (((ca,), (cb,)), ((), ())), precision=precision, preferred_element_type=f32
    )


def whole(shape):
    return pl.BlockSpec(shape, lambda i: (0,) * len(shape))


def smem():
    return pl.BlockSpec(memory_space=pltpu.SMEM)


def tail_mask(frames, length, width):
    row = lax.broadcasted_iota(jnp.int32, (TAIL, width), 0) + (frames - TAIL)
    return row < length


def fill_padded(x_ref, m, length, pad_ref):
    frames = x_ref.shape[1]
    body = frames - TAIL
    keep = tail_mask(frames, length, LANES)
    for c in range(x_ref.shape[2] // LANES):
        cs = slice(c * LANES, (c + 1) * LANES)
        x = x_ref[m, :, cs].astype(f32)
        pad_ref[m, c, HALO : HALO + body] = x[:body]
        pad_ref[m, c, HALO + body : HALO + frames] = jnp.where(keep, x[body:], 0.0)


def clear_halo(pad_ref, frames):
    zeros = jnp.zeros(pad_ref.shape[:2] + (HALO, LANES), f32)
    pad_ref[:, :, :HALO] = zeros
    pad_ref[:, :, HALO + frames :] = zeros


def conv_norm(pad_ref, m, small_ref, frames):
    parts = []
    for c in range(pad_ref.shape[1]):
        cs = slice(c * LANES, (c + 1) * LANES)
        acc = small_ref[CONV_BIAS : CONV_BIAS + 1, cs]
        for k in range(TAPS):
            start = HALO + k - TAPS // 2
            acc = acc + small_ref[k : k + 1, cs] * pad_ref[m, c, start : start + frames]
        parts.append(acc)
    conv = jnp.concatenate(parts, axis=1)
    centred = conv - jnp.mean(conv, axis=-1, keepdims=True)
    rstd = lax.rsqrt(jnp.mean(centred * centred, axis=-1, keepdims=True) + 1e-06)
    return (centred * rstd).astype(bf16), rstd


def store_output(out_ref, m, length, x_ref, branch):
    frames = x_ref.shape[1]
    body = frames - TAIL
    keep = tail_mask(frames, length, x_ref.shape[2])
    value = x_ref[m].astype(f32) + branch
    out_ref[m, :body] = value[:body].astype(bf16)
    out_ref[m, body:] = jnp.where(keep, value[body:], 0.0).astype(bf16)


def store_masked(dst_ref, m, length, src_ref):
    frames = src_ref.shape[1]
    body = frames - TAIL
    keep = tail_mask(frames, length, src_ref.shape[2])
    at = m * frames
    dst_ref[at : at + body] = src_ref[m, :body]
    dst_ref[at + body : at + frames] = jnp.where(keep, src_ref[m, body:].astype(f32), 0.0).astype(bf16)


def second_forward(
    len_ref, owner_ref, x_ref, cot_ref, *refs
):
    count = len(refs) - 15
    block_refs = [ref.at[j] for ref in refs[:count] for j in range(ref.shape[0])]
    second_forward_body(len_ref, owner_ref, x_ref, cot_ref, block_refs, *refs[count:])


def second_forward_body(
    len_ref, owner_ref, x_ref, cot_ref, block_refs,
    out_ref, xhat_ref, slope_ref, rstd_ref, up_ref, down_ref, small_ref, bias_ref, gdown_ref, rows_ref,
    pad_ref, act_ref, mcot_ref, acc_ref, csum_ref,
):
    step = pl.program_id(0)
    clips, frames, width = x_ref.shape
    hidden = up_ref.shape[1]
    parts = hidden // width

    @pl.when(step == 0)
    def _():
        devices = len(block_refs)
        up_rows, down_rows = width // devices, hidden // devices
        clear_halo(pad_ref, frames)
        small = jnp.zeros((SMALL, width), f32)
        for ref in block_refs:
            small = small + ref[2 * down_rows :].astype(f32)
        small_ref[...] = small
        scale = small[SCALE : SCALE + 1] * ROOT
        for j, ref in enumerate(block_refs):
            owner = owner_ref[j]
            at = pl.multiple_of(owner * up_rows, up_rows)
            for p in range(parts):
                up_ref[pl.ds(at, up_rows), p * width : (p + 1) * width] = ref[p * up_rows : (p + 1) * up_rows]
            at = pl.multiple_of(owner * down_rows, down_rows)
            down_ref[pl.ds(at, down_rows)] = (ref[down_rows : 2 * down_rows].astype(f32) * scale).astype(bf16)
        ratio = small[SHIFT : SHIFT + 1] / small[GAIN : GAIN + 1]
        shift = dot(
            jnp.broadcast_to(ratio, (8, width)), up_ref[...].astype(f32), precision=lax.Precision.HIGHEST
        )
        for p in range(parts):
            cs = slice(p * width, (p + 1) * width)
            bias_ref[:, cs] = shift[:, cs] + small[UP_BIAS + p : UP_BIAS + p + 1] * ROOT
        acc_ref[...] = jnp.zeros_like(acc_ref)
        csum_ref[...] = jnp.zeros_like(csum_ref)

    lengths = [len_ref[step * clips + m] for m in range(clips)]
    for m in range(clips):
        fill_padded(x_ref, m, lengths[m], pad_ref)
        xhat, rstd = conv_norm(pad_ref, m, small_ref, frames)
        xhat_ref[m * frames : (m + 1) * frames] = xhat
        rstd_ref[m * frames : (m + 1) * frames] = jnp.broadcast_to(rstd, (frames, LANES))
        store_masked(mcot_ref, m, lengths[m], cot_ref)

    xhat = xhat_ref[...]
    for p in range(parts):
        cs = slice(p * width, (p + 1) * width)
        u = dot(xhat, up_ref[:, cs]) + bias_ref[0:1, cs]
        s = 1.0 + lax.erf(u)
        act_ref[:, cs] = (u * s).astype(bf16)
        bell = jnp.exp2(u * u * (-math.log2(math.e)))
        slope_ref[:, cs] = (s + u * bell * (2.0 / math.sqrt(math.pi))).astype(bf16)

    down_bias = small_ref[DOWN_BIAS : DOWN_BIAS + 1] * small_ref[SCALE : SCALE + 1]
    branch = dot(act_ref[...], down_ref[...]) + down_bias
    for m in range(clips):
        store_output(out_ref, m, lengths[m], x_ref, branch[m * frames : (m + 1) * frames])

    mcot = mcot_ref[...]
    acc_ref[...] += dot(act_ref[...], mcot, 0, 0)
    csum_ref[...] += jnp.sum(mcot.astype(f32).reshape(-1, 8, width), axis=0)

    @pl.when(step == pl.num_programs(0) - 1)
    def _():
        total = acc_ref[...]
        gdown_ref[...] = total.astype(bf16)
        scale = small_ref[SCALE : SCALE + 1]
        csum = jnp.sum(csum_ref[...], axis=0, keepdims=True)
        cross = jnp.sum(total * down_ref[...].astype(f32), axis=0, keepdims=True)
        rows_ref[0:1] = csum * scale
        rows_ref[1:2] = cross / scale + csum * small_ref[DOWN_BIAS : DOWN_BIAS + 1]
        rows_ref[2:8] = jnp.zeros((6, width), f32)


def second_backward(
    packed, len_ref, core_ref, cot_ref, x_ref, xhat_ref, slope_ref, rstd_ref, up_ref, down_ref, small_ref, down_rows_ref, _,
    grad_ref, out_a_ref, out_b_ref,
    pad_ref, gh_ref, mcot_ref, acc_ref, hsum_ref, tsum_ref,
):
    step = pl.program_id(0)
    clips, frames, width = x_ref.shape
    hidden = up_ref.shape[1]
    parts = hidden // width

    @pl.when(step == 0)
    def _():
        clear_halo(pad_ref, frames)
        acc_ref[...] = jnp.zeros_like(acc_ref)
        hsum_ref[...] = jnp.zeros_like(hsum_ref)
        tsum_ref[...] = jnp.zeros_like(tsum_ref)

    lengths = [len_ref[step * clips + m] for m in range(clips)]
    for m in range(clips):
        store_masked(mcot_ref, m, lengths[m], cot_ref)
    mcot = mcot_ref[...]
    for p in range(parts):
        cs = slice(p * width, (p + 1) * width)
        ga = dot(mcot, down_ref[cs, :], 1, 1)
        gh = ga * slope_ref[:, cs].astype(f32)
        hsum_ref[:, cs] += jnp.sum(gh.reshape(-1, 8, width), axis=0)
        gh_ref[:, cs] = gh.astype(bf16)
    acc_ref[...] += dot(xhat_ref[...], gh_ref[...], 0, 0)
    g = dot(gh_ref[...], up_ref[...], 1, 1)
    for m in range(clips):
        rows = slice(m * frames, (m + 1) * frames)
        gm = g[rows]
        xhat = xhat_ref[rows].astype(f32)
        mean = jnp.mean(gm, axis=-1, keepdims=True)
        proj = jnp.mean(gm * xhat, axis=-1, keepdims=True)
        rstd = rstd_ref[rows]
        for c in range(width // LANES):
            cs = slice(c * LANES, (c + 1) * LANES)
            gc = (gm[:, cs] - mean - xhat[:, cs] * proj) * rstd
            pad_ref[m, c, HALO : HALO + frames] = gc
            tsum_ref[TAPS, :, cs] += jnp.sum(gc.reshape(-1, 8, LANES), axis=0)
    body = frames - TAIL
    for m in range(clips):
        keep = tail_mask(frames, lengths[m], LANES)
        for c in range(width // LANES):
            cs = slice(c * LANES, (c + 1) * LANES)
            x = x_ref[m, :, cs].astype(f32)
            x = jnp.concatenate([x[:body], jnp.where(keep, x[body:], 0.0)], axis=0)
            total = cot_ref[m, :, cs].astype(f32)
            for k in range(TAPS):
                start = HALO + TAPS // 2 - k
                gc = pad_ref[m, c, start : start + frames]
                total = total + small_ref[k : k + 1, cs] * gc
                tsum_ref[k, :, cs] += jnp.sum((gc * x).reshape(-1, 8, LANES), axis=0)
            grad_ref[m, :body, cs] = total[:body].astype(bf16)
            grad_ref[m, body:, cs] = jnp.where(keep, total[body:], 0.0).astype(bf16)

    @pl.when(step == pl.num_programs(0) - 1)
    def _():
        total = acc_ref[...]
        hsum = jnp.sum(hsum_ref[...], axis=0, keepdims=True)
        columns = small_ref[...].T
        gain, shift = columns[:, GAIN : GAIN + 1], columns[:, SHIFT : SHIFT + 1]
        total_up = (gain * total + shift * hsum) * ROOT
        up = up_ref[...].astype(f32)
        ones = jnp.ones((8, hidden), f32)
        exact = lax.Precision.HIGHEST
        inverse = 1.0 / small_ref[GAIN : GAIN + 1]
        rows = [jnp.sum(tsum_ref[k], axis=0, keepdims=True) for k in range(TAPS + 1)]
        rows.append(dot(ones, up * total, 1, 1, exact)[:1] * inverse)
        rows.append(dot(jnp.broadcast_to(hsum, (8, hidden)), up, 1, 1, exact)[:1] * inverse)
        rows.append(down_rows_ref[0:2])
        if not packed:
            out_a_ref[...] = total_up.astype(bf16)
            rows += [hsum[:, p * width : (p + 1) * width] * ROOT for p in range(parts)]
            rows.append(jnp.zeros((SMALL - UP_BIAS - parts, width), f32))
            out_b_ref[...] = jnp.concatenate(rows, axis=0)
            return
        rows.append(jnp.zeros((SMALL - UP_BIAS, width), f32))
        rows = jnp.concatenate(rows, axis=0)
        bias = hsum * ROOT
        lane = lax.broadcasted_iota(jnp.int32, (SMALL, LANES), 1)
        line = lax.broadcasted_iota(jnp.int32, (SMALL, LANES), 0)
        devices = width // 16
        for owner in range(devices):
            ref = out_a_ref if owner % 2 == 0 else out_b_ref
            for c in range(hidden // LANES):
                ref[owner // 2, c * 16 : (c + 1) * 16] = total_up[
                    owner * 16 : (owner + 1) * 16, c * LANES : (c + 1) * LANES
                ].astype(bf16)
            at = owner * 16 // LANES * LANES
            mine = pltpu.roll(rows[:, at : at + LANES], (LANES - owner * 16 % LANES) % LANES, 1)
            for r in range(parts):
                first = owner * 16 * parts + r * 16
                at = first // LANES * LANES
                part = pltpu.roll(
                    jnp.broadcast_to(bias[:, at : at + LANES], (SMALL, LANES)), (LANES - first % LANES) % LANES, 1
                )
                mine = jnp.where(line == UP_BIAS + r, part, mine)
            high = mine.astype(bf16).astype(f32)
            low = pltpu.roll(mine - high, LANES // 2, 1)
            mine = jnp.where(lane < 16, high, jnp.where((lane >= LANES // 2) & (lane < LANES // 2 + 16), low, 0.0))
            ref[owner // 2, hidden // LANES * 16 :] = mine.astype(bf16)


def first_forward(len_ref, x_ref, up_ref, down_ref, small_ref, bias_ref, _, out_ref, pad_ref, xhat_ref, act_ref):
    step = pl.program_id(0)
    clips, frames, width = x_ref.shape
    parts = up_ref.shape[1] // width

    @pl.when(step == 0)
    def _():
        clear_halo(pad_ref, frames)

    lengths = [len_ref[step * clips + m] for m in range(clips)]
    for m in range(clips):
        fill_padded(x_ref, m, lengths[m], pad_ref)
        xhat_ref[m * frames : (m + 1) * frames] = conv_norm(pad_ref, m, small_ref, frames)[0]
    xhat = xhat_ref[...]
    for p in range(parts):
        cs = slice(p * width, (p + 1) * width)
        u = dot(xhat, up_ref[:, cs]) + bias_ref[0:1, cs]
        act_ref[:, cs] = (u * (1.0 + lax.erf(u))).astype(bf16)
    down_bias = small_ref[DOWN_BIAS : DOWN_BIAS + 1] * small_ref[SCALE : SCALE + 1]
    branch = dot(act_ref[...], down_ref[...]) + down_bias
    for m in range(clips):
        store_output(out_ref, m, lengths[m], x_ref, branch[m * frames : (m + 1) * frames])


def kernel_call(body, name, args, specs, outs, scratch, steps, flops, elements):
    def size(a):
        return math.prod(a.shape) * jnp.dtype(a.dtype).itemsize

    return pl.pallas_call(
        body,
        grid=(steps,),
        in_specs=specs,
        out_specs=[spec for _, spec in outs],
        out_shape=[shape for shape, _ in outs],
        scratch_shapes=scratch,
        compiler_params=pltpu.CompilerParams(vmem_limit_bytes=VMEM),
        cost_estimate=pl.CostEstimate(
            flops=flops,
            bytes_accessed=sum(map(size, args)) + sum(size(s) for s, _ in outs),
            transcendentals=elements,
        ),
        name=name,
    )(*args)


def shape(dims, dtype):
    return jax.ShapeDtypeStruct(dims, dtype)


def own_block(
    me_ref, conv_ref, conv_bias_ref, gain_ref, shift_ref, up_ref, up_bias_ref, down_ref, down_bias_ref, scale_ref,
    block_ref,
    row_ref,
):
    own, hidden = up_ref.shape
    rows, width = down_ref.shape
    parts = hidden // width
    me = me_ref[0]
    i = lax.broadcasted_iota(jnp.int32, (own, own), 0)
    j = lax.broadcasted_iota(jnp.int32, (own, own), 1)
    scaled = dot(jnp.where(i == j, gain_ref[...].astype(f32), 0.0).astype(bf16), up_ref[...]) * ROOT
    for p in range(parts):
        block_ref[p * own : (p + 1) * own] = scaled[:, p * width : (p + 1) * width].astype(bf16)
    block_ref[rows : 2 * rows] = down_ref[...]
    vectors = [r[...].astype(f32) for r in (conv_bias_ref, gain_ref, shift_ref, down_bias_ref, scale_ref)]
    small = jnp.concatenate([conv_ref[...].astype(f32)] + vectors + [jnp.zeros((SMALL - UP_BIAS, own), f32)], axis=0)
    small = jnp.concatenate([small, jnp.zeros((SMALL, LANES - own), f32)], axis=1)
    row_ref[...] = jnp.zeros_like(row_ref)
    per = LANES // own
    at = pl.multiple_of(me // per * LANES, LANES)
    row_ref[:, pl.ds(at, LANES)] = pltpu.roll(small, me % per * own, 1)
    bias = jnp.concatenate([up_bias_ref[...].astype(f32), jnp.zeros((1, 2 * LANES - rows), f32)], axis=1)
    bias = pltpu.roll(jnp.broadcast_to(bias, (8, 2 * LANES)), me * rows % LANES, 1)
    first = me * rows // LANES
    tiles = width // LANES
    for t in range(hidden // LANES):
        part = jnp.where(first == t, bias[:1, :LANES], jnp.where(first + 1 == t, bias[:1, LANES:], 0.0))
        row_ref[UP_BIAS + t // tiles : UP_BIAS + t // tiles + 1, t % tiles * LANES : (t % tiles + 1) * LANES] = part

    block_ref[2 * rows :] = row_ref[...].astype(bf16)


def quick(width, hidden, devices):
    return devices == 32 and width == 16 * devices and hidden % width == 0


def flipped(a, bits, devices):
    return lax.ppermute(a, AXES, [(i, i ^ bits) for i in range(devices)])


def gather_weights(weights, devices):
    conv_weight, conv_bias, gain, shift, up, up_bias, down, down_bias, scale = weights
    up_rows, hidden = up.shape
    down_rows, width = down.shape
    parts = hidden // width
    me = lax.axis_index(AXES).astype(jnp.int32)
    if quick(width, hidden, devices):
        row = lambda v: v.reshape(1, -1)
        args = (me.reshape(1), conv_weight, row(conv_bias), row(gain), row(shift), up, row(up_bias), down, row(down_bias), row(scale))
        block = pl.pallas_call(
            own_block,
            in_specs=[smem()] + [pl.BlockSpec(memory_space=pltpu.VMEM)] * 9,
            out_specs=pl.BlockSpec(memory_space=pltpu.VMEM),
            out_shape=shape((2 * down_rows + SMALL, width), bf16),
            scratch_shapes=[pltpu.VMEM((SMALL, width), f32)],
            name="own_block",
        )(*args)
        both = jnp.stack([block, flipped(block, 16, devices)])
        have = {0: both}
        for flip, start in ((8, 0), (4, 0), (2, 0), (2, 4), (8, 2), (4, 8), (8, 6)):
            have[flip ^ start] = flipped(have[start], flip, devices)
        for start in list(have):
            have[start ^ 1] = flipped(have[start], 1, devices)
        order = [start ^ far for start in have for far in (0, 16)]
        return list(have.values()), me ^ jnp.array(order, jnp.int32)
    everyone = lambda a, axis: lax.all_gather(a, AXES, axis=axis, tiled=True)
    up = (up.astype(f32) * gain.astype(f32)[:, None] * ROOT).astype(bf16)
    up, down, up_bias = everyone(up, 0), everyone(down, 0), everyone(up_bias, 0)
    vectors = jnp.stack([conv_bias, gain, shift, down_bias, scale])
    small = jnp.concatenate([everyone(conv_weight, 1), everyone(vectors, 1), up_bias.reshape(parts, width)], axis=0)
    small = jnp.pad(small, ((0, SMALL - small.shape[0]), (0, 0)))
    count = width // 16
    up = up.reshape(count, 16, parts, width).swapaxes(1, 2).reshape(count, 16 * parts, width)
    down = down.reshape(count, 16 * parts, width)
    small = jnp.pad(small[None], ((0, count - 1), (0, 0), (0, 0)))
    return [jnp.concatenate([up, down, small], axis=1)], jnp.arange(count, dtype=jnp.int32)


def add_pair(keep_ref, got_ref, _, out_ref):
    out_ref[...] = (keep_ref[...].astype(f32) + got_ref[...].astype(f32)).astype(bf16)


def pair_sum(keep, got, after):
    half = keep.shape[0] // 2
    spec = pl.BlockSpec((half,) + keep.shape[1:], lambda i: (i, 0, 0))
    return pl.pallas_call(
        add_pair,
        grid=(2,),
        in_specs=[spec, spec, pl.BlockSpec(memory_space=pl.ANY)],
        out_specs=spec,
        out_shape=shape(keep.shape, bf16),
        name="add_pair",
    )(keep, got, after)


def finish(down_ref, up_ref, small_ref, grad_down_ref, grad_up_ref, rows_ref):
    total = jnp.zeros(down_ref.shape[1:], f32)
    for j in range(down_ref.shape[0]):
        total = total + down_ref[j].astype(f32)
    grad_down_ref[...] = total * (small_ref[SCALE : SCALE + 1] * ROOT)
    total = jnp.zeros(up_ref.shape[1:], f32)
    for j in range(up_ref.shape[0]):
        total = total + up_ref[j].astype(f32)
    own, hidden = grad_up_ref.shape
    for c in range(hidden // LANES):
        grad_up_ref[:, c * LANES : (c + 1) * LANES] = total[c * own : (c + 1) * own]
    rest = total[hidden // LANES * own :]
    rows_ref[...] = rest + pltpu.roll(rest, LANES // 2, 1)


def on_device(chips, first_input, second_input, cotangent, lengths, *weights):
    clips, frames, width = second_input.shape
    hidden = weights[6].shape[0] * chips * 2
    tokens = clips * frames
    block = math.gcd(clips, BLOCK)
    steps = clips // block
    rows = block * frames
    core = lax.axis_index("core").astype(jnp.int32)
    matmul = 2 * tokens * width * hidden

    blocks, owners = gather_weights(weights, chips * 2)

    clip_spec = pl.BlockSpec((block, frames, width), lambda i: (i, 0, 0))
    row_spec = lambda n: pl.BlockSpec((rows, n), lambda i: (i, 0))
    clip_out = (shape(second_input.shape, bf16), clip_spec)
    pad = pltpu.VMEM((block, width // LANES, frames + 2 * HALO, LANES), f32)

    second_output, xhat, slope, rstd, up, down, small, bias, gdown, down_grad_rows = kernel_call(
        second_forward,
        "second_forward",
        (lengths, owners, second_input, cotangent, *blocks),
        [smem(), smem(), clip_spec, clip_spec] + [whole(b.shape) for b in blocks],
        [
            clip_out,
            (shape((tokens, width), bf16), row_spec(width)),
            (shape((tokens, hidden), bf16), row_spec(hidden)),
            (shape((tokens, LANES), f32), row_spec(LANES)),
            (shape((width, hidden), bf16), whole((width, hidden))),
            (shape((hidden, width), bf16), whole((hidden, width))),
            (shape((SMALL, width), f32), whole((SMALL, width))),
            (shape((8, hidden), f32), whole((8, hidden))),
            (shape((hidden, width), bf16), whole((hidden, width))),
            (shape((8, width), f32), whole((8, width))),
        ],
        [
            pad,
            pltpu.VMEM((rows, hidden), bf16),
            pltpu.VMEM((rows, width), bf16),
            pltpu.VMEM((hidden, width), f32),
            pltpu.VMEM((8, width), f32),
        ],
        steps,
        3 * matmul,
        2 * tokens * hidden,
    )

    devices = chips * 2
    fast = quick(width, hidden, devices)
    if fast:
        gdown_parts = lax.all_to_all(gdown.reshape(devices, hidden // devices, width), AXES, 0, 0, tiled=True)
        payload = shape((chips, hidden // LANES * 16 + SMALL, LANES), bf16)
        outs = [(payload, whole(payload.shape))] * 2
    else:
        outs = [
            (shape((width, hidden), bf16), whole((width, hidden))),
            (shape((SMALL, width), f32), whole((SMALL, width))),
        ]

    input_grad, out_a, out_b = kernel_call(
        functools.partial(second_backward, fast),
        "second_backward",
        (lengths, core.reshape(1), cotangent, second_input, xhat, slope, rstd, up, down, small, down_grad_rows, gdown),
        [
            smem(), smem(), clip_spec, clip_spec, row_spec(width), row_spec(hidden), row_spec(LANES),
            whole(up.shape), whole(down.shape), whole(small.shape), whole(down_grad_rows.shape),
            pl.BlockSpec(memory_space=pl.ANY),
        ],
        [
            clip_out,
            *outs,
        ],
        [
            pad,
            pltpu.VMEM((rows, hidden), bf16),
            pltpu.VMEM((rows, width), bf16),
            pltpu.VMEM((width, hidden), f32),
            pltpu.VMEM((8, hidden), f32),
            pltpu.VMEM((TAPS + 1, 8, width), f32),
        ],
        steps,
        3 * matmul,
        0,
    )

    if fast:
        keep = jnp.where(core == 0, out_a, out_b)
        got = flipped(jnp.where(core == 0, out_b, out_a), 1, devices)
        gup_pair = pair_sum(keep, got, gdown_parts)
        gup_parts = lax.all_to_all(gup_pair, CHIPS, 0, 0, tiled=True)
    else:
        gup_pair = out_a

    (first_output,) = kernel_call(
        first_forward,
        "first_forward",
        (lengths, first_input, up, down, small, bias, gup_pair),
        [
            smem(), clip_spec, whole(up.shape), whole(down.shape), whole(small.shape), whole(bias.shape),
            pl.BlockSpec(memory_space=pl.ANY),
        ],
        [clip_out],
        [pad, pltpu.VMEM((rows, width), bf16), pltpu.VMEM((rows, hidden), bf16)],
        steps,
        2 * matmul,
        tokens * hidden,
    )

    own = width // devices
    if fast:
        grad_down, grad_up, sums = pl.pallas_call(
            finish,
            out_shape=[shape((hidden // devices, width), f32), shape((own, hidden), f32), shape((SMALL, LANES), f32)],
            name="finish",
        )(gdown_parts, gup_parts, small)
        vector = lambda r: sums[r, :own]
        grad_taps = sums[:TAPS, :own]
        grad_up_bias = sums[UP_BIAS : UP_BIAS + hidden // width, :own].reshape(-1)
    else:
        scatter = lambda a: lax.psum_scatter(a.astype(f32), AXES, scatter_dimension=0, tiled=True)
        me = lax.axis_index(AXES)
        grad_down = scatter(gdown) * (small[SCALE] * ROOT)
        grad_up = scatter(out_a)
        sums = lax.psum(out_b, AXES)
        vector = lambda r: lax.dynamic_slice(sums[r], (me * own,), (own,))
        grad_taps = lax.dynamic_slice(sums, (0, me * own), (TAPS, own))
        grad_up_bias = lax.dynamic_slice(
            sums[UP_BIAS : UP_BIAS + hidden // width].reshape(-1), (me * (hidden // devices),), (hidden // devices,)
        )
    return (
        first_output,
        second_output,
        input_grad,
        grad_taps,
        vector(CONV_BIAS),
        vector(GAIN),
        vector(SHIFT),
        grad_up,
        grad_up_bias,
        grad_down,
        vector(DOWN_BIAS),
        vector(SCALE),
    )


def solution(mesh):
    wide, narrow = mesh.devices.shape
    grid = Mesh(mesh.devices.reshape(wide, narrow // 2, 2), AXES)
    chips = wide * narrow // 2
    rows = P(AXES)
    columns = P(None, AXES)

    def run(*args):
        return on_device(chips, *args)

    return jax.shard_map(
        run,
        mesh=grid,
        in_specs=(rows, rows, rows, rows, columns, rows, rows, rows, rows, rows, rows, rows, rows),
        out_specs=(rows, rows, rows, columns, rows, rows, rows, rows, rows, rows, rows, rows),
        check_vma=False,
    )
```

time: 775 us -> 174 us (0.22); the launches traced: 765 us -> 174 us
  waiting for transfers between devices: 253 us -> 16.1 us
  matrix products: 206 us -> 0 us
  other arithmetic: 158 us -> 4.54 us
  blocking collectives: 120 us -> 0 us
  Pallas kernels: 0 us -> 115 us
  starting transfers between devices: 0.2 us -> 29.4 us
  between operations: 14.8 us -> 0.86 us
    reduce_scatter x2 -> x0, waiting for transfers between devices: 210 us -> none  [the longest x1 107 us: on_device(): lax.psum_scatter(up_grads[0], ('wide', 'narrow'), scatter_dimension=0, ti...]
    dot_general x8 -> x0, matrix products: 206 us -> none  [the longest x2 123 us: run_forward(): jnp.dot(normed_low, up_weight, preferred_element_type=jnp.float32)]
    pallas_call x0 -> x6, Pallas kernels: none -> 115 us  [the longest x3 109 us: kernel_call(): pl.pallas_call(body, grid=(steps,), in_specs=specs, out_specs=[spec for _...]
    reduce_sum x7 -> x0, other arithmetic: 114 us -> none  [the longest x1 50.1 us: depthwise(): result = result + kernel_taps[offset] * padded[:, offset:offset + frames]]
    unnamed x2 -> x0, blocking collectives: 79.4 us -> none
    unnamed x6 -> x0, waiting for transfers between devices: 43 us -> none
    all_gather x1 -> x0, blocking collectives: 40.7 us -> none  [on_device(): lax.all_gather(conv_weight, ('wide', 'narrow'), axis=1, tiled=True)]
    convert_element_type x9 -> x0, other arithmetic: 29.9 us -> none  [the longest x1 23.1 us: on_device(): grad_inputs.astype(jnp.bfloat16)]
  transfers between devices with their start and end apart: 5 -> 19, of which waited for: 3 -> 7; matrix products, arithmetic and copies ran while one was open for 31% -> 2% of each run, Pallas kernels for 0% -> 40%
where the time goes in v1:
time: 174 us
  Pallas kernels  115 us (66%)
  starting transfers between devices  29.4 us (17%)
  waiting for transfers between devices  16.1 us (9%)
  local copies, waits for them, and re-layouts  7.55 us (4%)
  other arithmetic  4.54 us (3%)
    pallas_call x3, Pallas kernels, kernel_call(): pl.pallas_call(body, grid=(steps,), in_specs=specs, out_specs=[spec for _...  109 us
    ppermute x17, waiting for transfers between devices, flipped(): return lax.ppermute(a, AXES, [(i, i ^ bits) for i in range(devices)])  16.1 us
    ppermute x17, starting transfers between devices, flipped(): return lax.ppermute(a, AXES, [(i, i ^ bits) for i in range(devices)])  15.9 us
    all_to_all x1, starting transfers between devices, on_device(): lax.all_to_all(gdown.reshape(devices, hidden // devices, width), AXES, 0,...  6.79 us
    all_to_all x1, starting transfers between devices, on_device(): gup_parts = lax.all_to_all(gup_pair, CHIPS, 0, 0, tiled=True)  6.68 us
    unnamed x38, local copies, waits for them, and re-layouts  3.67 us
  transfers between devices with their start and end apart: 19, of which 7 were waited for; matrix products, arithmetic and copies ran while one was open for 2% of the time, Pallas kernels for 40%

profile of v1, /device:TPU:0, one launch (start us, length us, event | category | flops | bytes accessed | tf_op | source)
XLA Modules:
  0.0 173.8 jit_solution(18119364520395142900)
XLA Ops:
  0.7 1.7 own_block.1
  2.4 4.0 %collective-permute-start = (bf16[112,512]{1,0:T(8,128)(2,1)}, bf16[112,512]{1,0:T(8,128)(2,1)S(1)}, u32[]{:S(2)}, u32[]{:S(2)}) collective-permute-start(bf16[112,512]{1,0:T(8,128)(2,1)} %own_block.1), channel_id=1, source_target_pairs={{0,16},{1,17},{2,18},{3,19},{4,20},{5,21},{6,22},{7,23},{8,24},{9,... | collective-permute-start | bytes 344072 | tf_op jit(solution)/shard_map/ppermute | solution.py:371
  6.4 5.8 %collective-permute-done = bf16[112,512]{1,0:T(8,128)(2,1)S(1)} collective-permute-done((bf16[112,512]{1,0:T(8,128)(2,1)}, bf16[112,512]{1,0:T(8,128)(2,1)S(1)}, u32[]{:S(2)}, u32[]{:S(2)}) %collective-permute-start) | collective-permute-done | bytes 114720 | tf_op jit(solution)/shard_map/ppermute | solution.py:371
  13.1 1.6 collective-permute-start.2
  14.8 1.5 collective-permute-start.3
  17.1 2.9 %collective-permute-done.2.refs_2_ = bf16[2,112,512]{2,1,0:T(8,128)(2,1)S(1)} collective-permute-done((bf16[2,112,512]{2,1,0:T(8,128)(2,1)S(1)}, bf16[2,112,512]{2,1,0:T(8,128)(2,1)S(1)}, u32[]{:S(2)}, u32[]{:S(2)}) %collective-permute-start.2) | collective-permute-done | bytes 229408 | tf_op jit(solution)/shard_map/ppermute | solution.py:371
  20.0 1.3 collective-permute-start.4
  21.3 1.8 %collective-permute-start.5 = (bf16[2,112,512]{2,1,0:T(8,128)(2,1)S(1)}, bf16[2,112,512]{2,1,0:T(8,128)(2,1)S(1)}, u32[]{:S(2)}, u32[]{:S(2)}) collective-permute-start(bf16[2,112,512]{2,1,0:T(8,128)(2,1)S(1)} %collective-permute-done.3.refs_3_), channel_id=1, source_target_pairs={{0,8},{1,9},{2,10},{3,11},{4,12},{5,13},{6,14},{7,15},{8,0},{9,1},... | collective-permute-start | bytes 688136 | tf_op jit(solution)/shard_map/ppermute | solution.py:371
  23.1 1.5 collective-permute-start.6
  26.0 2.2 %collective-permute-start.7 = (bf16[2,112,512]{2,1,0:T(8,128)(2,1)S(1)}, bf16[2,112,512]{2,1,0:T(8,128)(2,1)S(1)}, u32[]{:S(2)}, u32[]{:S(2)}) collective-permute-start(bf16[2,112,512]{2,1,0:T(8,128)(2,1)S(1)} %collective-permute-done.4.refs_4_), channel_id=1, source_target_pairs={{0,8},{1,9},{2,10},{3,11},{4,12},{5,13},{6,14},{7,15},{8,0},{9,1},... | collective-permute-start | bytes 688136 | tf_op jit(solution)/shard_map/ppermute | solution.py:371
  28.3 1.0 collective-permute-done.6.refs_6_
  29.8 2.9 %collective-permute-done.7.refs_7_ = bf16[2,112,512]{2,1,0:T(8,128)(2,1)S(1)} collective-permute-done((bf16[2,112,512]{2,1,0:T(8,128)(2,1)S(1)}, bf16[2,112,512]{2,1,0:T(8,128)(2,1)S(1)}, u32[]{:S(2)}, u32[]{:S(2)}) %collective-permute-start.7) | collective-permute-done | bytes 229408 | tf_op jit(solution)/shard_map/ppermute | solution.py:371
  32.7 1.2 broadcast_xor_fusion.owner_ref
  35.6 39.1 %second_forward.1 = (bf16[16,256,512]{2,1,0:T(8,128)(2,1)}, bf16[4096,512]{1,0:T(8,128)(2,1)}, bf16[4096,1536]{1,0:T(8,128)(2,1)}, f32[4096,128]{1,0:T(8,128)}, ...) custom-call(s32[16]{0:T(128)} %len_ref.5, ...), custom_call_target="tpu_custom_call" | custom-call | flops 19327352832 | bytes 39944384 | tf_op jit(solution)/shard_map/second_forward/pallas_call | solution.py:312
  74.6 6.8 %all-to-all-start = ((bf16[32,48,512]{2,1,0:T(8,128)(2,1)}), bf16[32,48,512]{2,1,0:T(8,128)(2,1)S(1)}, u32[]{:S(2)}, u32[]{:S(2)}) async-start(bf16[32,48,512]{2,1,0:T(8,128)(2,1)} %bitcast.21), calls=%async_computation | async-start | bytes 3145728 | tf_op jit(solution)/shard_map/all_to_all | solution.py:493
  81.4 46.3 %second_backward.1 = (bf16[16,256,512]{2,1,0:T(8,128)(2,1)}, bf16[16,208,128]{2,1,0:T(8,128)(2,1)}, bf16[16,208,128]{2,1,0:T(8,128)(2,1)}) custom-call(s32[16]{0:T(128)} %len_ref.5, s32[1]{0:T(128)} %bitcast.9.core_ref, bf16[16,256,512]{2,1,0:T(8,128)(2,1)} %cot_ref.3, bf16[16,256,512]{2,1,0:T(8,128)(2,1)} %x_ref.4, ...), custom_call_target="tpu_custom_call" | custom-call | flops 19327352832 | bytes 37929028 | tf_op jit(solution)/shard_map/second_backward/pallas_call | solution.py:312
  127.8 2.4 %broadcast_select_fusion = (bf16[16,208,128]{2,1,0:T(8,128)(2,1)S(1)}, bf16[16,208,128]{2,1,0:T(8,128)(2,1)}) fusion(bf16[16,208,128]{2,1,0:T(8,128)(2,1)} %get-tuple-element.38, bf16[16,208,128]{2,1,0:T(8,128)(2,1)} %get-tuple-element.37, pred[]{:T(512)S(6)} %eq.4), kind=kLoop, calls=%fused_computation | loop fusion | flops 851968 | bytes 3407873 | tf_op jit(solution)/shard_map/jit(_where)/select_n | solution.py:530
  130.3 2.3 %collective-permute-done.16.got_ref = bf16[16,208,128]{2,1,0:T(8,128)(2,1)S(1)} collective-permute-done((bf16[16,208,128]{2,1,0:T(8,128)(2,1)S(1)}, bf16[16,208,128]{2,1,0:T(8,128)(2,1)S(1)}, u32[]{:S(2)}, u32[]{:S(2)}) %collective-permute-start.16) | collective-permute-done | bytes 852000 | tf_op jit(solution)/shard_map/ppermute | solution.py:371
  134.0 2.2 %add_pair.1._ = bf16[16,208,128]{2,1,0:T(8,128)(2,1)} custom-call(bf16[16,208,128]{2,1,0:T(8,128)(2,1)} %get-tuple-element.45.keep_ref, bf16[16,208,128]{2,1,0:T(8,128)(2,1)} %copy-done.2, bf16[32,48,512]{2,1,0:T(8,128)(2,1)} %copy-done), custom_call_target="tpu_custom_call" | custom-call | tf_op jit(solution)/shard_map/add_pair/pallas_call | solution.py:419
  136.2 6.7 %all-to-all-start.1 = ((bf16[16,208,128]{2,1,0:T(8,128)(2,1)}), bf16[16,208,128]{2,1,0:T(8,128)(2,1)S(1)}, u32[]{:S(2)}, u32[]{:S(2)}) async-start(bf16[16,208,128]{2,1,0:T(8,128)(2,1)} %add_pair.1._), calls=%async_computation.1 | async-start | bytes 1703936 | tf_op jit(solution)/shard_map/all_to_all | solution.py:532
  142.9 23.4 %first_forward.1 = bf16[16,256,512]{2,1,0:T(8,128)(2,1)} custom-call(s32[16]{0:T(128)} %len_ref.5, bf16[16,256,512]{2,1,0:T(8,128)(2,1)} %x_ref.5, bf16[512,1536]{1,0:T(8,128)(2,1)} %get-tuple-element.28.up_ref, bf16[1536,512]{1,0:T(8,128)(2,1)} %get-tuple-element.29.down_ref, f32[16,512]{1,0:T(8,128)} %get-tuple-element.30.small_ref, ...), custom_call_target="tpu_custom_call" | custom-call | flops 12884901888 | bytes 12468288 | tf_op jit(solution)/shard_map/first_forward/pallas_call | solution.py:312
  167.3 2.6 %finish.1 = (f32[48,512]{1,0:T(8,128)}, f32[16,1536]{1,0:T(8,128)}, f32[16,128]{1,0:T(8,128)}) custom-call(bf16[32,48,512]{2,1,0:T(8,128)(2,1)} %copy-done, bf16[16,208,128]{2,1,0:T(8,128)(2,1)} %copy-done.1, f32[16,512]{1,0:T(8,128)} %get-tuple-element.30.small_ref), custom_call_target="tpu_custom_call" | custom-call | tf_op jit(solution)/shard_map/finish/pallas_call | solution.py:553
  169.9 1.3 slice.21
  171.2 1.4 slice_bitcast_fusion
  (65 shorter events, 9.0 us)
Async XLA Ops:
  2.4 9.8 %collective-permute-start = (bf16[112,512]{1,0:T(8,128)(2,1)}, bf16[112,512]{1,0:T(8,128)(2,1)S(1)}, u32[]{:S(2)}, u32[]{:S(2)}) collective-permute-start(bf16[112,512]{1,0:T(8,128)(2,1)} %own_block.1), channel_id=1, source_target_pairs={{0,16},{1,17},{2,18},{3,19},{4,20},{5,21},{6,22},{7,23},{8,24},{9,... | collective-permute-start | bytes 344072 | tf_op jit(solution)/shard_map/ppermute | solution.py:371
  13.1 21.1 %copy-start.3 = (bf16[2,112,512]{2,1,0:T(8,128)(2,1)}, bf16[2,112,512]{2,1,0:T(8,128)(2,1)S(1)}, u32[]{:S(2)}) copy-start(bf16[2,112,512]{2,1,0:T(8,128)(2,1)S(1)} %pad_maximum_fusion.refs_0_) | copy-start | bytes 688132
  13.1 6.9 %collective-permute-start.2 = (bf16[2,112,512]{2,1,0:T(8,128)(2,1)S(1)}, bf16[2,112,512]{2,1,0:T(8,128)(2,1)S(1)}, u32[]{:S(2)}, u32[]{:S(2)}) collective-permute-start(bf16[2,112,512]{2,1,0:T(8,128)(2,1)S(1)} %pad_maximum_fusion.refs_0_), channel_id=1, source_target_pairs={{0,4},{1,5},{2,6},{3,7},{4,0},{5,1},{6,2},{7,3},{8,12},{9,13},{10,... | collective-permute-start | bytes 688136 | tf_op jit(solution)/shard_map/ppermute | solution.py:371
  14.8 6.5 %collective-permute-start.3 = (bf16[2,112,512]{2,1,0:T(8,128)(2,1)S(1)}, bf16[2,112,512]{2,1,0:T(8,128)(2,1)S(1)}, u32[]{:S(2)}, u32[]{:S(2)}) collective-permute-start(bf16[2,112,512]{2,1,0:T(8,128)(2,1)S(1)} %pad_maximum_fusion.refs_0_), channel_id=1, source_target_pairs={{0,2},{1,3},{2,0},{3,1},{4,6},{5,7},{6,4},{7,5},{8,10},{9,11},{10,... | collective-permute-start | bytes 688136 | tf_op jit(solution)/shard_map/ppermute | solution.py:371
  16.3 6.8 %collective-permute-start.1 = (bf16[2,112,512]{2,1,0:T(8,128)(2,1)S(1)}, bf16[2,112,512]{2,1,0:T(8,128)(2,1)S(1)}, u32[]{:S(2)}, u32[]{:S(2)}) collective-permute-start(bf16[2,112,512]{2,1,0:T(8,128)(2,1)S(1)} %pad_maximum_fusion.refs_0_), channel_id=1, source_target_pairs={{0,8},{1,9},{2,10},{3,11},{4,12},{5,13},{6,14},{7,15},{8,0},{9,1},... | collective-permute-start | bytes 688136 | tf_op jit(solution)/shard_map/ppermute | solution.py:371
  17.0 7.5 %collective-permute-start.8 = (bf16[2,112,512]{2,1,0:T(8,128)(2,1)S(1)}, bf16[2,112,512]{2,1,0:T(8,128)(2,1)S(1)}, u32[]{:S(2)}, u32[]{:S(2)}) collective-permute-start(bf16[2,112,512]{2,1,0:T(8,128)(2,1)S(1)} %pad_maximum_fusion.refs_0_), channel_id=1, source_target_pairs={{0,1},{1,0},{2,3},{3,2},{4,5},{5,4},{6,7},{7,6},{8,9},{9,8},{10,11... | collective-permute-start | bytes 688136 | tf_op jit(solution)/shard_map/ppermute | solution.py:371
  20.0 14.2 %copy-start.4 = (bf16[2,112,512]{2,1,0:T(8,128)(2,1)}, bf16[2,112,512]{2,1,0:T(8,128)(2,1)S(1)}, u32[]{:S(2)}) copy-start(bf16[2,112,512]{2,1,0:T(8,128)(2,1)S(1)} %collective-permute-done.2.refs_2_) | copy-start | bytes 688132
  20.0 6.0 %collective-permute-start.4 = (bf16[2,112,512]{2,1,0:T(8,128)(2,1)S(1)}, bf16[2,112,512]{2,1,0:T(8,128)(2,1)S(1)}, u32[]{:S(2)}, u32[]{:S(2)}) collective-permute-start(bf16[2,112,512]{2,1,0:T(8,128)(2,1)S(1)} %collective-permute-done.2.refs_2_), channel_id=1, source_target_pairs={{0,2},{1,3},{2,0},{3,1},{4,6},{5,7},{6,4},{7,5},{8,10},{9,11},{10,... | collective-permute-start | bytes 688136 | tf_op jit(solution)/shard_map/ppermute | solution.py:371
  21.3 12.9 %copy-start.5 = (bf16[2,112,512]{2,1,0:T(8,128)(2,1)}, bf16[2,112,512]{2,1,0:T(8,128)(2,1)S(1)}, u32[]{:S(2)}) copy-start(bf16[2,112,512]{2,1,0:T(8,128)(2,1)S(1)} %collective-permute-done.3.refs_3_) | copy-start | bytes 688132
  21.3 7.0 %collective-permute-start.5 = (bf16[2,112,512]{2,1,0:T(8,128)(2,1)S(1)}, bf16[2,112,512]{2,1,0:T(8,128)(2,1)S(1)}, u32[]{:S(2)}, u32[]{:S(2)}) collective-permute-start(bf16[2,112,512]{2,1,0:T(8,128)(2,1)S(1)} %collective-permute-done.3.refs_3_), channel_id=1, source_target_pairs={{0,8},{1,9},{2,10},{3,11},{4,12},{5,13},{6,14},{7,15},{8,0},{9,1},... | collective-permute-start | bytes 688136 | tf_op jit(solution)/shard_map/ppermute | solution.py:371
  23.1 11.1 %copy-start.6 = (bf16[2,112,512]{2,1,0:T(8,128)(2,1)}, bf16[2,112,512]{2,1,0:T(8,128)(2,1)S(1)}, u32[]{:S(2)}) copy-start(bf16[2,112,512]{2,1,0:T(8,128)(2,1)S(1)} %collective-permute-done.1.refs_1_) | copy-start | bytes 688132
  23.1 6.1 %collective-permute-start.6 = (bf16[2,112,512]{2,1,0:T(8,128)(2,1)S(1)}, bf16[2,112,512]{2,1,0:T(8,128)(2,1)S(1)}, u32[]{:S(2)}, u32[]{:S(2)}) collective-permute-start(bf16[2,112,512]{2,1,0:T(8,128)(2,1)S(1)} %collective-permute-done.1.refs_1_), channel_id=1, source_target_pairs={{0,4},{1,5},{2,6},{3,7},{4,0},{5,1},{6,2},{7,3},{8,12},{9,13},{10,... | collective-permute-start | bytes 688136 | tf_op jit(solution)/shard_map/ppermute | solution.py:371
  24.6 4.6 %collective-permute-start.10 = (bf16[2,112,512]{2,1,0:T(8,128)(2,1)S(1)}, bf16[2,112,512]{2,1,0:T(8,128)(2,1)S(1)}, u32[]{:S(2)}, u32[]{:S(2)}) collective-permute-start(bf16[2,112,512]{2,1,0:T(8,128)(2,1)S(1)} %collective-permute-done.2.refs_2_), channel_id=1, source_target_pairs={{0,1},{1,0},{2,3},{3,2},{4,5},{5,4},{6,7},{7,6},{8,9},{9,8},{10,11... | collective-permute-start | bytes 688136 | tf_op jit(solution)/shard_map/ppermute | solution.py:371
  24.6 9.6 %copy-start.7 = (bf16[2,112,512]{2,1,0:T(8,128)(2,1)}, bf16[2,112,512]{2,1,0:T(8,128)(2,1)S(1)}, u32[]{:S(2)}) copy-start(bf16[2,112,512]{2,1,0:T(8,128)(2,1)S(1)} %collective-permute-done.8.refs_8_) | copy-start | bytes 688132
  24.6 5.1 %collective-permute-start.11 = (bf16[2,112,512]{2,1,0:T(8,128)(2,1)S(1)}, bf16[2,112,512]{2,1,0:T(8,128)(2,1)S(1)}, u32[]{:S(2)}, u32[]{:S(2)}) collective-permute-start(bf16[2,112,512]{2,1,0:T(8,128)(2,1)S(1)} %collective-permute-done.3.refs_3_), channel_id=1, source_target_pairs={{0,1},{1,0},{2,3},{3,2},{4,5},{5,4},{6,7},{7,6},{8,9},{9,8},{10,11... | collective-permute-start | bytes 688136 | tf_op jit(solution)/shard_map/ppermute | solution.py:371
  26.0 6.7 %collective-permute-start.7 = (bf16[2,112,512]{2,1,0:T(8,128)(2,1)S(1)}, bf16[2,112,512]{2,1,0:T(8,128)(2,1)S(1)}, u32[]{:S(2)}, u32[]{:S(2)}) collective-permute-start(bf16[2,112,512]{2,1,0:T(8,128)(2,1)S(1)} %collective-permute-done.4.refs_4_), channel_id=1, source_target_pairs={{0,8},{1,9},{2,10},{3,11},{4,12},{5,13},{6,14},{7,15},{8,0},{9,1},... | collective-permute-start | bytes 688136 | tf_op jit(solution)/shard_map/ppermute | solution.py:371
  28.3 5.7 %collective-permute-start.9 = (bf16[2,112,512]{2,1,0:T(8,128)(2,1)S(1)}, bf16[2,112,512]{2,1,0:T(8,128)(2,1)S(1)}, u32[]{:S(2)}, u32[]{:S(2)}) collective-permute-start(bf16[2,112,512]{2,1,0:T(8,128)(2,1)S(1)} %collective-permute-done.1.refs_1_), channel_id=1, source_target_pairs={{0,1},{1,0},{2,3},{3,2},{4,5},{5,4},{6,7},{7,6},{8,9},{9,8},{10,11... | collective-permute-start | bytes 688136 | tf_op jit(solution)/shard_map/ppermute | solution.py:371
  29.2 4.7 %collective-permute-start.12 = (bf16[2,112,512]{2,1,0:T(8,128)(2,1)S(1)}, bf16[2,112,512]{2,1,0:T(8,128)(2,1)S(1)}, u32[]{:S(2)}, u32[]{:S(2)}) collective-permute-start(bf16[2,112,512]{2,1,0:T(8,128)(2,1)S(1)} %collective-permute-done.4.refs_4_), channel_id=1, source_target_pairs={{0,1},{1,0},{2,3},{3,2},{4,5},{5,4},{6,7},{7,6},{8,9},{9,8},{10,11... | collective-permute-start | bytes 688136 | tf_op jit(solution)/shard_map/ppermute | solution.py:371
  29.2 4.7 %collective-permute-start.13 = (bf16[2,112,512]{2,1,0:T(8,128)(2,1)S(1)}, bf16[2,112,512]{2,1,0:T(8,128)(2,1)S(1)}, u32[]{:S(2)}, u32[]{:S(2)}) collective-permute-start(bf16[2,112,512]{2,1,0:T(8,128)(2,1)S(1)} %collective-permute-done.5.refs_5_), channel_id=1, source_target_pairs={{0,1},{1,0},{2,3},{3,2},{4,5},{5,4},{6,7},{7,6},{8,9},{9,8},{10,11... | collective-permute-start | bytes 688136 | tf_op jit(solution)/shard_map/ppermute | solution.py:371
  29.7 4.2 %collective-permute-start.14 = (bf16[2,112,512]{2,1,0:T(8,128)(2,1)S(1)}, bf16[2,112,512]{2,1,0:T(8,128)(2,1)S(1)}, u32[]{:S(2)}, u32[]{:S(2)}) collective-permute-start(bf16[2,112,512]{2,1,0:T(8,128)(2,1)S(1)} %collective-permute-done.6.refs_6_), channel_id=1, source_target_pairs={{0,1},{1,0},{2,3},{3,2},{4,5},{5,4},{6,7},{7,6},{8,9},{9,8},{10,11... | collective-permute-start | bytes 688136 | tf_op jit(solution)/shard_map/ppermute | solution.py:371
  32.7 1.5 collective-permute-start.15
  74.6 57.9 %all-to-all-start = ((bf16[32,48,512]{2,1,0:T(8,128)(2,1)}), bf16[32,48,512]{2,1,0:T(8,128)(2,1)S(1)}, u32[]{:S(2)}, u32[]{:S(2)}) async-start(bf16[32,48,512]{2,1,0:T(8,128)(2,1)} %bitcast.21), calls=%async_computation | async-start | bytes 3145728 | tf_op jit(solution)/shard_map/all_to_all | solution.py:493
  130.2 2.4 %collective-permute-start.16 = (bf16[16,208,128]{2,1,0:T(8,128)(2,1)S(1)}, bf16[16,208,128]{2,1,0:T(8,128)(2,1)S(1)}, u32[]{:S(2)}, u32[]{:S(2)}) collective-permute-start(bf16[16,208,128]{2,1,0:T(8,128)(2,1)S(1)} %get-tuple-element.44), channel_id=1, source_target_pairs={{0,1},{1,0},{2,3},{3,2},{4,5},{5,4},{6,7},{7,6},{8,9},{9,8},{10,11... | collective-permute-start | bytes 2555912 | tf_op jit(solution)/shard_map/ppermute | solution.py:371
  136.2 30.1 %all-to-all-start.1 = ((bf16[16,208,128]{2,1,0:T(8,128)(2,1)}), bf16[16,208,128]{2,1,0:T(8,128)(2,1)S(1)}, u32[]{:S(2)}, u32[]{:S(2)}) async-start(bf16[16,208,128]{2,1,0:T(8,128)(2,1)} %add_pair.1._), calls=%async_computation.1 | async-start | bytes 1703936 | tf_op jit(solution)/shard_map/all_to_all | solution.py:532
  (14 other events, 37.5 us)

commit v2 on v1

--- a/solution.py
+++ b/solution.py
@@ -16,6 +16,7 @@
 LANES = 128
 HALO = 8
 TAIL = 32
+CHUNK = 16
 SMALL = 16
 VMEM = 60 * 2**20
 BLOCK = 4
@@ -75,6 +76,27 @@
     return (centred * rstd).astype(bf16), rstd
 
 
+def conv_norm_into(pad_ref, m, small_ref, frames, xhat_ref, rstd_ref):
+    width = xhat_ref.shape[1]
+    for r in range(0, frames, CHUNK):
+        parts = []
+        for c in range(width // LANES):
+            cs = slice(c * LANES, (c + 1) * LANES)
+            acc = small_ref[CONV_BIAS : CONV_BIAS + 1, cs]
+            for k in range(TAPS):
+                start = HALO + k - TAPS // 2 + r
+                acc = acc + small_ref[k : k + 1, cs] * pad_ref[m, c, start : start + CHUNK]
+            parts.append(acc)
+        mean = jnp.sum(sum(parts[1:], parts[0]), axis=-1, keepdims=True) / width
+        parts = [p - mean for p in parts]
+        square = sum((p * p for p in parts[1:]), parts[0] * parts[0])
+        rstd = lax.rsqrt(jnp.sum(square, axis=-1, keepdims=True) / width + 1e-06)
+        rows = slice(m * frames + r, m * frames + r + CHUNK)
+        rstd_ref[rows] = jnp.broadcast_to(rstd, (CHUNK, LANES))
+        for c, p in enumerate(parts):
+            xhat_ref[rows, c * LANES : (c + 1) * LANES] = (p * rstd).astype(bf16)
+
+
 def store_output(out_ref, m, length, x_ref, branch):
     frames = x_ref.shape[1]
     body = frames - TAIL
@@ -94,17 +116,17 @@
 
 
 def second_forward(
-    len_ref, owner_ref, x_ref, cot_ref, *refs
+    owners, len_ref, me_ref, x_ref, next_ref, cot_ref, *refs
 ):
-    count = len(refs) - 15
+    count = len(refs) - 17
     block_refs = [ref.at[j] for ref in refs[:count] for j in range(ref.shape[0])]
-    second_forward_body(len_ref, owner_ref, x_ref, cot_ref, block_refs, *refs[count:])
+    second_forward_body(owners, len_ref, me_ref, x_ref, next_ref, cot_ref, block_refs, *refs[count:])
 
 
 def second_forward_body(
-    len_ref, owner_ref, x_ref, cot_ref, block_refs,
+    owners, len_ref, me_ref, x_ref, next_ref, cot_ref, block_refs,
     out_ref, xhat_ref, slope_ref, rstd_ref, up_ref, down_ref, small_ref, bias_ref, gdown_ref, rows_ref,
-    pad_ref, act_ref, mcot_ref, acc_ref, csum_ref,
+    pad_ref, act_ref, mcot_ref, acc_ref, csum_ref, xnext_ref, rnext_ref,
 ):
     step = pl.program_id(0)
     clips, frames, width = x_ref.shape
@@ -122,34 +144,34 @@
         small_ref[...] = small
         scale = small[SCALE : SCALE + 1] * ROOT
         for j, ref in enumerate(block_refs):
-            owner = owner_ref[j]
+            owner = me_ref[0] ^ owners[j]
             at = pl.multiple_of(owner * up_rows, up_rows)
             for p in range(parts):
                 up_ref[pl.ds(at, up_rows), p * width : (p + 1) * width] = ref[p * up_rows : (p + 1) * up_rows]
             at = pl.multiple_of(owner * down_rows, down_rows)
             down_ref[pl.ds(at, down_rows)] = (ref[down_rows : 2 * down_rows].astype(f32) * scale).astype(bf16)
-        ratio = small[SHIFT : SHIFT + 1] / small[GAIN : GAIN + 1]
-        shift = dot(
-            jnp.broadcast_to(ratio, (8, width)), up_ref[...].astype(f32), precision=lax.Precision.HIGHEST
-        )
+        columns = small.T
+        ratio = columns[:, SHIFT : SHIFT + 1] / columns[:, GAIN : GAIN + 1]
+        shift = jnp.sum((up_ref[...].astype(f32) * ratio).reshape(-1, 8, hidden), axis=0)
+        shift = jnp.broadcast_to(jnp.sum(shift, axis=0, keepdims=True), (8, hidden))
         for p in range(parts):
             cs = slice(p * width, (p + 1) * width)
             bias_ref[:, cs] = shift[:, cs] + small[UP_BIAS + p : UP_BIAS + p + 1] * ROOT
         acc_ref[...] = jnp.zeros_like(acc_ref)
         csum_ref[...] = jnp.zeros_like(csum_ref)
+        for m in range(clips):
+            fill_padded(x_ref, m, len_ref[m], pad_ref)
+            conv_norm_into(pad_ref, m, small_ref, frames, xnext_ref, rnext_ref)
 
     lengths = [len_ref[step * clips + m] for m in range(clips)]
-    for m in range(clips):
-        fill_padded(x_ref, m, lengths[m], pad_ref)
-        xhat, rstd = conv_norm(pad_ref, m, small_ref, frames)
-        xhat_ref[m * frames : (m + 1) * frames] = xhat
-        rstd_ref[m * frames : (m + 1) * frames] = jnp.broadcast_to(rstd, (frames, LANES))
+    xhat_ref[...] = xnext_ref[...]
+    rstd_ref[...] = rnext_ref[...]
+    for m in range(clips):
         store_masked(mcot_ref, m, lengths[m], cot_ref)
 
-    xhat = xhat_ref[...]
     for p in range(parts):
         cs = slice(p * width, (p + 1) * width)
-        u = dot(xhat, up_ref[:, cs]) + bias_ref[0:1, cs]
+        u = dot(xhat_ref[...], up_ref[:, cs]) + bias_ref[0:1, cs]
         s = 1.0 + lax.erf(u)
         act_ref[:, cs] = (u * s).astype(bf16)
         bell = jnp.exp2(u * u * (-math.log2(math.e)))
@@ -160,13 +182,16 @@
     for m in range(clips):
         store_output(out_ref, m, lengths[m], x_ref, branch[m * frames : (m + 1) * frames])
 
-    mcot = mcot_ref[...]
-    acc_ref[...] += dot(act_ref[...], mcot, 0, 0)
-    csum_ref[...] += jnp.sum(mcot.astype(f32).reshape(-1, 8, width), axis=0)
+    acc_ref[...] += dot(mcot_ref[...], act_ref[...], 0, 0)
+    csum_ref[...] += jnp.sum(mcot_ref[...].astype(f32).reshape(-1, 8, width), axis=0)
+    later = jnp.minimum(step + 1, pl.num_programs(0) - 1) * clips
+    for m in range(clips):
+        fill_padded(next_ref, m, len_ref[later + m], pad_ref)
+        conv_norm_into(pad_ref, m, small_ref, frames, xnext_ref, rnext_ref)
 
     @pl.when(step == pl.num_programs(0) - 1)
     def _():
-        total = acc_ref[...]
+        total = acc_ref[...].T
         gdown_ref[...] = total.astype(bf16)
         scale = small_ref[SCALE : SCALE + 1]
         csum = jnp.sum(csum_ref[...], axis=0, keepdims=True)
@@ -196,60 +221,65 @@
     lengths = [len_ref[step * clips + m] for m in range(clips)]
     for m in range(clips):
         store_masked(mcot_ref, m, lengths[m], cot_ref)
-    mcot = mcot_ref[...]
-    for p in range(parts):
-        cs = slice(p * width, (p + 1) * width)
-        ga = dot(mcot, down_ref[cs, :], 1, 1)
-        gh = ga * slope_ref[:, cs].astype(f32)
-        hsum_ref[:, cs] += jnp.sum(gh.reshape(-1, 8, width), axis=0)
-        gh_ref[:, cs] = gh.astype(bf16)
-    acc_ref[...] += dot(xhat_ref[...], gh_ref[...], 0, 0)
-    g = dot(gh_ref[...], up_ref[...], 1, 1)
     for m in range(clips):
         rows = slice(m * frames, (m + 1) * frames)
-        gm = g[rows]
+        for p in range(parts):
+            cs = slice(p * width, (p + 1) * width)
+            ga = dot(mcot_ref[rows], down_ref[cs, :], 1, 1)
+            gh = ga * slope_ref[rows, cs].astype(f32)
+            hsum_ref[:, cs] += jnp.sum(gh.reshape(-1, 8, width), axis=0)
+            gh_ref[rows, cs] = gh.astype(bf16)
+    for m in range(clips):
+        rows = slice(m * frames, (m + 1) * frames)
+        g = dot(gh_ref[rows], up_ref[...], 1, 1)
         xhat = xhat_ref[rows].astype(f32)
-        mean = jnp.mean(gm, axis=-1, keepdims=True)
-        proj = jnp.mean(gm * xhat, axis=-1, keepdims=True)
+        mean = jnp.mean(g, axis=-1, keepdims=True)
+        proj = jnp.mean(g * xhat, axis=-1, keepdims=True)
         rstd = rstd_ref[rows]
         for c in range(width // LANES):
             cs = slice(c * LANES, (c + 1) * LANES)
-            gc = (gm[:, cs] - mean - xhat[:, cs] * proj) * rstd
+            gc = (g[:, cs] - mean - xhat[:, cs] * proj) * rstd
             pad_ref[m, c, HALO : HALO + frames] = gc
             tsum_ref[TAPS, :, cs] += jnp.sum(gc.reshape(-1, 8, LANES), axis=0)
-    body = frames - TAIL
+    acc_ref[...] += dot(xhat_ref[...], gh_ref[...], 0, 0)
     for m in range(clips):
         keep = tail_mask(frames, lengths[m], LANES)
         for c in range(width // LANES):
             cs = slice(c * LANES, (c + 1) * LANES)
-            x = x_ref[m, :, cs].astype(f32)
-            x = jnp.concatenate([x[:body], jnp.where(keep, x[body:], 0.0)], axis=0)
-            total = cot_ref[m, :, cs].astype(f32)
+            sums = [jnp.zeros((8, LANES), f32)] * TAPS
+            for r in range(0, frames, TAIL):
+                x = x_ref[m, r : r + TAIL, cs].astype(f32)
+                total = cot_ref[m, r : r + TAIL, cs].astype(f32)
+                if r + TAIL == frames:
+                    x = jnp.where(keep, x, 0.0)
+                for k in range(TAPS):
+                    start = HALO + TAPS // 2 - k + r
+                    gc = pad_ref[m, c, start : start + TAIL]
+                    total = total + small_ref[k : k + 1, cs] * gc
+                    sums[k] = sums[k] + jnp.sum((gc * x).reshape(-1, 8, LANES), axis=0)
+                if r + TAIL == frames:
+                    total = jnp.where(keep, total, 0.0)
+                grad_ref[m, r : r + TAIL, cs] = total.astype(bf16)
             for k in range(TAPS):
-                start = HALO + TAPS // 2 - k
-                gc = pad_ref[m, c, start : start + frames]
-                total = total + small_ref[k : k + 1, cs] * gc
-                tsum_ref[k, :, cs] += jnp.sum((gc * x).reshape(-1, 8, LANES), axis=0)
-            grad_ref[m, :body, cs] = total[:body].astype(bf16)
-            grad_ref[m, body:, cs] = jnp.where(keep, total[body:], 0.0).astype(bf16)
+                tsum_ref[k, :, cs] += sums[k]
 
     @pl.when(step == pl.num_programs(0) - 1)
     def _():
         total = acc_ref[...]
         hsum = jnp.sum(hsum_ref[...], axis=0, keepdims=True)
         columns = small_ref[...].T
-        gain, shift = columns[:, GAIN : GAIN + 1], columns[:, SHIFT : SHIFT + 1]
-        total_up = (gain * total + shift * hsum) * ROOT
-        up = up_ref[...].astype(f32)
-        ones = jnp.ones((8, hidden), f32)
-        exact = lax.Precision.HIGHEST
+        gain, shift = columns[:, GAIN : GAIN + 1] * ROOT, columns[:, SHIFT : SHIFT + 1] * ROOT
         inverse = 1.0 / small_ref[GAIN : GAIN + 1]
         rows = [jnp.sum(tsum_ref[k], axis=0, keepdims=True) for k in range(TAPS + 1)]
-        rows.append(dot(ones, up * total, 1, 1, exact)[:1] * inverse)
-        rows.append(dot(jnp.broadcast_to(hsum, (8, hidden)), up, 1, 1, exact)[:1] * inverse)
+        up = up_ref[...].astype(f32)
+        for value in (up * total, up * hsum):
+            part = value[:, :LANES]
+            for c in range(1, hidden // LANES):
+                part = part + value[:, c * LANES : (c + 1) * LANES]
+            rows.append(jnp.sum(part.T, axis=0, keepdims=True) * inverse)
         rows.append(down_rows_ref[0:2])
         if not packed:
-            out_a_ref[...] = total_up.astype(bf16)
+            out_a_ref[...] = (gain * total + shift * hsum).astype(bf16)
             rows += [hsum[:, p * width : (p + 1) * width] * ROOT for p in range(parts)]
             rows.append(jnp.zeros((SMALL - UP_BIAS - parts, width), f32))
             out_b_ref[...] = jnp.concatenate(rows, axis=0)
@@ -260,12 +290,16 @@
         lane = lax.broadcasted_iota(jnp.int32, (SMALL, LANES), 1)
         line = lax.broadcasted_iota(jnp.int32, (SMALL, LANES), 0)
         devices = width // 16
+        even = core_ref[0] == 0
+        acc_ref[...] = gain * total + shift * hsum
+        for chip in range(devices // 2):
+            for ref, core in ((out_a_ref, core_ref[0]), (out_b_ref, 1 - core_ref[0])):
+                at = pl.multiple_of(chip * 32 + core * 16, 16)
+                for c in range(hidden // LANES):
+                    value = acc_ref[pl.ds(at, 16), c * LANES : (c + 1) * LANES]
+                    ref[chip, c * 16 : (c + 1) * 16] = value.astype(bf16)
+        pair = []
         for owner in range(devices):
-            ref = out_a_ref if owner % 2 == 0 else out_b_ref
-            for c in range(hidden // LANES):
-                ref[owner // 2, c * 16 : (c + 1) * 16] = total_up[
-                    owner * 16 : (owner + 1) * 16, c * LANES : (c + 1) * LANES
-                ].astype(bf16)
             at = owner * 16 // LANES * LANES
             mine = pltpu.roll(rows[:, at : at + LANES], (LANES - owner * 16 % LANES) % LANES, 1)
             for r in range(parts):
@@ -277,11 +311,23 @@
                 mine = jnp.where(line == UP_BIAS + r, part, mine)
             high = mine.astype(bf16).astype(f32)
             low = pltpu.roll(mine - high, LANES // 2, 1)
-            mine = jnp.where(lane < 16, high, jnp.where((lane >= LANES // 2) & (lane < LANES // 2 + 16), low, 0.0))
-            ref[owner // 2, hidden // LANES * 16 :] = mine.astype(bf16)
-
-
-def first_forward(len_ref, x_ref, up_ref, down_ref, small_ref, bias_ref, _, out_ref, pad_ref, xhat_ref, act_ref):
+            pair.append(jnp.where(lane < 16, high, jnp.where((lane >= LANES // 2) & (lane < LANES // 2 + 16), low, 0.0)))
+            if owner % 2:
+                first, second = pair[-2:]
+                out_a_ref[owner // 2, hidden // LANES * 16 :] = jnp.where(even, first, second).astype(bf16)
+                out_b_ref[owner // 2, hidden // LANES * 16 :] = jnp.where(even, second, first).astype(bf16)
+
+
+def first_forward(
+    len_ref, x_ref, up_ref, down_ref, small_ref, bias_ref, _, parts_ref, scale_ref,
+    out_ref, grad_down_ref,
+    pad_ref, xhat_ref, act_ref,
+):
+    total = jnp.zeros(parts_ref.shape[1:], f32)
+    for j in range(parts_ref.shape[0]):
+        total = total + parts_ref[j].astype(f32)
+    grad_down_ref[...] = total * (scale_ref[SCALE : SCALE + 1] * ROOT)
+
     step = pl.program_id(0)
     clips, frames, width = x_ref.shape
     parts = up_ref.shape[1] // width
@@ -291,18 +337,22 @@
         clear_halo(pad_ref, frames)
 
     lengths = [len_ref[step * clips + m] for m in range(clips)]
-    for m in range(clips):
+    down_bias = small_ref[DOWN_BIAS : DOWN_BIAS + 1] * small_ref[SCALE : SCALE + 1]
+
+    def front(m):
         fill_padded(x_ref, m, lengths[m], pad_ref)
         xhat_ref[m * frames : (m + 1) * frames] = conv_norm(pad_ref, m, small_ref, frames)[0]
-    xhat = xhat_ref[...]
-    for p in range(parts):
-        cs = slice(p * width, (p + 1) * width)
-        u = dot(xhat, up_ref[:, cs]) + bias_ref[0:1, cs]
-        act_ref[:, cs] = (u * (1.0 + lax.erf(u))).astype(bf16)
-    down_bias = small_ref[DOWN_BIAS : DOWN_BIAS + 1] * small_ref[SCALE : SCALE + 1]
-    branch = dot(act_ref[...], down_ref[...]) + down_bias
-    for m in range(clips):
-        store_output(out_ref, m, lengths[m], x_ref, branch[m * frames : (m + 1) * frames])
+
+    front(0)
+    for m in range(clips):
+        if m + 1 < clips:
+            front(m + 1)
+        rows = slice(m * frames, (m + 1) * frames)
+        for p in range(2 * parts):
+            cs = slice(p * width // 2, (p + 1) * width // 2)
+            u = dot(xhat_ref[rows], up_ref[:, cs]) + bias_ref[0:1, cs]
+            act_ref[rows, cs] = (u * (1.0 + lax.erf(u))).astype(bf16)
+        store_output(out_ref, m, lengths[m], x_ref, dot(act_ref[rows], down_ref[...]) + down_bias)
 
 
 def kernel_call(body, name, args, specs, outs, scratch, steps, flops, elements):
@@ -395,7 +445,7 @@
         for start in list(have):
             have[start ^ 1] = flipped(have[start], 1, devices)
         order = [start ^ far for start in have for far in (0, 16)]
-        return list(have.values()), me ^ jnp.array(order, jnp.int32)
+        return list(have.values()), order, me.reshape(1)
     everyone = lambda a, axis: lax.all_gather(a, AXES, axis=axis, tiled=True)
     up = (up.astype(f32) * gain.astype(f32)[:, None] * ROOT).astype(bf16)
     up, down, up_bias = everyone(up, 0), everyone(down, 0), everyone(up_bias, 0)
@@ -406,39 +456,24 @@
     up = up.reshape(count, 16, parts, width).swapaxes(1, 2).reshape(count, 16 * parts, width)
     down = down.reshape(count, 16 * parts, width)
     small = jnp.pad(small[None], ((0, count - 1), (0, 0), (0, 0)))
-    return [jnp.concatenate([up, down, small], axis=1)], jnp.arange(count, dtype=jnp.int32)
-
-
-def add_pair(keep_ref, got_ref, _, out_ref):
-    out_ref[...] = (keep_ref[...].astype(f32) + got_ref[...].astype(f32)).astype(bf16)
-
-
-def pair_sum(keep, got, after):
-    half = keep.shape[0] // 2
-    spec = pl.BlockSpec((half,) + keep.shape[1:], lambda i: (i, 0, 0))
-    return pl.pallas_call(
-        add_pair,
-        grid=(2,),
-        in_specs=[spec, spec, pl.BlockSpec(memory_space=pl.ANY)],
-        out_specs=spec,
-        out_shape=shape(keep.shape, bf16),
-        name="add_pair",
-    )(keep, got, after)
-
-
-def finish(down_ref, up_ref, small_ref, grad_down_ref, grad_up_ref, rows_ref):
-    total = jnp.zeros(down_ref.shape[1:], f32)
-    for j in range(down_ref.shape[0]):
-        total = total + down_ref[j].astype(f32)
-    grad_down_ref[...] = total * (small_ref[SCALE : SCALE + 1] * ROOT)
-    total = jnp.zeros(up_ref.shape[1:], f32)
-    for j in range(up_ref.shape[0]):
-        total = total + up_ref[j].astype(f32)
+    return [jnp.concatenate([up, down, small], axis=1)], list(range(count)), jnp.zeros((1,), jnp.int32)
+
+
+def finish(parts_ref, grad_up_ref, taps_ref, up_bias_ref, *vector_refs):
+    total = jnp.zeros(parts_ref.shape[1:], f32)
+    for j in range(parts_ref.shape[0]):
+        total = total + parts_ref[j].astype(f32)
     own, hidden = grad_up_ref.shape
     for c in range(hidden // LANES):
         grad_up_ref[:, c * LANES : (c + 1) * LANES] = total[c * own : (c + 1) * own]
-    rest = total[hidden // LANES * own :]
-    rows_ref[...] = rest + pltpu.roll(rest, LANES // 2, 1)
+    rows = total[hidden // LANES * own :]
+    rows = rows + pltpu.roll(rows, LANES // 2, 1)
+    taps_ref[...] = rows[:TAPS, :own]
+    up_bias_ref[...] = jnp.concatenate(
+        [rows[UP_BIAS + p : UP_BIAS + p + 1, :own] for p in range(up_bias_ref.shape[1] // own)], axis=1
+    )
+    for ref, r in zip(vector_refs, (CONV_BIAS, GAIN, SHIFT, DOWN_BIAS, SCALE)):
+        ref[...] = rows[r : r + 1, :own]
 
 
 def on_device(chips, first_input, second_input, cotangent, lengths, *weights):
@@ -451,23 +486,28 @@
     core = lax.axis_index("core").astype(jnp.int32)
     matmul = 2 * tokens * width * hidden
 
-    blocks, owners = gather_weights(weights, chips * 2)
+    blocks, owners, base = gather_weights(weights, chips * 2)
 
     clip_spec = pl.BlockSpec((block, frames, width), lambda i: (i, 0, 0))
-    row_spec = lambda n: pl.BlockSpec((rows, n), lambda i: (i, 0))
+    half = math.gcd(clips, BLOCK // 2)
+    half_clip = pl.BlockSpec((half, frames, width), lambda i: (i, 0, 0))
+    last = clips // half - 1
+    later_clip = pl.BlockSpec((half, frames, width), lambda i: (jnp.minimum(i + 1, last), 0, 0))
+    half_pad = pltpu.VMEM((half, width // LANES, frames + 2 * HALO, LANES), f32)
+    half_row = lambda n: pl.BlockSpec((half * frames, n), lambda i: (i, 0))
     clip_out = (shape(second_input.shape, bf16), clip_spec)
     pad = pltpu.VMEM((block, width // LANES, frames + 2 * HALO, LANES), f32)
 
     second_output, xhat, slope, rstd, up, down, small, bias, gdown, down_grad_rows = kernel_call(
-        second_forward,
+        functools.partial(second_forward, owners),
         "second_forward",
-        (lengths, owners, second_input, cotangent, *blocks),
-        [smem(), smem(), clip_spec, clip_spec] + [whole(b.shape) for b in blocks],
+        (lengths, base, second_input, second_input, cotangent, *blocks),
+        [smem(), smem(), half_clip, later_clip, half_clip] + [whole(b.shape) for b in blocks],
         [
-            clip_out,
-            (shape((tokens, width), bf16), row_spec(width)),
-            (shape((tokens, hidden), bf16), row_spec(hidden)),
-            (shape((tokens, LANES), f32), row_spec(LANES)),
+            (shape(second_input.shape, bf16), half_clip),
+            (shape((tokens, width), bf16), half_row(width)),
+            (shape((tokens, hidden), bf16), half_row(hidden)),
+            (shape((tokens, LANES), f32), half_row(LANES)),
             (shape((width, hidden), bf16), whole((width, hidden))),
             (shape((hidden, width), bf16), whole((hidden, width))),
             (shape((SMALL, width), f32), whole((SMALL, width))),
@@ -476,13 +516,15 @@
             (shape((8, width), f32), whole((8, width))),
         ],
         [
-            pad,
-            pltpu.VMEM((rows, hidden), bf16),
-            pltpu.VMEM((rows, width), bf16),
-            pltpu.VMEM((hidden, width), f32),
+            half_pad,
+            pltpu.VMEM((half * frames, hidden), bf16),
+            pltpu.VMEM((half * frames, width), bf16),
+            pltpu.VMEM((width, hidden), f32),
             pltpu.VMEM((8, width), f32),
+            pltpu.VMEM((half * frames, width), bf16),
+            pltpu.VMEM((half * frames, LANES), f32),
         ],
-        steps,
+        clips // half,
         3 * matmul,
         2 * tokens * hidden,
     )
@@ -504,44 +546,53 @@
         "second_backward",
         (lengths, core.reshape(1), cotangent, second_input, xhat, slope, rstd, up, down, small, down_grad_rows, gdown),
         [
-            smem(), smem(), clip_spec, clip_spec, row_spec(width), row_spec(hidden), row_spec(LANES),
+            smem(), smem(), half_clip, half_clip, half_row(width), half_row(hidden), half_row(LANES),
             whole(up.shape), whole(down.shape), whole(small.shape), whole(down_grad_rows.shape),
             pl.BlockSpec(memory_space=pl.ANY),
         ],
         [
-            clip_out,
+            (shape(second_input.shape, bf16), half_clip),
             *outs,
         ],
         [
-            pad,
-            pltpu.VMEM((rows, hidden), bf16),
-            pltpu.VMEM((rows, width), bf16),
+            half_pad,
+            pltpu.VMEM((half * frames, hidden), bf16),
+            pltpu.VMEM((half * frames, width), bf16),
             pltpu.VMEM((width, hidden), f32),
             pltpu.VMEM((8, hidden), f32),
             pltpu.VMEM((TAPS + 1, 8, width), f32),
         ],
-        steps,
+        clips // half,
         3 * matmul,
         0,
     )
 
     if fast:
-        keep = jnp.where(core == 0, out_a, out_b)
-        got = flipped(jnp.where(core == 0, out_b, out_a), 1, devices)
-        gup_pair = pair_sum(keep, got, gdown_parts)
+        got = flipped(out_b, 1, devices)
+        got, gdown_parts = lax.optimization_barrier((got, gdown_parts))
+        flat = (-1, LANES)
+        gup_pair = (out_a.reshape(flat).astype(f32) + got.reshape(flat).astype(f32)).astype(bf16).reshape(out_a.shape)
         gup_parts = lax.all_to_all(gup_pair, CHIPS, 0, 0, tiled=True)
     else:
-        gup_pair = out_a
-
-    (first_output,) = kernel_call(
+        gup_pair, gdown_parts = out_a, gdown[None]
+
+    down_shape = gdown_parts.shape
+    columns = width // steps if width % (steps * LANES) == 0 else width
+    part = lambda i: i if columns < width else 0
+    first_output, grad_down = kernel_call(
         first_forward,
         "first_forward",
-        (lengths, first_input, up, down, small, bias, gup_pair),
+        (lengths, first_input, up, down, small, bias, gup_pair, gdown_parts, small),
         [
             smem(), clip_spec, whole(up.shape), whole(down.shape), whole(small.shape), whole(bias.shape),
             pl.BlockSpec(memory_space=pl.ANY),
+            pl.BlockSpec(down_shape[:2] + (columns,), lambda i: (0, 0, part(i))),
+            pl.BlockSpec((SMALL, columns), lambda i: (0, part(i))),
         ],
-        [clip_out],
+        [
+            clip_out,
+            (shape(down_shape[1:], f32), pl.BlockSpec((down_shape[1], columns), lambda i: (0, part(i)))),
+        ],
         [pad, pltpu.VMEM((rows, width), bf16), pltpu.VMEM((rows, hidden), bf16)],
         steps,
         2 * matmul,
@@ -550,38 +601,39 @@
 
     own = width // devices
     if fast:
-        grad_down, grad_up, sums = pl.pallas_call(
+        vector = shape((1, own), f32)
+        grad_up, grad_taps, grad_up_bias, *vectors = pl.pallas_call(
             finish,
-            out_shape=[shape((hidden // devices, width), f32), shape((own, hidden), f32), shape((SMALL, LANES), f32)],
+            out_shape=[shape((own, hidden), f32), shape((TAPS, own), f32), shape((1, hidden // devices), f32)] + [vector] * 5,
             name="finish",
-        )(gdown_parts, gup_parts, small)
-        vector = lambda r: sums[r, :own]
-        grad_taps = sums[:TAPS, :own]
-        grad_up_bias = sums[UP_BIAS : UP_BIAS + hidden // width, :own].reshape(-1)
+        )(gup_parts)
+        grad_up_bias = grad_up_bias.reshape(-1)
+        vectors = [v.reshape(-1) for v in vectors]
     else:
         scatter = lambda a: lax.psum_scatter(a.astype(f32), AXES, scatter_dimension=0, tiled=True)
         me = lax.axis_index(AXES)
-        grad_down = scatter(gdown) * (small[SCALE] * ROOT)
+        grad_down = scatter(grad_down)
         grad_up = scatter(out_a)
         sums = lax.psum(out_b, AXES)
-        vector = lambda r: lax.dynamic_slice(sums[r], (me * own,), (own,))
+        vectors = [lax.dynamic_slice(sums[r], (me * own,), (own,)) for r in (CONV_BIAS, GAIN, SHIFT, DOWN_BIAS, SCALE)]
         grad_taps = lax.dynamic_slice(sums, (0, me * own), (TAPS, own))
         grad_up_bias = lax.dynamic_slice(
             sums[UP_BIAS : UP_BIAS + hidden // width].reshape(-1), (me * (hidden // devices),), (hidden // devices,)
         )
+    conv_bias, gain, shift, down_bias, scale = vectors
     return (
         first_output,
         second_output,
         input_grad,
         grad_taps,
-        vector(CONV_BIAS),
-        vector(GAIN),
-        vector(SHIFT),
+        conv_bias,
+        gain,
+        shift,
         grad_up,
         grad_up_bias,
         grad_down,
-        vector(DOWN_BIAS),
-        vector(SCALE),
+        down_bias,
+        scale,
     )
 
 

time: 174 us -> 157 us (0.902)
  Pallas kernels: 115 us -> 103 us
  local copies, waits for them, and re-layouts: 7.55 us -> 1.66 us
    pallas_call x3, Pallas kernels: 109 us -> 99.8 us  [kernel_call(): pl.pallas_call(body, grid=(steps,), in_specs=specs, out_specs=[spec for _...]
    pallas_call x2 -> x1, Pallas kernels: 4.87 us -> 1.97 us  [on_device(): pl.pallas_call(finish, out_shape=[shape((own, hidden), f32), shape((TAPS,...]
    convert_element_type x0 -> x1, other arithmetic: none -> 2.85 us  [on_device(): (out_a.reshape(flat).astype(f32) + got.reshape(flat).astype(f32)).astype(...]
    select_n x1 -> x0, other arithmetic: 2.43 us -> none  [on_device(): got = flipped(jnp.where(core == 0, out_b, out_a), 1, devices)]
    unnamed x38 -> x36, local copies, waits for them, and re-layouts: 3.67 us -> 1.66 us
    slice x2 -> x0, local copies, waits for them, and re-layouts: 1.94 us -> none  [the longest x1 1.27 us: on_device(): grad_taps = sums[:TAPS, :own]]
  transfers between devices with their start and end apart: 19 -> 19, of which waited for: 7 -> 7; matrix products, arithmetic and copies ran while one was open for 2% -> 0% of each run, Pallas kernels for 40% -> 40%
where the time goes in v2:
time: 157 us
  Pallas kernels  103 us (66%)
  starting transfers between devices  29.4 us (19%)
  waiting for transfers between devices  17.5 us (11%)
  other arithmetic  3.77 us (2%)
  local copies, waits for them, and re-layouts  1.66 us (1%)
    pallas_call x3, Pallas kernels, kernel_call(): pl.pallas_call(body, grid=(steps,), in_specs=specs, out_specs=[spec for _...  99.8 us
    ppermute x17, waiting for transfers between devices, flipped(): return lax.ppermute(a, AXES, [(i, i ^ bits) for i in range(devices)])  17.4 us
    ppermute x17, starting transfers between devices, flipped(): return lax.ppermute(a, AXES, [(i, i ^ bits) for i in range(devices)])  16 us
    all_to_all x1, starting transfers between devices, on_device(): lax.all_to_all(gdown.reshape(devices, hidden // devices, width), AXES, 0,...  6.71 us
    all_to_all x1, starting transfers between devices, on_device(): gup_parts = lax.all_to_all(gup_pair, CHIPS, 0, 0, tiled=True)  6.66 us
  transfers between devices with their start and end apart: 19, of which 7 were waited for; matrix products, arithmetic and copies ran while one was open for 0% of the time, Pallas kernels for 40%

profile of v2, /device:TPU:0, one launch (start us, length us, event | category | flops | bytes accessed | tf_op | source)
XLA Modules:
  0.0 156.7 jit_solution(16453783555527603339)
XLA Ops:
  0.7 1.7 %own_block.1 = bf16[112,512]{1,0:T(8,128)(2,1)} custom-call(s32[1]{0:T(128)} %bitcast.me_ref, bf16[7,16]{1,0:T(8,128)(2,1)} %conv_ref.1, bf16[1,16]{1,0:T(2,128)(2,1)} %bitcast.20, bf16[1,16]{1,0:T(2,128)(2,1)} %bitcast.21, bf16[1,16]{1,0:T(2,128)(2,1)} %bitcast.22, bf16[16,1536]{1,0:T(8,128)(2,1)} %up_ref.1, bf16[1,48]{1,0:T(2,128)(2,1)} %bitcast.23, ...), custom_call_target="tpu_custom_call" | custom-call | tf_op jit(solution)/shard_map/own_block/pallas_call | solution.py:433
  2.4 4.0 %collective-permute-start = (bf16[112,512]{1,0:T(8,128)(2,1)}, bf16[112,512]{1,0:T(8,128)(2,1)S(1)}, u32[]{:S(2)}, u32[]{:S(2)}) collective-permute-start(bf16[112,512]{1,0:T(8,128)(2,1)} %own_block.1), channel_id=1, source_target_pairs={{0,16},{1,17},{2,18},{3,19},{4,20},{5,21},{6,22},{7,23},{8,24},{9,... | collective-permute-start | bytes 344072 | tf_op jit(solution)/shard_map/ppermute | solution.py:421
  6.4 5.8 %collective-permute-done = bf16[112,512]{1,0:T(8,128)(2,1)S(1)} collective-permute-done((bf16[112,512]{1,0:T(8,128)(2,1)}, bf16[112,512]{1,0:T(8,128)(2,1)S(1)}, u32[]{:S(2)}, u32[]{:S(2)}) %collective-permute-start) | collective-permute-done | bytes 114720 | tf_op jit(solution)/shard_map/ppermute | solution.py:421
  12.2 0.9 pad_maximum_fusion.refs_0_
  13.1 1.6 %collective-permute-start.2 = (bf16[2,112,512]{2,1,0:T(8,128)(2,1)S(1)}, bf16[2,112,512]{2,1,0:T(8,128)(2,1)S(1)}, u32[]{:S(2)}, u32[]{:S(2)}) collective-permute-start(bf16[2,112,512]{2,1,0:T(8,128)(2,1)S(1)} %pad_maximum_fusion.refs_0_), channel_id=1, source_target_pairs={{0,4},{1,5},{2,6},{3,7},{4,0},{5,1},{6,2},{7,3},{8,12},{9,13},{10,... | collective-permute-start | bytes 688136 | tf_op jit(solution)/shard_map/ppermute | solution.py:421
  14.8 1.5 collective-permute-start.3
  17.1 2.9 %collective-permute-done.2.refs_2_ = bf16[2,112,512]{2,1,0:T(8,128)(2,1)S(1)} collective-permute-done((bf16[2,112,512]{2,1,0:T(8,128)(2,1)S(1)}, bf16[2,112,512]{2,1,0:T(8,128)(2,1)S(1)}, u32[]{:S(2)}, u32[]{:S(2)}) %collective-permute-start.2) | collective-permute-done | bytes 229408 | tf_op jit(solution)/shard_map/ppermute | solution.py:421
  20.0 1.3 collective-permute-start.4
  21.3 1.8 %collective-permute-start.5 = (bf16[2,112,512]{2,1,0:T(8,128)(2,1)S(1)}, bf16[2,112,512]{2,1,0:T(8,128)(2,1)S(1)}, u32[]{:S(2)}, u32[]{:S(2)}) collective-permute-start(bf16[2,112,512]{2,1,0:T(8,128)(2,1)S(1)} %collective-permute-done.3.refs_3_), channel_id=1, source_target_pairs={{0,8},{1,9},{2,10},{3,11},{4,12},{5,13},{6,14},{7,15},{8,0},{9,1},... | collective-permute-start | bytes 688136 | tf_op jit(solution)/shard_map/ppermute | solution.py:421
  23.1 1.5 collective-permute-start.6
  25.1 0.9 collective-permute-done.4.refs_4_
  26.0 2.2 %collective-permute-start.7 = (bf16[2,112,512]{2,1,0:T(8,128)(2,1)S(1)}, bf16[2,112,512]{2,1,0:T(8,128)(2,1)S(1)}, u32[]{:S(2)}, u32[]{:S(2)}) collective-permute-start(bf16[2,112,512]{2,1,0:T(8,128)(2,1)S(1)} %collective-permute-done.4.refs_4_), channel_id=1, source_target_pairs={{0,8},{1,9},{2,10},{3,11},{4,12},{5,13},{6,14},{7,15},{8,0},{9,1},... | collective-permute-start | bytes 688136 | tf_op jit(solution)/shard_map/ppermute | solution.py:421
  28.3 1.0 collective-permute-done.6.refs_6_
  29.8 2.9 %collective-permute-done.7.refs_7_ = bf16[2,112,512]{2,1,0:T(8,128)(2,1)S(1)} collective-permute-done((bf16[2,112,512]{2,1,0:T(8,128)(2,1)S(1)}, bf16[2,112,512]{2,1,0:T(8,128)(2,1)S(1)}, u32[]{:S(2)}, u32[]{:S(2)}) %collective-permute-start.7) | collective-permute-done | bytes 229408 | tf_op jit(solution)/shard_map/ppermute | solution.py:421
  32.8 1.4 collective-permute-done.15.refs_15_
  35.0 36.8 %second_forward.1 = (bf16[16,256,512]{2,1,0:T(8,128)(2,1)}, bf16[4096,512]{1,0:T(8,128)(2,1)}, bf16[4096,1536]{1,0:T(8,128)(2,1)}, f32[4096,128]{1,0:T(8,128)}, ...) custom-call(s32[16]{0:T(128)} %len_ref.5, ...), custom_call_target="tpu_custom_call" | custom-call | flops 19327352832 | bytes 44138564 | tf_op jit(solution)/shard_map/second_forward/pallas_call | solution.py:362
  71.8 6.7 %all-to-all-start = ((bf16[32,48,512]{2,1,0:T(8,128)(2,1)}), bf16[32,48,512]{2,1,0:T(8,128)(2,1)S(1)}, u32[]{:S(2)}, u32[]{:S(2)}) async-start(bf16[32,48,512]{2,1,0:T(8,128)(2,1)} %bitcast.17), calls=%async_computation | async-start | bytes 3145728 | tf_op jit(solution)/shard_map/all_to_all | solution.py:535
  78.5 39.7 %second_backward.1 = (bf16[16,256,512]{2,1,0:T(8,128)(2,1)}, bf16[16,208,128]{2,1,0:T(8,128)(2,1)}, bf16[16,208,128]{2,1,0:T(8,128)(2,1)}) custom-call(s32[16]{0:T(128)} %len_ref.5, s32[1]{0:T(128)} %bitcast.9.core_ref, bf16[16,256,512]{2,1,0:T(8,128)(2,1)} %cot_ref.3, bf16[16,256,512]{2,1,0:T(8,128)(2,1)} %x_ref.4, ...), custom_call_target="tpu_custom_call" | custom-call | flops 19327352832 | bytes 37929028 | tf_op jit(solution)/shard_map/second_backward/pallas_call | solution.py:362
  118.4 2.5 %collective-permute-done.16 = bf16[16,208,128]{2,1,0:T(8,128)(2,1)S(1)} collective-permute-done((bf16[16,208,128]{2,1,0:T(8,128)(2,1)}, bf16[16,208,128]{2,1,0:T(8,128)(2,1)S(1)}, u32[]{:S(2)}, u32[]{:S(2)}) %collective-permute-start.16) | collective-permute-done | bytes 852000 | tf_op jit(solution)/shard_map/ppermute | solution.py:421
  120.9 2.8 %add_convert_fusion._ = bf16[16,208,128]{2,1,0:T(8,128)(2,1)} fusion(bf16[16,208,128]{2,1,0:T(8,128)(2,1)S(1)} %collective-permute-done.16, bf16[16,208,128]{2,1,0:T(8,128)(2,1)} %get-tuple-element.46), kind=kLoop, calls=%fused_computation | loop fusion | flops 1703936 | bytes 2555904 | tf_op jit(solution)/shard_map/convert_element_type | solution.py:574
  123.8 6.7 %all-to-all-start.1 = ((bf16[16,208,128]{2,1,0:T(8,128)(2,1)}), bf16[16,208,128]{2,1,0:T(8,128)(2,1)S(1)}, u32[]{:S(2)}, u32[]{:S(2)}) async-start(bf16[16,208,128]{2,1,0:T(8,128)(2,1)} %add_convert_fusion._), calls=%async_computation.1 | async-start | bytes 1703936 | tf_op jit(solution)/shard_map/all_to_all | solution.py:575
  130.5 23.3 %first_forward.1 = (bf16[16,256,512]{2,1,0:T(8,128)(2,1)}, f32[48,512]{1,0:T(8,128)}) custom-call(s32[16]{0:T(128)} %len_ref.5, bf16[16,256,512]{2,1,0:T(8,128)(2,1)} %x_ref.5, bf16[512,1536]{1,0:T(8,128)(2,1)} %get-tuple-element.37.up_ref, bf16[1536,512]{1,0:T(8,128)(2,1)} %get-tuple-element.38.down_ref, f32[16,512]{1,0:T(8,128)} %get-tuple-element.39.small_ref.scale_ref, ...), custom_call_target="tpu_custom_call" | custom-call | flops 12884901888 | bytes 14172224 | tf_op jit(solution)/shard_map/first_forward/pallas_call | solution.py:362
  153.8 0.9 copy-done
  154.7 2.0 %finish.1 = (f32[16,1536]{1,0:T(8,128)}, f32[7,16]{1,0:T(8,128)}, f32[1,48]{1,0:T(1,128)}, f32[1,16]{1,0:T(1,128)}, f32[1,16]{1,0:T(1,128)}, /*index=5*/f32[1,16]{1,0:T(1,128)}, f32[1,16]{1,0:T(1,128)}, f32[1,16]{1,0:T(1,128)}) custom-call(bf16[16,208,128]{2,1,0:T(8,128)(2,1)} %copy-done), custom_call_target="tpu_custom_call" | custom-call | tf_op jit(solution)/shard_map/finish/pallas_call | solution.py:605
  (57 shorter events, 2.8 us)
Async XLA Ops:
  2.4 9.8 %collective-permute-start = (bf16[112,512]{1,0:T(8,128)(2,1)}, bf16[112,512]{1,0:T(8,128)(2,1)S(1)}, u32[]{:S(2)}, u32[]{:S(2)}) collective-permute-start(bf16[112,512]{1,0:T(8,128)(2,1)} %own_block.1), channel_id=1, source_target_pairs={{0,16},{1,17},{2,18},{3,19},{4,20},{5,21},{6,22},{7,23},{8,24},{9,... | collective-permute-start | bytes 344072 | tf_op jit(solution)/shard_map/ppermute | solution.py:421
  13.1 21.1 %copy-start.2 = (bf16[2,112,512]{2,1,0:T(8,128)(2,1)}, bf16[2,112,512]{2,1,0:T(8,128)(2,1)S(1)}, u32[]{:S(2)}) copy-start(bf16[2,112,512]{2,1,0:T(8,128)(2,1)S(1)} %pad_maximum_fusion.refs_0_) | copy-start | bytes 688132
  13.1 6.9 %collective-permute-start.2 = (bf16[2,112,512]{2,1,0:T(8,128)(2,1)S(1)}, bf16[2,112,512]{2,1,0:T(8,128)(2,1)S(1)}, u32[]{:S(2)}, u32[]{:S(2)}) collective-permute-start(bf16[2,112,512]{2,1,0:T(8,128)(2,1)S(1)} %pad_maximum_fusion.refs_0_), channel_id=1, source_target_pairs={{0,4},{1,5},{2,6},{3,7},{4,0},{5,1},{6,2},{7,3},{8,12},{9,13},{10,... | collective-permute-start | bytes 688136 | tf_op jit(solution)/shard_map/ppermute | solution.py:421
  14.8 6.5 %collective-permute-start.3 = (bf16[2,112,512]{2,1,0:T(8,128)(2,1)S(1)}, bf16[2,112,512]{2,1,0:T(8,128)(2,1)S(1)}, u32[]{:S(2)}, u32[]{:S(2)}) collective-permute-start(bf16[2,112,512]{2,1,0:T(8,128)(2,1)S(1)} %pad_maximum_fusion.refs_0_), channel_id=1, source_target_pairs={{0,2},{1,3},{2,0},{3,1},{4,6},{5,7},{6,4},{7,5},{8,10},{9,11},{10,... | collective-permute-start | bytes 688136 | tf_op jit(solution)/shard_map/ppermute | solution.py:421
  16.3 6.8 %collective-permute-start.1 = (bf16[2,112,512]{2,1,0:T(8,128)(2,1)S(1)}, bf16[2,112,512]{2,1,0:T(8,128)(2,1)S(1)}, u32[]{:S(2)}, u32[]{:S(2)}) collective-permute-start(bf16[2,112,512]{2,1,0:T(8,128)(2,1)S(1)} %pad_maximum_fusion.refs_0_), channel_id=1, source_target_pairs={{0,8},{1,9},{2,10},{3,11},{4,12},{5,13},{6,14},{7,15},{8,0},{9,1},... | collective-permute-start | bytes 688136 | tf_op jit(solution)/shard_map/ppermute | solution.py:421
  17.0 7.5 %collective-permute-start.8 = (bf16[2,112,512]{2,1,0:T(8,128)(2,1)S(1)}, bf16[2,112,512]{2,1,0:T(8,128)(2,1)S(1)}, u32[]{:S(2)}, u32[]{:S(2)}) collective-permute-start(bf16[2,112,512]{2,1,0:T(8,128)(2,1)S(1)} %pad_maximum_fusion.refs_0_), channel_id=1, source_target_pairs={{0,1},{1,0},{2,3},{3,2},{4,5},{5,4},{6,7},{7,6},{8,9},{9,8},{10,11... | collective-permute-start | bytes 688136 | tf_op jit(solution)/shard_map/ppermute | solution.py:421
  20.0 14.2 %copy-start.3 = (bf16[2,112,512]{2,1,0:T(8,128)(2,1)}, bf16[2,112,512]{2,1,0:T(8,128)(2,1)S(1)}, u32[]{:S(2)}) copy-start(bf16[2,112,512]{2,1,0:T(8,128)(2,1)S(1)} %collective-permute-done.2.refs_2_) | copy-start | bytes 688132
  20.0 6.0 %collective-permute-start.4 = (bf16[2,112,512]{2,1,0:T(8,128)(2,1)S(1)}, bf16[2,112,512]{2,1,0:T(8,128)(2,1)S(1)}, u32[]{:S(2)}, u32[]{:S(2)}) collective-permute-start(bf16[2,112,512]{2,1,0:T(8,128)(2,1)S(1)} %collective-permute-done.2.refs_2_), channel_id=1, source_target_pairs={{0,2},{1,3},{2,0},{3,1},{4,6},{5,7},{6,4},{7,5},{8,10},{9,11},{10,... | collective-permute-start | bytes 688136 | tf_op jit(solution)/shard_map/ppermute | solution.py:421
  21.3 12.9 %copy-start.4 = (bf16[2,112,512]{2,1,0:T(8,128)(2,1)}, bf16[2,112,512]{2,1,0:T(8,128)(2,1)S(1)}, u32[]{:S(2)}) copy-start(bf16[2,112,512]{2,1,0:T(8,128)(2,1)S(1)} %collective-permute-done.3.refs_3_) | copy-start | bytes 688132
  21.3 7.0 %collective-permute-start.5 = (bf16[2,112,512]{2,1,0:T(8,128)(2,1)S(1)}, bf16[2,112,512]{2,1,0:T(8,128)(2,1)S(1)}, u32[]{:S(2)}, u32[]{:S(2)}) collective-permute-start(bf16[2,112,512]{2,1,0:T(8,128)(2,1)S(1)} %collective-permute-done.3.refs_3_), channel_id=1, source_target_pairs={{0,8},{1,9},{2,10},{3,11},{4,12},{5,13},{6,14},{7,15},{8,0},{9,1},... | collective-permute-start | bytes 688136 | tf_op jit(solution)/shard_map/ppermute | solution.py:421
  23.1 11.1 %copy-start.5 = (bf16[2,112,512]{2,1,0:T(8,128)(2,1)}, bf16[2,112,512]{2,1,0:T(8,128)(2,1)S(1)}, u32[]{:S(2)}) copy-start(bf16[2,112,512]{2,1,0:T(8,128)(2,1)S(1)} %collective-permute-done.1.refs_1_) | copy-start | bytes 688132
  23.1 6.1 %collective-permute-start.6 = (bf16[2,112,512]{2,1,0:T(8,128)(2,1)S(1)}, bf16[2,112,512]{2,1,0:T(8,128)(2,1)S(1)}, u32[]{:S(2)}, u32[]{:S(2)}) collective-permute-start(bf16[2,112,512]{2,1,0:T(8,128)(2,1)S(1)} %collective-permute-done.1.refs_1_), channel_id=1, source_target_pairs={{0,4},{1,5},{2,6},{3,7},{4,0},{5,1},{6,2},{7,3},{8,12},{9,13},{10,... | collective-permute-start | bytes 688136 | tf_op jit(solution)/shard_map/ppermute | solution.py:421
  24.6 4.6 %collective-permute-start.10 = (bf16[2,112,512]{2,1,0:T(8,128)(2,1)S(1)}, bf16[2,112,512]{2,1,0:T(8,128)(2,1)S(1)}, u32[]{:S(2)}, u32[]{:S(2)}) collective-permute-start(bf16[2,112,512]{2,1,0:T(8,128)(2,1)S(1)} %collective-permute-done.2.refs_2_), channel_id=1, source_target_pairs={{0,1},{1,0},{2,3},{3,2},{4,5},{5,4},{6,7},{7,6},{8,9},{9,8},{10,11... | collective-permute-start | bytes 688136 | tf_op jit(solution)/shard_map/ppermute | solution.py:421
  24.6 9.6 %copy-start.6 = (bf16[2,112,512]{2,1,0:T(8,128)(2,1)}, bf16[2,112,512]{2,1,0:T(8,128)(2,1)S(1)}, u32[]{:S(2)}) copy-start(bf16[2,112,512]{2,1,0:T(8,128)(2,1)S(1)} %collective-permute-done.8.refs_8_) | copy-start | bytes 688132
  24.6 5.1 %collective-permute-start.11 = (bf16[2,112,512]{2,1,0:T(8,128)(2,1)S(1)}, bf16[2,112,512]{2,1,0:T(8,128)(2,1)S(1)}, u32[]{:S(2)}, u32[]{:S(2)}) collective-permute-start(bf16[2,112,512]{2,1,0:T(8,128)(2,1)S(1)} %collective-permute-done.3.refs_3_), channel_id=1, source_target_pairs={{0,1},{1,0},{2,3},{3,2},{4,5},{5,4},{6,7},{7,6},{8,9},{9,8},{10,11... | collective-permute-start | bytes 688136 | tf_op jit(solution)/shard_map/ppermute | solution.py:421
  26.0 6.7 %collective-permute-start.7 = (bf16[2,112,512]{2,1,0:T(8,128)(2,1)S(1)}, bf16[2,112,512]{2,1,0:T(8,128)(2,1)S(1)}, u32[]{:S(2)}, u32[]{:S(2)}) collective-permute-start(bf16[2,112,512]{2,1,0:T(8,128)(2,1)S(1)} %collective-permute-done.4.refs_4_), channel_id=1, source_target_pairs={{0,8},{1,9},{2,10},{3,11},{4,12},{5,13},{6,14},{7,15},{8,0},{9,1},... | collective-permute-start | bytes 688136 | tf_op jit(solution)/shard_map/ppermute | solution.py:421
  28.3 4.5 %collective-permute-start.9 = (bf16[2,112,512]{2,1,0:T(8,128)(2,1)S(1)}, bf16[2,112,512]{2,1,0:T(8,128)(2,1)S(1)}, u32[]{:S(2)}, u32[]{:S(2)}) collective-permute-start(bf16[2,112,512]{2,1,0:T(8,128)(2,1)S(1)} %collective-permute-done.1.refs_1_), channel_id=1, source_target_pairs={{0,1},{1,0},{2,3},{3,2},{4,5},{5,4},{6,7},{7,6},{8,9},{9,8},{10,11... | collective-permute-start | bytes 688136 | tf_op jit(solution)/shard_map/ppermute | solution.py:421
  29.2 3.5 %collective-permute-start.12 = (bf16[2,112,512]{2,1,0:T(8,128)(2,1)S(1)}, bf16[2,112,512]{2,1,0:T(8,128)(2,1)S(1)}, u32[]{:S(2)}, u32[]{:S(2)}) collective-permute-start(bf16[2,112,512]{2,1,0:T(8,128)(2,1)S(1)} %collective-permute-done.4.refs_4_), channel_id=1, source_target_pairs={{0,1},{1,0},{2,3},{3,2},{4,5},{5,4},{6,7},{7,6},{8,9},{9,8},{10,11... | collective-permute-start | bytes 688136 | tf_op jit(solution)/shard_map/ppermute | solution.py:421
  29.2 3.5 %collective-permute-start.13 = (bf16[2,112,512]{2,1,0:T(8,128)(2,1)S(1)}, bf16[2,112,512]{2,1,0:T(8,128)(2,1)S(1)}, u32[]{:S(2)}, u32[]{:S(2)}) collective-permute-start(bf16[2,112,512]{2,1,0:T(8,128)(2,1)S(1)} %collective-permute-done.5.refs_5_), channel_id=1, source_target_pairs={{0,1},{1,0},{2,3},{3,2},{4,5},{5,4},{6,7},{7,6},{8,9},{9,8},{10,11... | collective-permute-start | bytes 688136 | tf_op jit(solution)/shard_map/ppermute | solution.py:421
  29.7 3.0 %collective-permute-start.14 = (bf16[2,112,512]{2,1,0:T(8,128)(2,1)S(1)}, bf16[2,112,512]{2,1,0:T(8,128)(2,1)S(1)}, u32[]{:S(2)}, u32[]{:S(2)}) collective-permute-start(bf16[2,112,512]{2,1,0:T(8,128)(2,1)S(1)} %collective-permute-done.6.refs_6_), channel_id=1, source_target_pairs={{0,1},{1,0},{2,3},{3,2},{4,5},{5,4},{6,7},{7,6},{8,9},{9,8},{10,11... | collective-permute-start | bytes 688136 | tf_op jit(solution)/shard_map/ppermute | solution.py:421
  32.7 1.5 collective-permute-start.15
  71.8 49.1 %all-to-all-start = ((bf16[32,48,512]{2,1,0:T(8,128)(2,1)}), bf16[32,48,512]{2,1,0:T(8,128)(2,1)S(1)}, u32[]{:S(2)}, u32[]{:S(2)}) async-start(bf16[32,48,512]{2,1,0:T(8,128)(2,1)} %bitcast.17), calls=%async_computation | async-start | bytes 3145728 | tf_op jit(solution)/shard_map/all_to_all | solution.py:535
  118.3 2.7 %collective-permute-start.16 = (bf16[16,208,128]{2,1,0:T(8,128)(2,1)}, bf16[16,208,128]{2,1,0:T(8,128)(2,1)S(1)}, u32[]{:S(2)}, u32[]{:S(2)}) collective-permute-start(bf16[16,208,128]{2,1,0:T(8,128)(2,1)} %get-tuple-element.47), channel_id=1, source_target_pairs={{0,1},{1,0},{2,3},{3,2},{4,5},{5,4},{6,7},{7,6},{8,9},{9,8},{10,11... | collective-permute-start | bytes 2555912 | tf_op jit(solution)/shard_map/ppermute | solution.py:421
  123.8 30.0 %all-to-all-start.1 = ((bf16[16,208,128]{2,1,0:T(8,128)(2,1)}), bf16[16,208,128]{2,1,0:T(8,128)(2,1)S(1)}, u32[]{:S(2)}, u32[]{:S(2)}) async-start(bf16[16,208,128]{2,1,0:T(8,128)(2,1)} %add_convert_fusion._), calls=%async_computation.1 | async-start | bytes 1703936 | tf_op jit(solution)/shard_map/all_to_all | solution.py:575
  (13 other events, 47.7 us)

commit v3 on v2

--- a/solution.py
+++ b/solution.py
@@ -73,10 +73,11 @@
     conv = jnp.concatenate(parts, axis=1)
     centred = conv - jnp.mean(conv, axis=-1, keepdims=True)
     rstd = lax.rsqrt(jnp.mean(centred * centred, axis=-1, keepdims=True) + 1e-06)
-    return (centred * rstd).astype(bf16), rstd
-
-
-def conv_norm_into(pad_ref, m, small_ref, frames, xhat_ref, rstd_ref):
+    normed = centred * rstd * small_ref[GAIN : GAIN + 1] + small_ref[SHIFT : SHIFT + 1]
+    return normed.astype(bf16)
+
+
+def conv_norm_into(pad_ref, m, small_ref, frames, xhat_ref, normed_ref, rstd_ref):
     width = xhat_ref.shape[1]
     for r in range(0, frames, CHUNK):
         parts = []
@@ -94,7 +95,11 @@
         rows = slice(m * frames + r, m * frames + r + CHUNK)
         rstd_ref[rows] = jnp.broadcast_to(rstd, (CHUNK, LANES))
         for c, p in enumerate(parts):
-            xhat_ref[rows, c * LANES : (c + 1) * LANES] = (p * rstd).astype(bf16)
+            cs = slice(c * LANES, (c + 1) * LANES)
+            xhat = p * rstd
+            xhat_ref[rows, cs] = xhat.astype(bf16)
+            normed = xhat * small_ref[GAIN : GAIN + 1, cs] + small_ref[SHIFT : SHIFT + 1, cs]
+            normed_ref[rows, cs] = normed.astype(bf16)
 
 
 def store_output(out_ref, m, length, x_ref, branch):
@@ -118,7 +123,7 @@
 def second_forward(
     owners, len_ref, me_ref, x_ref, next_ref, cot_ref, *refs
 ):
-    count = len(refs) - 17
+    count = len(refs) - 18
     block_refs = [ref.at[j] for ref in refs[:count] for j in range(ref.shape[0])]
     second_forward_body(owners, len_ref, me_ref, x_ref, next_ref, cot_ref, block_refs, *refs[count:])
 
@@ -126,7 +131,7 @@
 def second_forward_body(
     owners, len_ref, me_ref, x_ref, next_ref, cot_ref, block_refs,
     out_ref, xhat_ref, slope_ref, rstd_ref, up_ref, down_ref, small_ref, bias_ref, gdown_ref, rows_ref,
-    pad_ref, act_ref, mcot_ref, acc_ref, csum_ref, xnext_ref, rnext_ref,
+    pad_ref, act_ref, mcot_ref, acc_ref, csum_ref, xnext_ref, normed_ref, rnext_ref,
 ):
     step = pl.program_id(0)
     clips, frames, width = x_ref.shape
@@ -142,7 +147,7 @@
         for ref in block_refs:
             small = small + ref[2 * down_rows :].astype(f32)
         small_ref[...] = small
-        scale = small[SCALE : SCALE + 1] * ROOT
+        scale = small[SCALE : SCALE + 1] * 0.5
         for j, ref in enumerate(block_refs):
             owner = me_ref[0] ^ owners[j]
             at = pl.multiple_of(owner * up_rows, up_rows)
@@ -150,18 +155,14 @@
                 up_ref[pl.ds(at, up_rows), p * width : (p + 1) * width] = ref[p * up_rows : (p + 1) * up_rows]
             at = pl.multiple_of(owner * down_rows, down_rows)
             down_ref[pl.ds(at, down_rows)] = (ref[down_rows : 2 * down_rows].astype(f32) * scale).astype(bf16)
-        columns = small.T
-        ratio = columns[:, SHIFT : SHIFT + 1] / columns[:, GAIN : GAIN + 1]
-        shift = jnp.sum((up_ref[...].astype(f32) * ratio).reshape(-1, 8, hidden), axis=0)
-        shift = jnp.broadcast_to(jnp.sum(shift, axis=0, keepdims=True), (8, hidden))
         for p in range(parts):
-            cs = slice(p * width, (p + 1) * width)
-            bias_ref[:, cs] = shift[:, cs] + small[UP_BIAS + p : UP_BIAS + p + 1] * ROOT
+            bias = small[UP_BIAS + p : UP_BIAS + p + 1]
+            bias_ref[:, p * width : (p + 1) * width] = jnp.broadcast_to(bias, (8, width))
         acc_ref[...] = jnp.zeros_like(acc_ref)
         csum_ref[...] = jnp.zeros_like(csum_ref)
         for m in range(clips):
             fill_padded(x_ref, m, len_ref[m], pad_ref)
-            conv_norm_into(pad_ref, m, small_ref, frames, xnext_ref, rnext_ref)
+            conv_norm_into(pad_ref, m, small_ref, frames, xnext_ref, normed_ref, rnext_ref)
 
     lengths = [len_ref[step * clips + m] for m in range(clips)]
     xhat_ref[...] = xnext_ref[...]
@@ -171,11 +172,11 @@
 
     for p in range(parts):
         cs = slice(p * width, (p + 1) * width)
-        u = dot(xhat_ref[...], up_ref[:, cs]) + bias_ref[0:1, cs]
-        s = 1.0 + lax.erf(u)
+        u = dot(normed_ref[...], up_ref[:, cs]) + bias_ref[0:1, cs]
+        s = 1.0 + lax.erf(u * ROOT)
         act_ref[:, cs] = (u * s).astype(bf16)
-        bell = jnp.exp2(u * u * (-math.log2(math.e)))
-        slope_ref[:, cs] = (s + u * bell * (2.0 / math.sqrt(math.pi))).astype(bf16)
+        bell = jnp.exp2(u * u * (-0.5 * math.log2(math.e)))
+        slope_ref[:, cs] = (s + u * bell * math.sqrt(2.0 / math.pi)).astype(bf16)
 
     down_bias = small_ref[DOWN_BIAS : DOWN_BIAS + 1] * small_ref[SCALE : SCALE + 1]
     branch = dot(act_ref[...], down_ref[...]) + down_bias
@@ -187,7 +188,7 @@
     later = jnp.minimum(step + 1, pl.num_programs(0) - 1) * clips
     for m in range(clips):
         fill_padded(next_ref, m, len_ref[later + m], pad_ref)
-        conv_norm_into(pad_ref, m, small_ref, frames, xnext_ref, rnext_ref)
+        conv_norm_into(pad_ref, m, small_ref, frames, xnext_ref, normed_ref, rnext_ref)
 
     @pl.when(step == pl.num_programs(0) - 1)
     def _():
@@ -231,7 +232,7 @@
             gh_ref[rows, cs] = gh.astype(bf16)
     for m in range(clips):
         rows = slice(m * frames, (m + 1) * frames)
-        g = dot(gh_ref[rows], up_ref[...], 1, 1)
+        g = dot(gh_ref[rows], up_ref[...], 1, 1) * small_ref[GAIN : GAIN + 1]
         xhat = xhat_ref[rows].astype(f32)
         mean = jnp.mean(g, axis=-1, keepdims=True)
         proj = jnp.mean(g * xhat, axis=-1, keepdims=True)
@@ -268,25 +269,24 @@
         total = acc_ref[...]
         hsum = jnp.sum(hsum_ref[...], axis=0, keepdims=True)
         columns = small_ref[...].T
-        gain, shift = columns[:, GAIN : GAIN + 1] * ROOT, columns[:, SHIFT : SHIFT + 1] * ROOT
-        inverse = 1.0 / small_ref[GAIN : GAIN + 1]
+        gain, shift = columns[:, GAIN : GAIN + 1], columns[:, SHIFT : SHIFT + 1]
         rows = [jnp.sum(tsum_ref[k], axis=0, keepdims=True) for k in range(TAPS + 1)]
         up = up_ref[...].astype(f32)
         for value in (up * total, up * hsum):
             part = value[:, :LANES]
             for c in range(1, hidden // LANES):
                 part = part + value[:, c * LANES : (c + 1) * LANES]
-            rows.append(jnp.sum(part.T, axis=0, keepdims=True) * inverse)
+            rows.append(jnp.sum(part.T, axis=0, keepdims=True))
         rows.append(down_rows_ref[0:2])
         if not packed:
             out_a_ref[...] = (gain * total + shift * hsum).astype(bf16)
-            rows += [hsum[:, p * width : (p + 1) * width] * ROOT for p in range(parts)]
+            rows += [hsum[:, p * width : (p + 1) * width] for p in range(parts)]
             rows.append(jnp.zeros((SMALL - UP_BIAS - parts, width), f32))
             out_b_ref[...] = jnp.concatenate(rows, axis=0)
             return
         rows.append(jnp.zeros((SMALL - UP_BIAS, width), f32))
         rows = jnp.concatenate(rows, axis=0)
-        bias = hsum * ROOT
+        bias = hsum
         lane = lax.broadcasted_iota(jnp.int32, (SMALL, LANES), 1)
         line = lax.broadcasted_iota(jnp.int32, (SMALL, LANES), 0)
         devices = width // 16
@@ -326,7 +326,7 @@
     total = jnp.zeros(parts_ref.shape[1:], f32)
     for j in range(parts_ref.shape[0]):
         total = total + parts_ref[j].astype(f32)
-    grad_down_ref[...] = total * (scale_ref[SCALE : SCALE + 1] * ROOT)
+    grad_down_ref[...] = total * (scale_ref[SCALE : SCALE + 1] * 0.5)
 
     step = pl.program_id(0)
     clips, frames, width = x_ref.shape
@@ -341,7 +341,7 @@
 
     def front(m):
         fill_padded(x_ref, m, lengths[m], pad_ref)
-        xhat_ref[m * frames : (m + 1) * frames] = conv_norm(pad_ref, m, small_ref, frames)[0]
+        xhat_ref[m * frames : (m + 1) * frames] = conv_norm(pad_ref, m, small_ref, frames)
 
     front(0)
     for m in range(clips):
@@ -351,7 +351,7 @@
         for p in range(2 * parts):
             cs = slice(p * width // 2, (p + 1) * width // 2)
             u = dot(xhat_ref[rows], up_ref[:, cs]) + bias_ref[0:1, cs]
-            act_ref[rows, cs] = (u * (1.0 + lax.erf(u))).astype(bf16)
+            act_ref[rows, cs] = (u * (1.0 + lax.erf(u * ROOT))).astype(bf16)
         store_output(out_ref, m, lengths[m], x_ref, dot(act_ref[rows], down_ref[...]) + down_bias)
 
 
@@ -389,11 +389,8 @@
     rows, width = down_ref.shape
     parts = hidden // width
     me = me_ref[0]
-    i = lax.broadcasted_iota(jnp.int32, (own, own), 0)
-    j = lax.broadcasted_iota(jnp.int32, (own, own), 1)
-    scaled = dot(jnp.where(i == j, gain_ref[...].astype(f32), 0.0).astype(bf16), up_ref[...]) * ROOT
     for p in range(parts):
-        block_ref[p * own : (p + 1) * own] = scaled[:, p * width : (p + 1) * width].astype(bf16)
+        block_ref[p * own : (p + 1) * own] = up_ref[:, p * width : (p + 1) * width]
     block_ref[rows : 2 * rows] = down_ref[...]
     vectors = [r[...].astype(f32) for r in (conv_bias_ref, gain_ref, shift_ref, down_bias_ref, scale_ref)]
     small = jnp.concatenate([conv_ref[...].astype(f32)] + vectors + [jnp.zeros((SMALL - UP_BIAS, own), f32)], axis=0)
@@ -447,7 +444,6 @@
         order = [start ^ far for start in have for far in (0, 16)]
         return list(have.values()), order, me.reshape(1)
     everyone = lambda a, axis: lax.all_gather(a, AXES, axis=axis, tiled=True)
-    up = (up.astype(f32) * gain.astype(f32)[:, None] * ROOT).astype(bf16)
     up, down, up_bias = everyone(up, 0), everyone(down, 0), everyone(up_bias, 0)
     vectors = jnp.stack([conv_bias, gain, shift, down_bias, scale])
     small = jnp.concatenate([everyone(conv_weight, 1), everyone(vectors, 1), up_bias.reshape(parts, width)], axis=0)
@@ -521,6 +517,7 @@
             pltpu.VMEM((half * frames, width), bf16),
             pltpu.VMEM((width, hidden), f32),
             pltpu.VMEM((8, width), f32),
+            pltpu.VMEM((half * frames, width), bf16),
             pltpu.VMEM((half * frames, width), bf16),
             pltpu.VMEM((half * frames, LANES), f32),
         ],

time: 157 us -> 159 us (1.013)
  Pallas kernels: 103 us -> 105 us
where the time goes in v3:
time: 159 us; the launch traced here: 158 us
  Pallas kernels  105 us (66%)
  starting transfers between devices  29.4 us (18%)
  waiting for transfers between devices  17.5 us (11%)
  other arithmetic  3.77 us (2%)
  local copies, waits for them, and re-layouts  1.66 us (1%)
    pallas_call x3, Pallas kernels, kernel_call(): pl.pallas_call(body, grid=(steps,), in_specs=specs, out_specs=[spec for _...  101 us
    ppermute x17, waiting for transfers between devices, flipped(): return lax.ppermute(a, AXES, [(i, i ^ bits) for i in range(devices)])  17.4 us
    ppermute x17, starting transfers between devices, flipped(): return lax.ppermute(a, AXES, [(i, i ^ bits) for i in range(devices)])  16 us
    all_to_all x1, starting transfers between devices, on_device(): lax.all_to_all(gdown.reshape(devices, hidden // devices, width), AXES, 0,...  6.71 us
    all_to_all x1, starting transfers between devices, on_device(): gup_parts = lax.all_to_all(gup_pair, CHIPS, 0, 0, tiled=True)  6.67 us
  transfers between devices with their start and end apart: 19, of which 7 were waited for; matrix products, arithmetic and copies ran while one was open for 0% of the time, Pallas kernels for 40%

profile of v3, /device:TPU:0, one launch (start us, length us, event | category | flops | bytes accessed | tf_op | source)
XLA Modules:
  0.0 158.1 jit_solution(1045865505413725043)
XLA Ops:
  0.7 1.7 %own_block.1 = bf16[112,512]{1,0:T(8,128)(2,1)} custom-call(s32[1]{0:T(128)} %bitcast.me_ref, bf16[7,16]{1,0:T(8,128)(2,1)} %conv_ref.1, bf16[1,16]{1,0:T(2,128)(2,1)} %bitcast.20, bf16[1,16]{1,0:T(2,128)(2,1)} %bitcast.21, bf16[1,16]{1,0:T(2,128)(2,1)} %bitcast.22, bf16[16,1536]{1,0:T(8,128)(2,1)} %up_ref.1, bf16[1,48]{1,0:T(2,128)(2,1)} %bitcast.23, ...), custom_call_target="tpu_custom_call" | custom-call | tf_op jit(solution)/shard_map/own_block/pallas_call | solution.py:430
  2.3 4.0 %collective-permute-start = (bf16[112,512]{1,0:T(8,128)(2,1)}, bf16[112,512]{1,0:T(8,128)(2,1)S(1)}, u32[]{:S(2)}, u32[]{:S(2)}) collective-permute-start(bf16[112,512]{1,0:T(8,128)(2,1)} %own_block.1), channel_id=1, source_target_pairs={{0,16},{1,17},{2,18},{3,19},{4,20},{5,21},{6,22},{7,23},{8,24},{9,... | collective-permute-start | bytes 344072 | tf_op jit(solution)/shard_map/ppermute | solution.py:418
  6.4 5.8 %collective-permute-done = bf16[112,512]{1,0:T(8,128)(2,1)S(1)} collective-permute-done((bf16[112,512]{1,0:T(8,128)(2,1)}, bf16[112,512]{1,0:T(8,128)(2,1)S(1)}, u32[]{:S(2)}, u32[]{:S(2)}) %collective-permute-start) | collective-permute-done | bytes 114720 | tf_op jit(solution)/shard_map/ppermute | solution.py:418
  12.2 0.9 pad_maximum_fusion.refs_0_
  13.1 1.6 %collective-permute-start.2 = (bf16[2,112,512]{2,1,0:T(8,128)(2,1)S(1)}, bf16[2,112,512]{2,1,0:T(8,128)(2,1)S(1)}, u32[]{:S(2)}, u32[]{:S(2)}) collective-permute-start(bf16[2,112,512]{2,1,0:T(8,128)(2,1)S(1)} %pad_maximum_fusion.refs_0_), channel_id=1, source_target_pairs={{0,4},{1,5},{2,6},{3,7},{4,0},{5,1},{6,2},{7,3},{8,12},{9,13},{10,... | collective-permute-start | bytes 688136 | tf_op jit(solution)/shard_map/ppermute | solution.py:418
  14.7 1.5 collective-permute-start.3
  17.0 2.9 %collective-permute-done.2.refs_2_ = bf16[2,112,512]{2,1,0:T(8,128)(2,1)S(1)} collective-permute-done((bf16[2,112,512]{2,1,0:T(8,128)(2,1)S(1)}, bf16[2,112,512]{2,1,0:T(8,128)(2,1)S(1)}, u32[]{:S(2)}, u32[]{:S(2)}) %collective-permute-start.2) | collective-permute-done | bytes 229408 | tf_op jit(solution)/shard_map/ppermute | solution.py:418
  20.0 1.3 collective-permute-start.4
  21.2 1.8 %collective-permute-start.5 = (bf16[2,112,512]{2,1,0:T(8,128)(2,1)S(1)}, bf16[2,112,512]{2,1,0:T(8,128)(2,1)S(1)}, u32[]{:S(2)}, u32[]{:S(2)}) collective-permute-start(bf16[2,112,512]{2,1,0:T(8,128)(2,1)S(1)} %collective-permute-done.3.refs_3_), channel_id=1, source_target_pairs={{0,8},{1,9},{2,10},{3,11},{4,12},{5,13},{6,14},{7,15},{8,0},{9,1},... | collective-permute-start | bytes 688136 | tf_op jit(solution)/shard_map/ppermute | solution.py:418
  23.1 1.5 collective-permute-start.6
  25.1 0.9 collective-permute-done.4.refs_4_
  26.0 2.2 %collective-permute-start.7 = (bf16[2,112,512]{2,1,0:T(8,128)(2,1)S(1)}, bf16[2,112,512]{2,1,0:T(8,128)(2,1)S(1)}, u32[]{:S(2)}, u32[]{:S(2)}) collective-permute-start(bf16[2,112,512]{2,1,0:T(8,128)(2,1)S(1)} %collective-permute-done.4.refs_4_), channel_id=1, source_target_pairs={{0,8},{1,9},{2,10},{3,11},{4,12},{5,13},{6,14},{7,15},{8,0},{9,1},... | collective-permute-start | bytes 688136 | tf_op jit(solution)/shard_map/ppermute | solution.py:418
  28.2 1.0 collective-permute-done.6.refs_6_
  29.8 2.9 %collective-permute-done.7.refs_7_ = bf16[2,112,512]{2,1,0:T(8,128)(2,1)S(1)} collective-permute-done((bf16[2,112,512]{2,1,0:T(8,128)(2,1)S(1)}, bf16[2,112,512]{2,1,0:T(8,128)(2,1)S(1)}, u32[]{:S(2)}, u32[]{:S(2)}) %collective-permute-start.7) | collective-permute-done | bytes 229408 | tf_op jit(solution)/shard_map/ppermute | solution.py:418
  32.7 1.4 collective-permute-done.15.refs_15_
  35.0 37.6 %second_forward.1 = (bf16[16,256,512]{2,1,0:T(8,128)(2,1)}, bf16[4096,512]{1,0:T(8,128)(2,1)}, bf16[4096,1536]{1,0:T(8,128)(2,1)}, f32[4096,128]{1,0:T(8,128)}, ...) custom-call(s32[16]{0:T(128)} %len_ref.5, ...), custom_call_target="tpu_custom_call" | custom-call | flops 19327352832 | bytes 44138564 | tf_op jit(solution)/shard_map/second_forward/pallas_call | solution.py:362
  72.6 6.7 %all-to-all-start = ((bf16[32,48,512]{2,1,0:T(8,128)(2,1)}), bf16[32,48,512]{2,1,0:T(8,128)(2,1)S(1)}, u32[]{:S(2)}, u32[]{:S(2)}) async-start(bf16[32,48,512]{2,1,0:T(8,128)(2,1)} %bitcast.17), calls=%async_computation | async-start | bytes 3145728 | tf_op jit(solution)/shard_map/all_to_all | solution.py:532
  79.3 39.8 %second_backward.1 = (bf16[16,256,512]{2,1,0:T(8,128)(2,1)}, bf16[16,208,128]{2,1,0:T(8,128)(2,1)}, bf16[16,208,128]{2,1,0:T(8,128)(2,1)}) custom-call(s32[16]{0:T(128)} %len_ref.5, s32[1]{0:T(128)} %bitcast.9.core_ref, bf16[16,256,512]{2,1,0:T(8,128)(2,1)} %cot_ref.3, bf16[16,256,512]{2,1,0:T(8,128)(2,1)} %x_ref.4, ...), custom_call_target="tpu_custom_call" | custom-call | flops 19327352832 | bytes 37929028 | tf_op jit(solution)/shard_map/second_backward/pallas_call | solution.py:362
  119.3 2.5 %collective-permute-done.16 = bf16[16,208,128]{2,1,0:T(8,128)(2,1)S(1)} collective-permute-done((bf16[16,208,128]{2,1,0:T(8,128)(2,1)}, bf16[16,208,128]{2,1,0:T(8,128)(2,1)S(1)}, u32[]{:S(2)}, u32[]{:S(2)}) %collective-permute-start.16) | collective-permute-done | bytes 852000 | tf_op jit(solution)/shard_map/ppermute | solution.py:418
  121.8 2.8 %add_convert_fusion._ = bf16[16,208,128]{2,1,0:T(8,128)(2,1)} fusion(bf16[16,208,128]{2,1,0:T(8,128)(2,1)S(1)} %collective-permute-done.16, bf16[16,208,128]{2,1,0:T(8,128)(2,1)} %get-tuple-element.46), kind=kLoop, calls=%fused_computation | loop fusion | flops 1703936 | bytes 2555904 | tf_op jit(solution)/shard_map/convert_element_type | solution.py:571
  124.7 6.7 %all-to-all-start.1 = ((bf16[16,208,128]{2,1,0:T(8,128)(2,1)}), bf16[16,208,128]{2,1,0:T(8,128)(2,1)S(1)}, u32[]{:S(2)}, u32[]{:S(2)}) async-start(bf16[16,208,128]{2,1,0:T(8,128)(2,1)} %add_convert_fusion._), calls=%async_computation.1 | async-start | bytes 1703936 | tf_op jit(solution)/shard_map/all_to_all | solution.py:572
  131.3 23.9 %first_forward.1 = (bf16[16,256,512]{2,1,0:T(8,128)(2,1)}, f32[48,512]{1,0:T(8,128)}) custom-call(s32[16]{0:T(128)} %len_ref.5, bf16[16,256,512]{2,1,0:T(8,128)(2,1)} %x_ref.5, bf16[512,1536]{1,0:T(8,128)(2,1)} %get-tuple-element.37.up_ref, bf16[1536,512]{1,0:T(8,128)(2,1)} %get-tuple-element.38.down_ref, f32[16,512]{1,0:T(8,128)} %get-tuple-element.39.small_ref.scale_ref, ...), custom_call_target="tpu_custom_call" | custom-call | flops 12884901888 | bytes 14172224 | tf_op jit(solution)/shard_map/first_forward/pallas_call | solution.py:362
  155.2 0.9 copy-done
  156.1 2.0 %finish.1 = (f32[16,1536]{1,0:T(8,128)}, f32[7,16]{1,0:T(8,128)}, f32[1,48]{1,0:T(1,128)}, f32[1,16]{1,0:T(1,128)}, f32[1,16]{1,0:T(1,128)}, /*index=5*/f32[1,16]{1,0:T(1,128)}, f32[1,16]{1,0:T(1,128)}, f32[1,16]{1,0:T(1,128)}) custom-call(bf16[16,208,128]{2,1,0:T(8,128)(2,1)} %copy-done), custom_call_target="tpu_custom_call" | custom-call | tf_op jit(solution)/shard_map/finish/pallas_call | solution.py:602
  (57 shorter events, 2.8 us)
Async XLA Ops:
  2.3 9.8 %collective-permute-start = (bf16[112,512]{1,0:T(8,128)(2,1)}, bf16[112,512]{1,0:T(8,128)(2,1)S(1)}, u32[]{:S(2)}, u32[]{:S(2)}) collective-permute-start(bf16[112,512]{1,0:T(8,128)(2,1)} %own_block.1), channel_id=1, source_target_pairs={{0,16},{1,17},{2,18},{3,19},{4,20},{5,21},{6,22},{7,23},{8,24},{9,... | collective-permute-start | bytes 344072 | tf_op jit(solution)/shard_map/ppermute | solution.py:418
  13.1 21.1 %copy-start.2 = (bf16[2,112,512]{2,1,0:T(8,128)(2,1)}, bf16[2,112,512]{2,1,0:T(8,128)(2,1)S(1)}, u32[]{:S(2)}) copy-start(bf16[2,112,512]{2,1,0:T(8,128)(2,1)S(1)} %pad_maximum_fusion.refs_0_) | copy-start | bytes 688132
  13.1 6.9 %collective-permute-start.2 = (bf16[2,112,512]{2,1,0:T(8,128)(2,1)S(1)}, bf16[2,112,512]{2,1,0:T(8,128)(2,1)S(1)}, u32[]{:S(2)}, u32[]{:S(2)}) collective-permute-start(bf16[2,112,512]{2,1,0:T(8,128)(2,1)S(1)} %pad_maximum_fusion.refs_0_), channel_id=1, source_target_pairs={{0,4},{1,5},{2,6},{3,7},{4,0},{5,1},{6,2},{7,3},{8,12},{9,13},{10,... | collective-permute-start | bytes 688136 | tf_op jit(solution)/shard_map/ppermute | solution.py:418
  14.7 6.5 %collective-permute-start.3 = (bf16[2,112,512]{2,1,0:T(8,128)(2,1)S(1)}, bf16[2,112,512]{2,1,0:T(8,128)(2,1)S(1)}, u32[]{:S(2)}, u32[]{:S(2)}) collective-permute-start(bf16[2,112,512]{2,1,0:T(8,128)(2,1)S(1)} %pad_maximum_fusion.refs_0_), channel_id=1, source_target_pairs={{0,2},{1,3},{2,0},{3,1},{4,6},{5,7},{6,4},{7,5},{8,10},{9,11},{10,... | collective-permute-start | bytes 688136 | tf_op jit(solution)/shard_map/ppermute | solution.py:418
  16.2 6.8 %collective-permute-start.1 = (bf16[2,112,512]{2,1,0:T(8,128)(2,1)S(1)}, bf16[2,112,512]{2,1,0:T(8,128)(2,1)S(1)}, u32[]{:S(2)}, u32[]{:S(2)}) collective-permute-start(bf16[2,112,512]{2,1,0:T(8,128)(2,1)S(1)} %pad_maximum_fusion.refs_0_), channel_id=1, source_target_pairs={{0,8},{1,9},{2,10},{3,11},{4,12},{5,13},{6,14},{7,15},{8,0},{9,1},... | collective-permute-start | bytes 688136 | tf_op jit(solution)/shard_map/ppermute | solution.py:418
  17.0 7.5 %collective-permute-start.8 = (bf16[2,112,512]{2,1,0:T(8,128)(2,1)S(1)}, bf16[2,112,512]{2,1,0:T(8,128)(2,1)S(1)}, u32[]{:S(2)}, u32[]{:S(2)}) collective-permute-start(bf16[2,112,512]{2,1,0:T(8,128)(2,1)S(1)} %pad_maximum_fusion.refs_0_), channel_id=1, source_target_pairs={{0,1},{1,0},{2,3},{3,2},{4,5},{5,4},{6,7},{7,6},{8,9},{9,8},{10,11... | collective-permute-start | bytes 688136 | tf_op jit(solution)/shard_map/ppermute | solution.py:418
  20.0 14.2 %copy-start.3 = (bf16[2,112,512]{2,1,0:T(8,128)(2,1)}, bf16[2,112,512]{2,1,0:T(8,128)(2,1)S(1)}, u32[]{:S(2)}) copy-start(bf16[2,112,512]{2,1,0:T(8,128)(2,1)S(1)} %collective-permute-done.2.refs_2_) | copy-start | bytes 688132
  20.0 6.0 %collective-permute-start.4 = (bf16[2,112,512]{2,1,0:T(8,128)(2,1)S(1)}, bf16[2,112,512]{2,1,0:T(8,128)(2,1)S(1)}, u32[]{:S(2)}, u32[]{:S(2)}) collective-permute-start(bf16[2,112,512]{2,1,0:T(8,128)(2,1)S(1)} %collective-permute-done.2.refs_2_), channel_id=1, source_target_pairs={{0,2},{1,3},{2,0},{3,1},{4,6},{5,7},{6,4},{7,5},{8,10},{9,11},{10,... | collective-permute-start | bytes 688136 | tf_op jit(solution)/shard_map/ppermute | solution.py:418
  21.2 12.9 %copy-start.4 = (bf16[2,112,512]{2,1,0:T(8,128)(2,1)}, bf16[2,112,512]{2,1,0:T(8,128)(2,1)S(1)}, u32[]{:S(2)}) copy-start(bf16[2,112,512]{2,1,0:T(8,128)(2,1)S(1)} %collective-permute-done.3.refs_3_) | copy-start | bytes 688132
  21.2 7.0 %collective-permute-start.5 = (bf16[2,112,512]{2,1,0:T(8,128)(2,1)S(1)}, bf16[2,112,512]{2,1,0:T(8,128)(2,1)S(1)}, u32[]{:S(2)}, u32[]{:S(2)}) collective-permute-start(bf16[2,112,512]{2,1,0:T(8,128)(2,1)S(1)} %collective-permute-done.3.refs_3_), channel_id=1, source_target_pairs={{0,8},{1,9},{2,10},{3,11},{4,12},{5,13},{6,14},{7,15},{8,0},{9,1},... | collective-permute-start | bytes 688136 | tf_op jit(solution)/shard_map/ppermute | solution.py:418
  23.1 11.1 %copy-start.5 = (bf16[2,112,512]{2,1,0:T(8,128)(2,1)}, bf16[2,112,512]{2,1,0:T(8,128)(2,1)S(1)}, u32[]{:S(2)}) copy-start(bf16[2,112,512]{2,1,0:T(8,128)(2,1)S(1)} %collective-permute-done.1.refs_1_) | copy-start | bytes 688132
  23.1 6.1 %collective-permute-start.6 = (bf16[2,112,512]{2,1,0:T(8,128)(2,1)S(1)}, bf16[2,112,512]{2,1,0:T(8,128)(2,1)S(1)}, u32[]{:S(2)}, u32[]{:S(2)}) collective-permute-start(bf16[2,112,512]{2,1,0:T(8,128)(2,1)S(1)} %collective-permute-done.1.refs_1_), channel_id=1, source_target_pairs={{0,4},{1,5},{2,6},{3,7},{4,0},{5,1},{6,2},{7,3},{8,12},{9,13},{10,... | collective-permute-start | bytes 688136 | tf_op jit(solution)/shard_map/ppermute | solution.py:418
  24.5 4.6 %collective-permute-start.10 = (bf16[2,112,512]{2,1,0:T(8,128)(2,1)S(1)}, bf16[2,112,512]{2,1,0:T(8,128)(2,1)S(1)}, u32[]{:S(2)}, u32[]{:S(2)}) collective-permute-start(bf16[2,112,512]{2,1,0:T(8,128)(2,1)S(1)} %collective-permute-done.2.refs_2_), channel_id=1, source_target_pairs={{0,1},{1,0},{2,3},{3,2},{4,5},{5,4},{6,7},{7,6},{8,9},{9,8},{10,11... | collective-permute-start | bytes 688136 | tf_op jit(solution)/shard_map/ppermute | solution.py:418
  24.6 9.6 %copy-start.6 = (bf16[2,112,512]{2,1,0:T(8,128)(2,1)}, bf16[2,112,512]{2,1,0:T(8,128)(2,1)S(1)}, u32[]{:S(2)}) copy-start(bf16[2,112,512]{2,1,0:T(8,128)(2,1)S(1)} %collective-permute-done.8.refs_8_) | copy-start | bytes 688132
  24.6 5.1 %collective-permute-start.11 = (bf16[2,112,512]{2,1,0:T(8,128)(2,1)S(1)}, bf16[2,112,512]{2,1,0:T(8,128)(2,1)S(1)}, u32[]{:S(2)}, u32[]{:S(2)}) collective-permute-start(bf16[2,112,512]{2,1,0:T(8,128)(2,1)S(1)} %collective-permute-done.3.refs_3_), channel_id=1, source_target_pairs={{0,1},{1,0},{2,3},{3,2},{4,5},{5,4},{6,7},{7,6},{8,9},{9,8},{10,11... | collective-permute-start | bytes 688136 | tf_op jit(solution)/shard_map/ppermute | solution.py:418
  26.0 6.7 %collective-permute-start.7 = (bf16[2,112,512]{2,1,0:T(8,128)(2,1)S(1)}, bf16[2,112,512]{2,1,0:T(8,128)(2,1)S(1)}, u32[]{:S(2)}, u32[]{:S(2)}) collective-permute-start(bf16[2,112,512]{2,1,0:T(8,128)(2,1)S(1)} %collective-permute-done.4.refs_4_), channel_id=1, source_target_pairs={{0,8},{1,9},{2,10},{3,11},{4,12},{5,13},{6,14},{7,15},{8,0},{9,1},... | collective-permute-start | bytes 688136 | tf_op jit(solution)/shard_map/ppermute | solution.py:418
  28.2 4.5 %collective-permute-start.9 = (bf16[2,112,512]{2,1,0:T(8,128)(2,1)S(1)}, bf16[2,112,512]{2,1,0:T(8,128)(2,1)S(1)}, u32[]{:S(2)}, u32[]{:S(2)}) collective-permute-start(bf16[2,112,512]{2,1,0:T(8,128)(2,1)S(1)} %collective-permute-done.1.refs_1_), channel_id=1, source_target_pairs={{0,1},{1,0},{2,3},{3,2},{4,5},{5,4},{6,7},{7,6},{8,9},{9,8},{10,11... | collective-permute-start | bytes 688136 | tf_op jit(solution)/shard_map/ppermute | solution.py:418
  29.2 3.5 %collective-permute-start.12 = (bf16[2,112,512]{2,1,0:T(8,128)(2,1)S(1)}, bf16[2,112,512]{2,1,0:T(8,128)(2,1)S(1)}, u32[]{:S(2)}, u32[]{:S(2)}) collective-permute-start(bf16[2,112,512]{2,1,0:T(8,128)(2,1)S(1)} %collective-permute-done.4.refs_4_), channel_id=1, source_target_pairs={{0,1},{1,0},{2,3},{3,2},{4,5},{5,4},{6,7},{7,6},{8,9},{9,8},{10,11... | collective-permute-start | bytes 688136 | tf_op jit(solution)/shard_map/ppermute | solution.py:418
  29.2 3.5 %collective-permute-start.13 = (bf16[2,112,512]{2,1,0:T(8,128)(2,1)S(1)}, bf16[2,112,512]{2,1,0:T(8,128)(2,1)S(1)}, u32[]{:S(2)}, u32[]{:S(2)}) collective-permute-start(bf16[2,112,512]{2,1,0:T(8,128)(2,1)S(1)} %collective-permute-done.5.refs_5_), channel_id=1, source_target_pairs={{0,1},{1,0},{2,3},{3,2},{4,5},{5,4},{6,7},{7,6},{8,9},{9,8},{10,11... | collective-permute-start | bytes 688136 | tf_op jit(solution)/shard_map/ppermute | solution.py:418
  29.7 3.0 %collective-permute-start.14 = (bf16[2,112,512]{2,1,0:T(8,128)(2,1)S(1)}, bf16[2,112,512]{2,1,0:T(8,128)(2,1)S(1)}, u32[]{:S(2)}, u32[]{:S(2)}) collective-permute-start(bf16[2,112,512]{2,1,0:T(8,128)(2,1)S(1)} %collective-permute-done.6.refs_6_), channel_id=1, source_target_pairs={{0,1},{1,0},{2,3},{3,2},{4,5},{5,4},{6,7},{7,6},{8,9},{9,8},{10,11... | collective-permute-start | bytes 688136 | tf_op jit(solution)/shard_map/ppermute | solution.py:418
  32.7 1.5 collective-permute-start.15
  72.6 49.2 %all-to-all-start = ((bf16[32,48,512]{2,1,0:T(8,128)(2,1)}), bf16[32,48,512]{2,1,0:T(8,128)(2,1)S(1)}, u32[]{:S(2)}, u32[]{:S(2)}) async-start(bf16[32,48,512]{2,1,0:T(8,128)(2,1)} %bitcast.17), calls=%async_computation | async-start | bytes 3145728 | tf_op jit(solution)/shard_map/all_to_all | solution.py:532
  119.1 2.7 %collective-permute-start.16 = (bf16[16,208,128]{2,1,0:T(8,128)(2,1)}, bf16[16,208,128]{2,1,0:T(8,128)(2,1)S(1)}, u32[]{:S(2)}, u32[]{:S(2)}) collective-permute-start(bf16[16,208,128]{2,1,0:T(8,128)(2,1)} %get-tuple-element.47), channel_id=1, source_target_pairs={{0,1},{1,0},{2,3},{3,2},{4,5},{5,4},{6,7},{7,6},{8,9},{9,8},{10,11... | collective-permute-start | bytes 2555912 | tf_op jit(solution)/shard_map/ppermute | solution.py:418
  124.7 30.6 %all-to-all-start.1 = ((bf16[16,208,128]{2,1,0:T(8,128)(2,1)}), bf16[16,208,128]{2,1,0:T(8,128)(2,1)S(1)}, u32[]{:S(2)}, u32[]{:S(2)}) async-start(bf16[16,208,128]{2,1,0:T(8,128)(2,1)} %add_convert_fusion._), calls=%async_computation.1 | async-start | bytes 1703936 | tf_op jit(solution)/shard_map/all_to_all | solution.py:572
  (13 other events, 47.7 us)

commit v4 on v3

--- a/solution.py
+++ b/solution.py
@@ -232,16 +232,22 @@
             gh_ref[rows, cs] = gh.astype(bf16)
     for m in range(clips):
         rows = slice(m * frames, (m + 1) * frames)
-        g = dot(gh_ref[rows], up_ref[...], 1, 1) * small_ref[GAIN : GAIN + 1]
-        xhat = xhat_ref[rows].astype(f32)
-        mean = jnp.mean(g, axis=-1, keepdims=True)
-        proj = jnp.mean(g * xhat, axis=-1, keepdims=True)
-        rstd = rstd_ref[rows]
-        for c in range(width // LANES):
-            cs = slice(c * LANES, (c + 1) * LANES)
-            gc = (g[:, cs] - mean - xhat[:, cs] * proj) * rstd
-            pad_ref[m, c, HALO : HALO + frames] = gc
-            tsum_ref[TAPS, :, cs] += jnp.sum(gc.reshape(-1, 8, LANES), axis=0)
+        g = dot(gh_ref[rows], up_ref[...], 1, 1)
+        tiles = [slice(c * LANES, (c + 1) * LANES) for c in range(width // LANES)]
+        sums = [jnp.zeros((8, LANES), f32)] * len(tiles)
+        for r in range(0, frames, TAIL):
+            at = slice(m * frames + r, m * frames + r + TAIL)
+            gs = [g[r : r + TAIL, cs] * small_ref[GAIN : GAIN + 1, cs] for cs in tiles]
+            xs = [xhat_ref[at, cs].astype(f32) for cs in tiles]
+            mean = jnp.sum(sum(gs[1:], gs[0]), axis=-1, keepdims=True) / width
+            products = [p * q for p, q in zip(gs, xs)]
+            proj = jnp.sum(sum(products[1:], products[0]), axis=-1, keepdims=True) / width
+            for c in range(len(tiles)):
+                gc = (gs[c] - mean - xs[c] * proj) * rstd_ref[at]
+                pad_ref[m, c, HALO + r : HALO + r + TAIL] = gc
+                sums[c] = sums[c] + jnp.sum(gc.reshape(-1, 8, LANES), axis=0)
+        for c, cs in enumerate(tiles):
+            tsum_ref[TAPS, :, cs] += sums[c]
     acc_ref[...] += dot(xhat_ref[...], gh_ref[...], 0, 0)
     for m in range(clips):
         keep = tail_mask(frames, lengths[m], LANES)

time: 159 us -> 158 us (level)
  no operation moved by 1% of the time
where the time goes in v4:
time: 158 us
  Pallas kernels  105 us (66%)
  starting transfers between devices  29.4 us (19%)
  waiting for transfers between devices  17.5 us (11%)
  other arithmetic  3.77 us (2%)
  local copies, waits for them, and re-layouts  1.66 us (1%)
    pallas_call x3, Pallas kernels, kernel_call(): pl.pallas_call(body, grid=(steps,), in_specs=specs, out_specs=[spec for _...  101 us
    ppermute x17, waiting for transfers between devices, flipped(): return lax.ppermute(a, AXES, [(i, i ^ bits) for i in range(devices)])  17.4 us
    ppermute x17, starting transfers between devices, flipped(): return lax.ppermute(a, AXES, [(i, i ^ bits) for i in range(devices)])  16 us
    all_to_all x1, starting transfers between devices, on_device(): lax.all_to_all(gdown.reshape(devices, hidden // devices, width), AXES, 0,...  6.71 us
    all_to_all x1, starting transfers between devices, on_device(): gup_parts = lax.all_to_all(gup_pair, CHIPS, 0, 0, tiled=True)  6.66 us
  transfers between devices with their start and end apart: 19, of which 7 were waited for; matrix products, arithmetic and copies ran while one was open for 0% of the time, Pallas kernels for 40%

profile of v4, /device:TPU:0, one launch (start us, length us, event | category | flops | bytes accessed | tf_op | source)
XLA Modules:
  0.0 158.0 jit_solution(342376939304760799)
XLA Ops:
  0.7 1.7 %own_block.1 = bf16[112,512]{1,0:T(8,128)(2,1)} custom-call(s32[1]{0:T(128)} %bitcast.me_ref, bf16[7,16]{1,0:T(8,128)(2,1)} %conv_ref.1, bf16[1,16]{1,0:T(2,128)(2,1)} %bitcast.20, bf16[1,16]{1,0:T(2,128)(2,1)} %bitcast.21, bf16[1,16]{1,0:T(2,128)(2,1)} %bitcast.22, bf16[16,1536]{1,0:T(8,128)(2,1)} %up_ref.1, bf16[1,48]{1,0:T(2,128)(2,1)} %bitcast.23, ...), custom_call_target="tpu_custom_call" | custom-call | tf_op jit(solution)/shard_map/own_block/pallas_call | solution.py:436
  2.3 4.0 %collective-permute-start = (bf16[112,512]{1,0:T(8,128)(2,1)}, bf16[112,512]{1,0:T(8,128)(2,1)S(1)}, u32[]{:S(2)}, u32[]{:S(2)}) collective-permute-start(bf16[112,512]{1,0:T(8,128)(2,1)} %own_block.1), channel_id=1, source_target_pairs={{0,16},{1,17},{2,18},{3,19},{4,20},{5,21},{6,22},{7,23},{8,24},{9,... | collective-permute-start | bytes 344072 | tf_op jit(solution)/shard_map/ppermute | solution.py:424
  6.4 5.8 %collective-permute-done = bf16[112,512]{1,0:T(8,128)(2,1)S(1)} collective-permute-done((bf16[112,512]{1,0:T(8,128)(2,1)}, bf16[112,512]{1,0:T(8,128)(2,1)S(1)}, u32[]{:S(2)}, u32[]{:S(2)}) %collective-permute-start) | collective-permute-done | bytes 114720 | tf_op jit(solution)/shard_map/ppermute | solution.py:424
  12.2 0.9 pad_maximum_fusion.refs_0_
  13.1 1.6 %collective-permute-start.2 = (bf16[2,112,512]{2,1,0:T(8,128)(2,1)S(1)}, bf16[2,112,512]{2,1,0:T(8,128)(2,1)S(1)}, u32[]{:S(2)}, u32[]{:S(2)}) collective-permute-start(bf16[2,112,512]{2,1,0:T(8,128)(2,1)S(1)} %pad_maximum_fusion.refs_0_), channel_id=1, source_target_pairs={{0,4},{1,5},{2,6},{3,7},{4,0},{5,1},{6,2},{7,3},{8,12},{9,13},{10,... | collective-permute-start | bytes 688136 | tf_op jit(solution)/shard_map/ppermute | solution.py:424
  14.7 1.5 collective-permute-start.3
  17.0 2.9 %collective-permute-done.2.refs_2_ = bf16[2,112,512]{2,1,0:T(8,128)(2,1)S(1)} collective-permute-done((bf16[2,112,512]{2,1,0:T(8,128)(2,1)S(1)}, bf16[2,112,512]{2,1,0:T(8,128)(2,1)S(1)}, u32[]{:S(2)}, u32[]{:S(2)}) %collective-permute-start.2) | collective-permute-done | bytes 229408 | tf_op jit(solution)/shard_map/ppermute | solution.py:424
  20.0 1.3 collective-permute-start.4
  21.2 1.8 %collective-permute-start.5 = (bf16[2,112,512]{2,1,0:T(8,128)(2,1)S(1)}, bf16[2,112,512]{2,1,0:T(8,128)(2,1)S(1)}, u32[]{:S(2)}, u32[]{:S(2)}) collective-permute-start(bf16[2,112,512]{2,1,0:T(8,128)(2,1)S(1)} %collective-permute-done.3.refs_3_), channel_id=1, source_target_pairs={{0,8},{1,9},{2,10},{3,11},{4,12},{5,13},{6,14},{7,15},{8,0},{9,1},... | collective-permute-start | bytes 688136 | tf_op jit(solution)/shard_map/ppermute | solution.py:424
  23.1 1.5 collective-permute-start.6
  25.1 0.9 collective-permute-done.4.refs_4_
  26.0 2.2 %collective-permute-start.7 = (bf16[2,112,512]{2,1,0:T(8,128)(2,1)S(1)}, bf16[2,112,512]{2,1,0:T(8,128)(2,1)S(1)}, u32[]{:S(2)}, u32[]{:S(2)}) collective-permute-start(bf16[2,112,512]{2,1,0:T(8,128)(2,1)S(1)} %collective-permute-done.4.refs_4_), channel_id=1, source_target_pairs={{0,8},{1,9},{2,10},{3,11},{4,12},{5,13},{6,14},{7,15},{8,0},{9,1},... | collective-permute-start | bytes 688136 | tf_op jit(solution)/shard_map/ppermute | solution.py:424
  28.2 1.0 collective-permute-done.6.refs_6_
  29.8 2.9 %collective-permute-done.7.refs_7_ = bf16[2,112,512]{2,1,0:T(8,128)(2,1)S(1)} collective-permute-done((bf16[2,112,512]{2,1,0:T(8,128)(2,1)S(1)}, bf16[2,112,512]{2,1,0:T(8,128)(2,1)S(1)}, u32[]{:S(2)}, u32[]{:S(2)}) %collective-permute-start.7) | collective-permute-done | bytes 229408 | tf_op jit(solution)/shard_map/ppermute | solution.py:424
  32.7 1.4 collective-permute-done.15.refs_15_
  35.0 37.6 %second_forward.1 = (bf16[16,256,512]{2,1,0:T(8,128)(2,1)}, bf16[4096,512]{1,0:T(8,128)(2,1)}, bf16[4096,1536]{1,0:T(8,128)(2,1)}, f32[4096,128]{1,0:T(8,128)}, ...) custom-call(s32[16]{0:T(128)} %len_ref.5, ...), custom_call_target="tpu_custom_call" | custom-call | flops 19327352832 | bytes 44138564 | tf_op jit(solution)/shard_map/second_forward/pallas_call | solution.py:368
  72.6 6.7 %all-to-all-start = ((bf16[32,48,512]{2,1,0:T(8,128)(2,1)}), bf16[32,48,512]{2,1,0:T(8,128)(2,1)S(1)}, u32[]{:S(2)}, u32[]{:S(2)}) async-start(bf16[32,48,512]{2,1,0:T(8,128)(2,1)} %bitcast.17), calls=%async_computation | async-start | bytes 3145728 | tf_op jit(solution)/shard_map/all_to_all | solution.py:538
  79.3 39.7 %second_backward.1 = (bf16[16,256,512]{2,1,0:T(8,128)(2,1)}, bf16[16,208,128]{2,1,0:T(8,128)(2,1)}, bf16[16,208,128]{2,1,0:T(8,128)(2,1)}) custom-call(s32[16]{0:T(128)} %len_ref.5, s32[1]{0:T(128)} %bitcast.9.core_ref, bf16[16,256,512]{2,1,0:T(8,128)(2,1)} %cot_ref.3, bf16[16,256,512]{2,1,0:T(8,128)(2,1)} %x_ref.4, ...), custom_call_target="tpu_custom_call" | custom-call | flops 19327352832 | bytes 37929028 | tf_op jit(solution)/shard_map/second_backward/pallas_call | solution.py:368
  119.2 2.5 %collective-permute-done.16 = bf16[16,208,128]{2,1,0:T(8,128)(2,1)S(1)} collective-permute-done((bf16[16,208,128]{2,1,0:T(8,128)(2,1)}, bf16[16,208,128]{2,1,0:T(8,128)(2,1)S(1)}, u32[]{:S(2)}, u32[]{:S(2)}) %collective-permute-start.16) | collective-permute-done | bytes 852000 | tf_op jit(solution)/shard_map/ppermute | solution.py:424
  121.8 2.8 %add_convert_fusion._ = bf16[16,208,128]{2,1,0:T(8,128)(2,1)} fusion(bf16[16,208,128]{2,1,0:T(8,128)(2,1)S(1)} %collective-permute-done.16, bf16[16,208,128]{2,1,0:T(8,128)(2,1)} %get-tuple-element.46), kind=kLoop, calls=%fused_computation | loop fusion | flops 1703936 | bytes 2555904 | tf_op jit(solution)/shard_map/convert_element_type | solution.py:577
  124.6 6.7 %all-to-all-start.1 = ((bf16[16,208,128]{2,1,0:T(8,128)(2,1)}), bf16[16,208,128]{2,1,0:T(8,128)(2,1)S(1)}, u32[]{:S(2)}, u32[]{:S(2)}) async-start(bf16[16,208,128]{2,1,0:T(8,128)(2,1)} %add_convert_fusion._), calls=%async_computation.1 | async-start | bytes 1703936 | tf_op jit(solution)/shard_map/all_to_all | solution.py:578
  131.3 23.9 %first_forward.1 = (bf16[16,256,512]{2,1,0:T(8,128)(2,1)}, f32[48,512]{1,0:T(8,128)}) custom-call(s32[16]{0:T(128)} %len_ref.5, bf16[16,256,512]{2,1,0:T(8,128)(2,1)} %x_ref.5, bf16[512,1536]{1,0:T(8,128)(2,1)} %get-tuple-element.37.up_ref, bf16[1536,512]{1,0:T(8,128)(2,1)} %get-tuple-element.38.down_ref, f32[16,512]{1,0:T(8,128)} %get-tuple-element.39.small_ref.scale_ref, ...), custom_call_target="tpu_custom_call" | custom-call | flops 12884901888 | bytes 14172224 | tf_op jit(solution)/shard_map/first_forward/pallas_call | solution.py:368
  155.2 0.9 copy-done
  156.1 2.0 %finish.1 = (f32[16,1536]{1,0:T(8,128)}, f32[7,16]{1,0:T(8,128)}, f32[1,48]{1,0:T(1,128)}, f32[1,16]{1,0:T(1,128)}, f32[1,16]{1,0:T(1,128)}, /*index=5*/f32[1,16]{1,0:T(1,128)}, f32[1,16]{1,0:T(1,128)}, f32[1,16]{1,0:T(1,128)}) custom-call(bf16[16,208,128]{2,1,0:T(8,128)(2,1)} %copy-done), custom_call_target="tpu_custom_call" | custom-call | tf_op jit(solution)/shard_map/finish/pallas_call | solution.py:608
  (57 shorter events, 2.8 us)
Async XLA Ops:
  2.3 9.8 %collective-permute-start = (bf16[112,512]{1,0:T(8,128)(2,1)}, bf16[112,512]{1,0:T(8,128)(2,1)S(1)}, u32[]{:S(2)}, u32[]{:S(2)}) collective-permute-start(bf16[112,512]{1,0:T(8,128)(2,1)} %own_block.1), channel_id=1, source_target_pairs={{0,16},{1,17},{2,18},{3,19},{4,20},{5,21},{6,22},{7,23},{8,24},{9,... | collective-permute-start | bytes 344072 | tf_op jit(solution)/shard_map/ppermute | solution.py:424
  13.1 21.1 %copy-start.2 = (bf16[2,112,512]{2,1,0:T(8,128)(2,1)}, bf16[2,112,512]{2,1,0:T(8,128)(2,1)S(1)}, u32[]{:S(2)}) copy-start(bf16[2,112,512]{2,1,0:T(8,128)(2,1)S(1)} %pad_maximum_fusion.refs_0_) | copy-start | bytes 688132
  13.1 6.9 %collective-permute-start.2 = (bf16[2,112,512]{2,1,0:T(8,128)(2,1)S(1)}, bf16[2,112,512]{2,1,0:T(8,128)(2,1)S(1)}, u32[]{:S(2)}, u32[]{:S(2)}) collective-permute-start(bf16[2,112,512]{2,1,0:T(8,128)(2,1)S(1)} %pad_maximum_fusion.refs_0_), channel_id=1, source_target_pairs={{0,4},{1,5},{2,6},{3,7},{4,0},{5,1},{6,2},{7,3},{8,12},{9,13},{10,... | collective-permute-start | bytes 688136 | tf_op jit(solution)/shard_map/ppermute | solution.py:424
  14.7 6.5 %collective-permute-start.3 = (bf16[2,112,512]{2,1,0:T(8,128)(2,1)S(1)}, bf16[2,112,512]{2,1,0:T(8,128)(2,1)S(1)}, u32[]{:S(2)}, u32[]{:S(2)}) collective-permute-start(bf16[2,112,512]{2,1,0:T(8,128)(2,1)S(1)} %pad_maximum_fusion.refs_0_), channel_id=1, source_target_pairs={{0,2},{1,3},{2,0},{3,1},{4,6},{5,7},{6,4},{7,5},{8,10},{9,11},{10,... | collective-permute-start | bytes 688136 | tf_op jit(solution)/shard_map/ppermute | solution.py:424
  16.2 6.8 %collective-permute-start.1 = (bf16[2,112,512]{2,1,0:T(8,128)(2,1)S(1)}, bf16[2,112,512]{2,1,0:T(8,128)(2,1)S(1)}, u32[]{:S(2)}, u32[]{:S(2)}) collective-permute-start(bf16[2,112,512]{2,1,0:T(8,128)(2,1)S(1)} %pad_maximum_fusion.refs_0_), channel_id=1, source_target_pairs={{0,8},{1,9},{2,10},{3,11},{4,12},{5,13},{6,14},{7,15},{8,0},{9,1},... | collective-permute-start | bytes 688136 | tf_op jit(solution)/shard_map/ppermute | solution.py:424
  17.0 7.5 %collective-permute-start.8 = (bf16[2,112,512]{2,1,0:T(8,128)(2,1)S(1)}, bf16[2,112,512]{2,1,0:T(8,128)(2,1)S(1)}, u32[]{:S(2)}, u32[]{:S(2)}) collective-permute-start(bf16[2,112,512]{2,1,0:T(8,128)(2,1)S(1)} %pad_maximum_fusion.refs_0_), channel_id=1, source_target_pairs={{0,1},{1,0},{2,3},{3,2},{4,5},{5,4},{6,7},{7,6},{8,9},{9,8},{10,11... | collective-permute-start | bytes 688136 | tf_op jit(solution)/shard_map/ppermute | solution.py:424
  20.0 14.2 %copy-start.3 = (bf16[2,112,512]{2,1,0:T(8,128)(2,1)}, bf16[2,112,512]{2,1,0:T(8,128)(2,1)S(1)}, u32[]{:S(2)}) copy-start(bf16[2,112,512]{2,1,0:T(8,128)(2,1)S(1)} %collective-permute-done.2.refs_2_) | copy-start | bytes 688132
  20.0 6.0 %collective-permute-start.4 = (bf16[2,112,512]{2,1,0:T(8,128)(2,1)S(1)}, bf16[2,112,512]{2,1,0:T(8,128)(2,1)S(1)}, u32[]{:S(2)}, u32[]{:S(2)}) collective-permute-start(bf16[2,112,512]{2,1,0:T(8,128)(2,1)S(1)} %collective-permute-done.2.refs_2_), channel_id=1, source_target_pairs={{0,2},{1,3},{2,0},{3,1},{4,6},{5,7},{6,4},{7,5},{8,10},{9,11},{10,... | collective-permute-start | bytes 688136 | tf_op jit(solution)/shard_map/ppermute | solution.py:424
  21.2 12.9 %copy-start.4 = (bf16[2,112,512]{2,1,0:T(8,128)(2,1)}, bf16[2,112,512]{2,1,0:T(8,128)(2,1)S(1)}, u32[]{:S(2)}) copy-start(bf16[2,112,512]{2,1,0:T(8,128)(2,1)S(1)} %collective-permute-done.3.refs_3_) | copy-start | bytes 688132
  21.2 7.0 %collective-permute-start.5 = (bf16[2,112,512]{2,1,0:T(8,128)(2,1)S(1)}, bf16[2,112,512]{2,1,0:T(8,128)(2,1)S(1)}, u32[]{:S(2)}, u32[]{:S(2)}) collective-permute-start(bf16[2,112,512]{2,1,0:T(8,128)(2,1)S(1)} %collective-permute-done.3.refs_3_), channel_id=1, source_target_pairs={{0,8},{1,9},{2,10},{3,11},{4,12},{5,13},{6,14},{7,15},{8,0},{9,1},... | collective-permute-start | bytes 688136 | tf_op jit(solution)/shard_map/ppermute | solution.py:424
  23.1 11.1 %copy-start.5 = (bf16[2,112,512]{2,1,0:T(8,128)(2,1)}, bf16[2,112,512]{2,1,0:T(8,128)(2,1)S(1)}, u32[]{:S(2)}) copy-start(bf16[2,112,512]{2,1,0:T(8,128)(2,1)S(1)} %collective-permute-done.1.refs_1_) | copy-start | bytes 688132
  23.1 6.1 %collective-permute-start.6 = (bf16[2,112,512]{2,1,0:T(8,128)(2,1)S(1)}, bf16[2,112,512]{2,1,0:T(8,128)(2,1)S(1)}, u32[]{:S(2)}, u32[]{:S(2)}) collective-permute-start(bf16[2,112,512]{2,1,0:T(8,128)(2,1)S(1)} %collective-permute-done.1.refs_1_), channel_id=1, source_target_pairs={{0,4},{1,5},{2,6},{3,7},{4,0},{5,1},{6,2},{7,3},{8,12},{9,13},{10,... | collective-permute-start | bytes 688136 | tf_op jit(solution)/shard_map/ppermute | solution.py:424
  24.5 4.6 %collective-permute-start.10 = (bf16[2,112,512]{2,1,0:T(8,128)(2,1)S(1)}, bf16[2,112,512]{2,1,0:T(8,128)(2,1)S(1)}, u32[]{:S(2)}, u32[]{:S(2)}) collective-permute-start(bf16[2,112,512]{2,1,0:T(8,128)(2,1)S(1)} %collective-permute-done.2.refs_2_), channel_id=1, source_target_pairs={{0,1},{1,0},{2,3},{3,2},{4,5},{5,4},{6,7},{7,6},{8,9},{9,8},{10,11... | collective-permute-start | bytes 688136 | tf_op jit(solution)/shard_map/ppermute | solution.py:424
  24.6 9.6 %copy-start.6 = (bf16[2,112,512]{2,1,0:T(8,128)(2,1)}, bf16[2,112,512]{2,1,0:T(8,128)(2,1)S(1)}, u32[]{:S(2)}) copy-start(bf16[2,112,512]{2,1,0:T(8,128)(2,1)S(1)} %collective-permute-done.8.refs_8_) | copy-start | bytes 688132
  24.6 5.1 %collective-permute-start.11 = (bf16[2,112,512]{2,1,0:T(8,128)(2,1)S(1)}, bf16[2,112,512]{2,1,0:T(8,128)(2,1)S(1)}, u32[]{:S(2)}, u32[]{:S(2)}) collective-permute-start(bf16[2,112,512]{2,1,0:T(8,128)(2,1)S(1)} %collective-permute-done.3.refs_3_), channel_id=1, source_target_pairs={{0,1},{1,0},{2,3},{3,2},{4,5},{5,4},{6,7},{7,6},{8,9},{9,8},{10,11... | collective-permute-start | bytes 688136 | tf_op jit(solution)/shard_map/ppermute | solution.py:424
  26.0 6.7 %collective-permute-start.7 = (bf16[2,112,512]{2,1,0:T(8,128)(2,1)S(1)}, bf16[2,112,512]{2,1,0:T(8,128)(2,1)S(1)}, u32[]{:S(2)}, u32[]{:S(2)}) collective-permute-start(bf16[2,112,512]{2,1,0:T(8,128)(2,1)S(1)} %collective-permute-done.4.refs_4_), channel_id=1, source_target_pairs={{0,8},{1,9},{2,10},{3,11},{4,12},{5,13},{6,14},{7,15},{8,0},{9,1},... | collective-permute-start | bytes 688136 | tf_op jit(solution)/shard_map/ppermute | solution.py:424
  28.2 4.5 %collective-permute-start.9 = (bf16[2,112,512]{2,1,0:T(8,128)(2,1)S(1)}, bf16[2,112,512]{2,1,0:T(8,128)(2,1)S(1)}, u32[]{:S(2)}, u32[]{:S(2)}) collective-permute-start(bf16[2,112,512]{2,1,0:T(8,128)(2,1)S(1)} %collective-permute-done.1.refs_1_), channel_id=1, source_target_pairs={{0,1},{1,0},{2,3},{3,2},{4,5},{5,4},{6,7},{7,6},{8,9},{9,8},{10,11... | collective-permute-start | bytes 688136 | tf_op jit(solution)/shard_map/ppermute | solution.py:424
  29.2 3.5 %collective-permute-start.12 = (bf16[2,112,512]{2,1,0:T(8,128)(2,1)S(1)}, bf16[2,112,512]{2,1,0:T(8,128)(2,1)S(1)}, u32[]{:S(2)}, u32[]{:S(2)}) collective-permute-start(bf16[2,112,512]{2,1,0:T(8,128)(2,1)S(1)} %collective-permute-done.4.refs_4_), channel_id=1, source_target_pairs={{0,1},{1,0},{2,3},{3,2},{4,5},{5,4},{6,7},{7,6},{8,9},{9,8},{10,11... | collective-permute-start | bytes 688136 | tf_op jit(solution)/shard_map/ppermute | solution.py:424
  29.2 3.5 %collective-permute-start.13 = (bf16[2,112,512]{2,1,0:T(8,128)(2,1)S(1)}, bf16[2,112,512]{2,1,0:T(8,128)(2,1)S(1)}, u32[]{:S(2)}, u32[]{:S(2)}) collective-permute-start(bf16[2,112,512]{2,1,0:T(8,128)(2,1)S(1)} %collective-permute-done.5.refs_5_), channel_id=1, source_target_pairs={{0,1},{1,0},{2,3},{3,2},{4,5},{5,4},{6,7},{7,6},{8,9},{9,8},{10,11... | collective-permute-start | bytes 688136 | tf_op jit(solution)/shard_map/ppermute | solution.py:424
  29.7 3.0 %collective-permute-start.14 = (bf16[2,112,512]{2,1,0:T(8,128)(2,1)S(1)}, bf16[2,112,512]{2,1,0:T(8,128)(2,1)S(1)}, u32[]{:S(2)}, u32[]{:S(2)}) collective-permute-start(bf16[2,112,512]{2,1,0:T(8,128)(2,1)S(1)} %collective-permute-done.6.refs_6_), channel_id=1, source_target_pairs={{0,1},{1,0},{2,3},{3,2},{4,5},{5,4},{6,7},{7,6},{8,9},{9,8},{10,11... | collective-permute-start | bytes 688136 | tf_op jit(solution)/shard_map/ppermute | solution.py:424
  32.7 1.5 collective-permute-start.15
  72.6 49.1 %all-to-all-start = ((bf16[32,48,512]{2,1,0:T(8,128)(2,1)}), bf16[32,48,512]{2,1,0:T(8,128)(2,1)S(1)}, u32[]{:S(2)}, u32[]{:S(2)}) async-start(bf16[32,48,512]{2,1,0:T(8,128)(2,1)} %bitcast.17), calls=%async_computation | async-start | bytes 3145728 | tf_op jit(solution)/shard_map/all_to_all | solution.py:538
  119.1 2.7 %collective-permute-start.16 = (bf16[16,208,128]{2,1,0:T(8,128)(2,1)}, bf16[16,208,128]{2,1,0:T(8,128)(2,1)S(1)}, u32[]{:S(2)}, u32[]{:S(2)}) collective-permute-start(bf16[16,208,128]{2,1,0:T(8,128)(2,1)} %get-tuple-element.47), channel_id=1, source_target_pairs={{0,1},{1,0},{2,3},{3,2},{4,5},{5,4},{6,7},{7,6},{8,9},{9,8},{10,11... | collective-permute-start | bytes 2555912 | tf_op jit(solution)/shard_map/ppermute | solution.py:424
  124.6 30.5 %all-to-all-start.1 = ((bf16[16,208,128]{2,1,0:T(8,128)(2,1)}), bf16[16,208,128]{2,1,0:T(8,128)(2,1)S(1)}, u32[]{:S(2)}, u32[]{:S(2)}) async-start(bf16[16,208,128]{2,1,0:T(8,128)(2,1)} %add_convert_fusion._), calls=%async_computation.1 | async-start | bytes 1703936 | tf_op jit(solution)/shard_map/all_to_all | solution.py:578
  (13 other events, 47.7 us)
